TPU v7x, 512 devices: a whole 4x8x8 slice. The times are simulated.
512 devices in a mesh: depth: 16 (over y_hi, x), tile: 32 (over y_lo, z, core).
Axes of the slice: x: 4, y: 8 (y_hi: 4, y_lo: 2; y = y_hi * 2 + y_lo), z: 8, core: 2. Of those that a mesh axis runs over, the one named last changes fastest.
Arguments:
- volume: float32 [128, 256, 256], P('depth', 'tile'), may hold values from 0.01 to 4
- measured: float32 [128, 256, 256], P('depth', 'tile'), may hold values from 0.3 to 3
- point_spread: bfloat16 [11, 11, 128, 128], replicated, may hold values from 1.5625e-05 to 0.28125
Outputs:
- updated: float32 [128, 256, 256], P('depth', 'tile')
All inputs are finite; a program needn't handle non-finite values.
Results may differ from a plain program's by a relative error of at most 0.0008.
Values may be sent and summed in bfloat16 or wider, within the bound.
No kernel may reach another device: no remote copies, remote signals or barrier semaphores. Data moves between devices by JAX's collectives and lax.ppermute only.
A program may use at most 64 MiB of HBM per device.

v0:
```python
import jax
import jax.numpy as jnp
from jax import lax
from jax.sharding import PartitionSpec as P


def extended(cells, sides, width):
    for axis, dim in sides:
        count = lax.axis_size(axis)
        ends = count - 1
        head = lax.slice_in_dim(cells, 0, width, axis=dim)
        tail = lax.slice_in_dim(cells, cells.shape[dim] - width, cells.shape[dim], axis=dim)
        cells = jnp.concatenate(
            [
                lax.ppermute(tail, axis, [(i, (i + 1) % count) for i in range(ends)]),
                cells,
                lax.ppermute(head, axis, [((i + 1) % count, i) for i in range(ends)]),
            ],
            axis=dim,
        )
    return cells


def split_up(x, dim, length):
    before, after = (x.shape[:dim], x.shape[dim + 1 :])
    return jnp.moveaxis(x.reshape(*before, length, -1, *after), dim, 0)


def sum_at_owner(x, axis, dim):
    length = lax.axis_size(axis)
    blocks = lax.all_to_all(split_up(x, dim, length), axis, 0, 0, tiled=True)
    return jnp.sum(blocks.astype(jnp.float32), axis=0)


def in_order(blocks, dim):
    lengths = list(blocks.shape[1:])
    lengths[dim] *= blocks.shape[0]
    return jnp.moveaxis(blocks, 0, dim).reshape(lengths)


def copy_for_each(x, axis):
    length = lax.axis_size(axis)
    return lax.all_to_all(jnp.broadcast_to(x[None], (length, *x.shape)), axis, 0, 0, tiled=True)


def collect(x, axis, dim):
    return in_order(copy_for_each(x, axis), dim)


def correlate_windows(edge, kernel, pattern):
    extent = kernel.shape[0]
    height = edge.shape[1] - extent + 1
    breadth = edge.shape[2] - extent + 1
    windows = jnp.stack(
        [
            edge[:, row_shift : row_shift + height, col_shift : col_shift + breadth]
            for row_shift in range(extent)
            for col_shift in range(extent)
        ],
        axis=0,
    )
    tap_table = kernel.reshape((extent * extent,) + kernel.shape[2:])
    return jnp.einsum(pattern, windows, tap_table, preferred_element_type=jnp.float32)


def correlate_products(edge, kernel, pattern):
    extent = kernel.shape[0]
    height = edge.shape[1] - extent + 1
    breadth = edge.shape[2] - extent + 1
    summed = jnp.zeros((kernel.shape[2], height, breadth), jnp.float32)
    for row_shift in range(extent):
        row_slab = edge[:, row_shift : row_shift + height, :]
        partial_out = jnp.einsum(
            pattern, row_slab, kernel[row_shift], preferred_element_type=jnp.float32
        )
        for col_shift in range(extent):
            summed = summed + partial_out[col_shift, :, :, col_shift : col_shift + breadth]
    return summed


def body(volume, measured, point_spread):
    radius = point_spread.shape[0] // 2
    planes_here = volume.shape[0]
    own_kernel = lax.dynamic_slice_in_dim(
        point_spread, lax.axis_index("depth") * planes_here, planes_here, 2
    )
    volume_low = volume.astype(jnp.bfloat16)
    volume_rows = extended(volume_low, (("tile", 1),), radius)
    volume_edge = jnp.pad(volume_rows, ((0, 0), (0, 0), (radius, radius)))
    projection = sum_at_owner(
        correlate_windows(volume_edge, own_kernel, "tcyx,tco->oyx").astype(jnp.bfloat16), "depth", 0
    )
    ratio = (measured / projection).astype(jnp.bfloat16)
    ratio_rows = extended(ratio, (("tile", 1),), radius)
    every_ratio = collect(ratio_rows, "depth", 0)
    ratio_edge = jnp.pad(every_ratio, ((0, 0), (0, 0), (radius, radius)))
    back_sum = correlate_products(ratio_edge, own_kernel[::-1, ::-1], "cyx,joc->joyx")
    weight = jnp.sum(own_kernel.astype(jnp.float32), axis=(0, 1, 3))
    return volume * back_sum / weight[:, None, None]


def solution(mesh):
    in_specs = (P("depth", "tile", None), P("depth", "tile", None), P())
    out_specs = P("depth", "tile", None)
    return jax.shard_map(body, mesh=mesh, in_specs=in_specs, out_specs=out_specs, check_vma=False)
```

profile of v0, /device:TPU:193, one launch (start us, length us, event | category | flops | bytes accessed | tf_op | source)
XLA Modules:
  0.0 102.0 jit_solution(10695359258554619980)
XLA Ops:
  0.0 0.9 copy.536
  0.9 5.8 %collective-permute-start = (bf16[8,5,256]{2,0,1:T(8,128)(2,1)S(1)}, bf16[8,5,256]{2,0,1:T(8,128)(2,1)S(1)}, u32[]{:S(2)}, u32[]{:S(2)}) collective-permute-start(bf16[8,5,256]{2,0,1:T(8,128)(2,1)S(1)} %get-tuple-element.20), channel_id=1, source_target_pairs={{0,1},{1,2},{2,3},{3,4},{4,5},{5,6},{6,7},{7,8},{8,9},{9,10},{10,1... | collective-permute-start | bytes 61448 | tf_op jit(solution)/shard_map/ppermute | solution.py:15
  6.7 1.9 %collective-permute-start.1 = (bf16[8,5,256]{2,0,1:T(8,128)(2,1)S(1)}, bf16[8,5,256]{2,0,1:T(8,128)(2,1)S(1)}, u32[]{:S(2)}, u32[]{:S(2)}) collective-permute-start(bf16[8,5,256]{2,0,1:T(8,128)(2,1)S(1)} %get-tuple-element.21), channel_id=1, source_target_pairs={{1,0},{2,1},{3,2},{4,3},{5,4},{6,5},{7,6},{8,7},{9,8},{10,9},{11,1... | collective-permute-start | bytes 61448 | tf_op jit(solution)/shard_map/ppermute | solution.py:17
  8.7 1.2 %convert_reduce_fusion.1 = (f32[8]{0:T(128)S(1)}, bf16[11,11,8,128]{3,2,1,0:T(8,128)(2,1)S(1)}) fusion(bf16[11,11,128,128]{3,2,1,0:T(8,128)(2,1)} %param.5, s32[]{:T(128)S(6)} %select_n.3), kind=kLoop, calls=%fused_computation.38 | loop fusion | flops 247800 | bytes 495652 | tf_op jit(solution)/shard_map/reduce_sum | solution.py:98
  9.9 3.2 %collective-permute-done.1 = bf16[8,5,256]{2,0,1:T(8,128)(2,1)S(1)} collective-permute-done((bf16[8,5,256]{2,0,1:T(8,128)(2,1)S(1)}, bf16[8,5,256]{2,0,1:T(8,128)(2,1)S(1)}, u32[]{:S(2)}, u32[]{:S(2)}) %collective-permute-start.1) | collective-permute-done | bytes 20512 | tf_op jit(solution)/shard_map/ppermute | solution.py:17
  13.0 0.1 fusion.51
  13.4 0.1 constant_dynamic-update-slice_fusion.116
  13.7 0.1 constant_dynamic-update-slice_fusion.111
  13.8 0.1 constant_dynamic-update-slice_fusion.110
  14.2 0.1 constant_dynamic-update-slice_fusion.105
  14.5 0.1 constant_dynamic-update-slice_fusion.100
  14.6 0.1 constant_dynamic-update-slice_fusion.99
  14.9 0.1 constant_dynamic-update-slice_fusion.94
  15.2 0.1 constant_dynamic-update-slice_fusion.89
  15.3 0.1 constant_dynamic-update-slice_fusion.88
  15.7 0.1 constant_dynamic-update-slice_fusion.83
  17.6 0.1 constant_dynamic-update-slice_fusion.55
  17.9 0.1 constant_dynamic-update-slice_fusion.50
  18.7 0.1 constant_dynamic-update-slice_fusion.39
  19.0 0.1 constant_dynamic-update-slice_fusion.34
  19.8 0.1 constant_dynamic-update-slice_fusion.23
  20.5 0.1 constant_dynamic-update-slice_fusion.12
  21.0 0.1 constant_dynamic-update-slice_fusion.6
  21.3 0.1 constant_dynamic-update-slice_fusion.1
  21.5 0.8 fusion.1
  22.3 24.7 %all_to_all.10 = bf16[16,8,8,256]{3,1,2,0:T(8,128)(2,1)S(1)} all-to-all(bf16[16,8,8,256]{3,1,2,0:T(8,128)(2,1)S(1)} %copy.506), channel_id=1, replica_groups=mesh['depth'=16,'tile'=32] {'depth'}, dimensions={0} | all-to-all | bytes 1048576 | tf_op jit(solution)/shard_map/all_to_all | solution.py:31
  47.1 5.3 %collective-permute-start.2 = (bf16[8,5,256]{2,0,1:T(8,128)(2,1)S(1)}, bf16[8,5,256]{2,0,1:T(8,128)(2,1)S(1)}, u32[]{:S(2)}, u32[]{:S(2)}) collective-permute-start(bf16[8,5,256]{2,0,1:T(8,128)(2,1)S(1)} %get-tuple-element.18), channel_id=1, source_target_pairs={{0,1},{1,2},{2,3},{3,4},{4,5},{5,6},{6,7},{7,8},{8,9},{9,10},{10,1... | collective-permute-start | bytes 61448 | tf_op jit(solution)/shard_map/ppermute | solution.py:15
  52.4 1.9 %collective-permute-start.3 = (bf16[8,5,256]{2,0,1:T(8,128)(2,1)S(1)}, bf16[8,5,256]{2,0,1:T(8,128)(2,1)S(1)}, u32[]{:S(2)}, u32[]{:S(2)}) collective-permute-start(bf16[8,5,256]{2,0,1:T(8,128)(2,1)S(1)} %get-tuple-element.19), channel_id=1, source_target_pairs={{1,0},{2,1},{3,2},{4,3},{5,4},{6,5},{7,6},{8,7},{9,8},{10,9},{11,1... | collective-permute-start | bytes 61448 | tf_op jit(solution)/shard_map/ppermute | solution.py:17
  54.3 4.4 %collective-permute-done.3 = bf16[8,5,256]{2,0,1:T(8,128)(2,1)S(1)} collective-permute-done((bf16[8,5,256]{2,0,1:T(8,128)(2,1)S(1)}, bf16[8,5,256]{2,0,1:T(8,128)(2,1)S(1)}, u32[]{:S(2)}, u32[]{:S(2)}) %collective-permute-start.3) | collective-permute-done | bytes 20512 | tf_op jit(solution)/shard_map/ppermute | solution.py:17
  58.7 1.1 %broadcast_in_dim.2 = bf16[16,8,18,256]{3,1,2,0:T(8,128)(2,1)} broadcast(bf16[8,18,256]{2,0,1:T(8,128)(2,1)S(1)} %pad_maximum_fusion), dimensions={1,2,3} | broadcast | bytes 1253376 | tf_op jit(solution)/shard_map/broadcast_in_dim | solution.py:43
  59.8 4.1 %all-to-all-start.1 = ((bf16[16,8,18,256]{3,1,2,0:T(8,128)(2,1)}), bf16[16,8,18,256]{3,1,2,0:T(8,128)(2,1)S(1)}, u32[]{:S(2)}, u32[]{:S(2)}) async-start(bf16[16,8,18,256]{3,1,2,0:T(8,128)(2,1)} %broadcast_in_dim.2), calls=%async_computation.1 | async-start | bytes 2359296 | tf_op jit(solution)/shard_map/all_to_all | solution.py:43
  63.9 0.9 constant_dynamic-slice_fusion.10
  64.9 29.1 %all-to-all-done.1 = bf16[16,8,18,256]{3,1,2,0:T(8,128)(2,1)S(1)} async-done(((bf16[16,8,18,256]{3,1,2,0:T(8,128)(2,1)}), bf16[16,8,18,256]{3,1,2,0:T(8,128)(2,1)S(1)}, u32[]{:S(2)}, u32[]{:S(2)}) %all-to-all-start.1) | async-done | bytes 1179680 | tf_op jit(solution)/shard_map/all_to_all | solution.py:43
  94.1 0.1 copy.538
  94.2 0.7 copy.510
  94.9 0.4 fusion.20
  95.3 0.4 fusion.18
  95.7 0.4 fusion.16
  96.1 0.4 fusion.14
  96.6 0.4 fusion.12
  97.0 0.4 fusion.10
  97.4 0.4 fusion.8
  97.8 0.4 fusion.6
  98.2 0.4 fusion.4
  98.6 0.4 fusion.2
  99.0 0.4 fusion.22
  99.4 1.9 %fusion.54 = f32[8,8,256]{2,0,1:T(8,128)S(1)} fusion(f32[11,8,8,266]{3,1,2,0:T(8,128)S(1)} %fusion.2, f32[11,8,8,266]{3,1,2,0:T(8,128)S(1)} %fusion.4, f32[11,8,8,266]{3,1,2,0:T(8,128)S(1)} %fusion.6, f32[11,8,8,266]{3,1,2,0:T(8,128)S(1)} %fusion.8, f32[11,8,8,266]{3,1,2,0:T(8,128)S(1)} %fusion.10, f32[11,8,8,266]{3,1,2,0:T(8,128)S(1)} %fusion.12, ...), kind=kLoop, calls=%fused_computation.191 | loop fusion | flops 1998848 | bytes 8060960 | tf_op jit(solution)/shard_map/div | solution.py:99
  101.3 0.7 copy.512
  (126 shorter events, 6.9 us)
Async XLA Ops:
  0.0 17.3 %copy-start = (f32[8,8,256]{2,1,0:T(8,128)S(1)}, f32[8,8,256]{2,1,0:T(8,128)}, u32[]{:S(2)}) copy-start(f32[8,8,256]{2,1,0:T(8,128)} %param.3) | copy-start | bytes 196612
  0.9 8.9 %collective-permute-start = (bf16[8,5,256]{2,0,1:T(8,128)(2,1)S(1)}, bf16[8,5,256]{2,0,1:T(8,128)(2,1)S(1)}, u32[]{:S(2)}, u32[]{:S(2)}) collective-permute-start(bf16[8,5,256]{2,0,1:T(8,128)(2,1)S(1)} %get-tuple-element.20), channel_id=1, source_target_pairs={{0,1},{1,2},{2,3},{3,4},{4,5},{5,6},{6,7},{7,8},{8,9},{9,10},{10,1... | collective-permute-start | bytes 61448 | tf_op jit(solution)/shard_map/ppermute | solution.py:15
  6.7 6.3 %collective-permute-start.1 = (bf16[8,5,256]{2,0,1:T(8,128)(2,1)S(1)}, bf16[8,5,256]{2,0,1:T(8,128)(2,1)S(1)}, u32[]{:S(2)}, u32[]{:S(2)}) collective-permute-start(bf16[8,5,256]{2,0,1:T(8,128)(2,1)S(1)} %get-tuple-element.21), channel_id=1, source_target_pairs={{1,0},{2,1},{3,2},{4,3},{5,4},{6,5},{7,6},{8,7},{9,8},{10,9},{11,1... | collective-permute-start | bytes 61448 | tf_op jit(solution)/shard_map/ppermute | solution.py:17
  21.0 26.1 %copy-start.1 = (f32[8,8,256]{2,1,0:T(8,128)S(1)}, f32[8,8,256]{2,1,0:T(8,128)}, u32[]{:S(2)}) copy-start(f32[8,8,256]{2,1,0:T(8,128)} %param.4) | copy-start | bytes 196612
  47.1 7.2 %collective-permute-start.2 = (bf16[8,5,256]{2,0,1:T(8,128)(2,1)S(1)}, bf16[8,5,256]{2,0,1:T(8,128)(2,1)S(1)}, u32[]{:S(2)}, u32[]{:S(2)}) collective-permute-start(bf16[8,5,256]{2,0,1:T(8,128)(2,1)S(1)} %get-tuple-element.18), channel_id=1, source_target_pairs={{0,1},{1,2},{2,3},{3,4},{4,5},{5,6},{6,7},{7,8},{8,9},{9,10},{10,1... | collective-permute-start | bytes 61448 | tf_op jit(solution)/shard_map/ppermute | solution.py:15
  52.4 6.3 %collective-permute-start.3 = (bf16[8,5,256]{2,0,1:T(8,128)(2,1)S(1)}, bf16[8,5,256]{2,0,1:T(8,128)(2,1)S(1)}, u32[]{:S(2)}, u32[]{:S(2)}) collective-permute-start(bf16[8,5,256]{2,0,1:T(8,128)(2,1)S(1)} %get-tuple-element.19), channel_id=1, source_target_pairs={{1,0},{2,1},{3,2},{4,3},{5,4},{6,5},{7,6},{8,7},{9,8},{10,9},{11,1... | collective-permute-start | bytes 61448 | tf_op jit(solution)/shard_map/ppermute | solution.py:17
  59.8 34.3 %all-to-all-start.1 = ((bf16[16,8,18,256]{3,1,2,0:T(8,128)(2,1)}), bf16[16,8,18,256]{3,1,2,0:T(8,128)(2,1)S(1)}, u32[]{:S(2)}, u32[]{:S(2)}) async-start(bf16[16,8,18,256]{3,1,2,0:T(8,128)(2,1)} %broadcast_in_dim.2), calls=%async_computation.1 | async-start | bytes 2359296 | tf_op jit(solution)/shard_map/all_to_all | solution.py:43
where the time goes:
time: 102 us
  waiting for transfers between devices  36.7 us (36%)
  blocking collectives  24.7 us (24%)
  starting transfers between devices  18.9 us (19%)
  local copies, waits for them, and re-layouts  12.7 us (12%)
  matrix products  5.23 us (5%)
  other arithmetic  3.36 us (3%)
    all_to_all x1, waiting for transfers between devices, copy_for_each(): lax.all_to_all(jnp.broadcast_to(x[None], (length, *x.shape)), axis, 0, 0,...  29.1 us
    all_to_all x1, blocking collectives, sum_at_owner(): blocks = lax.all_to_all(split_up(x, dim, length), axis, 0, 0, tiled=True)  24.7 us
    ppermute x2, starting transfers between devices, extended(): lax.ppermute(tail, axis, [(i, (i + 1) % count) for i in range(ends)])  11 us
    unnamed x115, local copies, waits for them, and re-layouts  8.93 us
    ppermute x2, waiting for transfers between devices, extended(): lax.ppermute(head, axis, [((i + 1) % count, i) for i in range(ends)])  7.56 us
    dot_general x11, matrix products, correlate_products(): jnp.einsum(pattern, row_slab, kernel[row_shift], preferred_element_type=j...  4.46 us
    all_to_all x1, starting transfers between devices, copy_for_each(): lax.all_to_all(jnp.broadcast_to(x[None], (length, *x.shape)), axis, 0, 0,...  4.06 us
    ppermute x2, starting transfers between devices, extended(): lax.ppermute(head, axis, [((i + 1) % count, i) for i in range(ends)])  3.84 us
  transfers between devices with their start and end apart: 5, of which 3 were waited for; matrix products, arithmetic and copies ran while one was open for 2% of the time, Pallas kernels for 0%

commit v1 on v0

v1 whole, which is shorter than its diff:
```python
import jax
import jax.numpy as jnp
from jax import lax
from jax.experimental import pallas as pl
from jax.experimental.pallas import tpu as pltpu
from jax.sharding import PartitionSpec as P

R = 5
E = 11
Z = 128
TILES = 16
W = 16
H = 8
S = 32
F32 = jnp.float32
BF16 = jnp.bfloat16
VM = pl.BlockSpec(memory_space=pltpu.VMEM)
PARAMS = pltpu.CompilerParams(vmem_limit_bytes=40 * 1024 * 1024)


def lanes(shape=(8, 128)):
    return lax.broadcasted_iota(jnp.int32, shape, 1)


def pack_kernel(vol_ref, meas_ref, out_ref):
    lane = lanes()
    slot = lane // S
    inside = lane % S
    rolled = {}

    def turned(ref, key, y, half, shift):
        name = (key, y, half, shift % 128)
        if name not in rolled:
            part = ref[:, y, half * 128 : half * 128 + 128]
            rolled[name] = pltpu.roll(part, shift % 128, 1) if shift % 128 else part
        return rolled[name]

    def window(t, y):
        start = W * t - R
        shift = S * (y % 4) - start
        low, high = max(start, 0) // 128, min(start + W + 2 * R - 1, 255) // 128
        value = turned(vol_ref, 0, y, low, shift)
        if high != low:
            value = jnp.where(inside < 128 - start, value, turned(vol_ref, 0, y, high, shift))
        if start < 0:
            value = jnp.where(inside < -start, 0.0, value)
        if start + W + 2 * R > 256:
            value = jnp.where(inside < 256 - start, value, 0.0)
        return value

    for t in range(TILES):
        for g in range(2):
            value = window(t, 4 * g)
            for s in range(1, 4):
                value = jnp.where(slot < s, value, window(t, 4 * g + s))
            out_ref[t, :, g * 128 : g * 128 + 128] = value.astype(BF16)
        value = turned(meas_ref, 1, 0, t // 8, -W * t)
        for y in range(1, H):
            value = jnp.where(lane < W * y, value, turned(meas_ref, 1, y, t // 8, W * y - W * t))
        head = value.astype(BF16)
        out_ref[t, :, 256:384] = head
        out_ref[t, :, 384:512] = (value - head.astype(F32)).astype(BF16)


def ratio_kernel(own_ref, up_ref, down_ref, psf_ref, out_ref, rows_ref, taps_ref):
    def group(ref, g):
        return ref[:, :, g * 128 : g * 128 + 128].astype(F32).reshape(Z, 128)

    lane = lanes((Z, 128))
    mixed = jnp.where(lane < S, group(down_ref, 1), group(up_ref, 0))
    blocks = [mixed, group(up_ref, 1), group(own_ref, 0), group(own_ref, 1), group(down_ref, 0)]
    for i, block in enumerate(blocks):
        rows_ref[i * 128 : i * 128 + 128, :] = block.T
    for y in range(H + 2 * R):
        at = S * ((3 + y) % 20)
        for b in range(E):
            taps_ref[y * W : y * W + W, b * 128 : b * 128 + 128] = rows_ref[at + b : at + b + W, :].astype(BF16)
    total = jnp.zeros((H * W, Z), F32)
    for a in range(E):
        total = total + jnp.dot(
            taps_ref[a * W : a * W + H * W, :], psf_ref[a].reshape(E * Z, Z), preferred_element_type=F32
        )
    measured = (group(own_ref, 2) + group(own_ref, 3)).T
    out_ref[...] = (measured / total).astype(BF16)


def back_kernel(own_ref, up_ref, down_ref, psf_ref, out_ref, rows_ref, taps_ref):
    rows = H + 2 * R
    pitch = 48
    zeros = jnp.zeros((16, 128), F32)
    for y in range(rows):
        if y < R:
            value = up_ref[(y + H - R) * W : (y + H - R) * W + W, :]
        elif y < R + H:
            value = own_ref[(y - R) * W : (y - R) * W + W, :]
        else:
            value = down_ref[(y - R - H) * W : (y - R - H) * W + W, :]
        rows_ref[y * pitch : y * pitch + 16, :] = zeros
        rows_ref[y * pitch + 16 : y * pitch + 32, :] = value.astype(F32)
        rows_ref[y * pitch + 32 : y * pitch + 48, :] = zeros
    last = lax.broadcasted_iota(jnp.int32, (S, 128), 0) == S - 1
    for y in range(rows):
        for b in range(E):
            start = y * pitch + 16 - b
            value = jnp.where(last, 1.0, rows_ref[start : start + S, :])
            taps_ref[y * S : y * S + S, b * 128 : b * 128 + 128] = value.astype(BF16)
    total = jnp.zeros((Z, H * S), F32)
    for a in range(E):
        kernel = jnp.concatenate([psf_ref[a, b] for b in range(E)], axis=1)
        start = (2 * R - a) * S
        total = total + lax.dot_general(
            kernel, taps_ref[start : start + H * S, :], (((1,), (1,)), ((), ())), preferred_element_type=F32
        )
    out_ref[...] = total.reshape(TILES, 8, H * S)


def final_kernel(parts_ref, vol_ref, out_ref):
    lane = lanes()
    weight = parts_ref[0, :, S - 1 : S]

    for y in range(H):
        g, s = y // 4, y % 4
        turned = []
        for t in range(TILES):
            part = parts_ref[t, :, g * 128 : g * 128 + 128]
            shift = (W * t - R - S * s) % 128
            turned.append(pltpu.roll(part, shift, 1) if shift else part)
        for half in range(2):
            sums = [None, None]
            for t in range(TILES):
                start, stop = W * t - R - 128 * half, W * t + W + R - 128 * half
                start, stop = max(start, 0), min(stop, 128)
                if start >= stop:
                    continue
                before = sums[t % 2]
                sums[t % 2] = jnp.where(
                    (lane >= start) & (lane < stop), turned[t], 0.0 if before is None else before
                )
            here = slice(half * 128, half * 128 + 128)
            out_ref[:, y, here] = vol_ref[:, y, here] * (sums[0] + sums[1]) / weight


def both_ways(x, axis):
    count = lax.axis_size(axis)
    down = lax.ppermute(x, axis, [(i, i + 1) for i in range(count - 1)])
    up = lax.ppermute(x, axis, [(i + 1, i) for i in range(count - 1)])
    return down, up


def body(volume, measured, point_spread):
    packed = pl.pallas_call(
        pack_kernel,
        out_shape=jax.ShapeDtypeStruct((TILES, 8, 512), BF16),
        in_specs=[VM, VM],
        out_specs=VM,
        compiler_params=PARAMS,
        name="pack",
    )(volume, measured)
    own = lax.all_to_all(packed, "depth", 0, 0, tiled=True)
    above, below = both_ways(own[:, :, :256], "tile")
    ratio = pl.pallas_call(
        ratio_kernel,
        out_shape=jax.ShapeDtypeStruct((H * W, Z), BF16),
        in_specs=[VM] * 4,
        out_specs=VM,
        scratch_shapes=[
            pltpu.VMEM((5 * 128, 128), F32),
            pltpu.VMEM(((H + 2 * R) * W, E * Z), BF16),
        ],
        compiler_params=PARAMS,
        name="ratio",
    )(own, above, below, point_spread)
    above, below = both_ways(ratio, "tile")
    shares = pl.pallas_call(
        back_kernel,
        out_shape=jax.ShapeDtypeStruct((TILES, 8, H * S), F32),
        in_specs=[VM] * 4,
        out_specs=VM,
        scratch_shapes=[
            pltpu.VMEM(((H + 2 * R) * 48, 128), F32),
            pltpu.VMEM(((H + 2 * R) * S, E * Z), BF16),
        ],
        compiler_params=PARAMS,
        name="back",
    )(ratio, above, below, point_spread)
    parts = lax.all_to_all(shares, "depth", 0, 0, tiled=True)
    return pl.pallas_call(
        final_kernel,
        out_shape=jax.ShapeDtypeStruct(volume.shape, F32),
        in_specs=[VM, VM],
        out_specs=VM,
        compiler_params=PARAMS,
        name="final",
    )(parts, volume)


def solution(mesh):
    in_specs = (P("depth", "tile", None), P("depth", "tile", None), P())
    out_specs = P("depth", "tile", None)
    return jax.shard_map(body, mesh=mesh, in_specs=in_specs, out_specs=out_specs, check_vma=False)
```

time: 102 us -> 68.8 us (0.67)
  the two profiles are of different devices: /device:TPU:193 before, /device:TPU:8 now
where the time goes in v1:
time: 68.8 us; the launch traced here: 68.4 us
  blocking collectives  33 us (48%)
  starting transfers between devices  15.9 us (23%)
  waiting for transfers between devices  10.7 us (16%)
  Pallas kernels  4.94 us (7%)
  local copies, waits for them, and re-layouts  3.81 us (6%)
    all_to_all x1, blocking collectives, body(): own = lax.all_to_all(packed, 'depth', 0, 0, tiled=True)  19.1 us
    all_to_all x1, blocking collectives, body(): parts = lax.all_to_all(shares, 'depth', 0, 0, tiled=True)  13.9 us
    ppermute x2, starting transfers between devices, both_ways(): up = lax.ppermute(x, axis, [(i + 1, i) for i in range(count - 1)])  11.5 us
    ppermute x2, waiting for transfers between devices, both_ways(): down = lax.ppermute(x, axis, [(i, i + 1) for i in range(count - 1)])  10.7 us
    ppermute x2, starting transfers between devices, both_ways(): down = lax.ppermute(x, axis, [(i, i + 1) for i in range(count - 1)])  4.33 us
    unnamed x8, local copies, waits for them, and re-layouts  3.8 us
    pallas_call x1, Pallas kernels, body(): pl.pallas_call(back_kernel, out_shape=jax.ShapeDtypeStruct((TILES, 8, H *...  2.52 us
  transfers between devices with their start and end apart: 4, of which 2 were waited for; matrix products, arithmetic and copies ran while one was open for 0% of the time, Pallas kernels for 0%

profile of v1, /device:TPU:8, one launch (start us, length us, event | category | flops | bytes accessed | tf_op | source)
XLA Modules:
  0.0 68.4 jit_solution(5591605173573405624)
XLA Ops:
  0.0 0.0 copy-start.2
  0.0 0.8 %copy-done.2 = f32[8,8,256]{2,1,0:T(8,128)S(1)} copy-done((f32[8,8,256]{2,1,0:T(8,128)S(1)}, f32[8,8,256]{2,1,0:T(8,128)}, u32[]{:S(2)}) %copy-start.2) | copy-done | bytes 65560
  0.8 0.0 copy-start.3
  0.8 0.8 %copy-done.3 = f32[8,8,256]{2,1,0:T(8,128)S(1)} copy-done((f32[8,8,256]{2,1,0:T(8,128)S(1)}, f32[8,8,256]{2,1,0:T(8,128)}, u32[]{:S(2)}) %copy-start.3) | copy-done | bytes 65560
  1.7 0.3 pack.1
  2.0 19.1 %all_to_all.10.own_ref = bf16[16,8,512]{2,1,0:T(8,128)(2,1)S(1)} all-to-all(bf16[16,8,512]{2,1,0:T(8,128)(2,1)S(1)} %pack.1), channel_id=1, replica_groups=mesh['depth'=16,'tile'=32] {'depth'}, dimensions={0} | all-to-all | bytes 262144 | tf_op jit(solution)/shard_map/all_to_all | solution.py:159
  21.0 9.6 %collective-permute-start.1 = (bf16[16,8,256]{2,1,0:T(8,128)(2,1)S(1)}, bf16[16,8,256]{2,1,0:T(8,128)(2,1)S(1)}, u32[]{:S(2)}, u32[]{:S(2)}) collective-permute-start(bf16[16,8,256]{2,1,0:T(8,128)(2,1)S(1)} %slice.4), channel_id=1, source_target_pairs={{1,0},{2,1},{3,2},{4,3},{5,4},{6,5},{7,6},{8,7},{9,8},{10,9},{11,1... | collective-permute-start | bytes 196616 | tf_op jit(solution)/shard_map/ppermute | solution.py:146
  30.7 1.9 %collective-permute-start = (bf16[16,8,256]{2,1,0:T(8,128)(2,1)S(1)}, bf16[16,8,256]{2,1,0:T(8,128)(2,1)S(1)}, u32[]{:S(2)}, u32[]{:S(2)}) collective-permute-start(bf16[16,8,256]{2,1,0:T(8,128)(2,1)S(1)} %slice.4), channel_id=1, source_target_pairs={{0,1},{1,2},{2,3},{3,4},{4,5},{5,6},{6,7},{7,8},{8,9},{9,10},{10,1... | collective-permute-start | bytes 196616 | tf_op jit(solution)/shard_map/ppermute | solution.py:145
  32.6 0.0 collective-permute-done.1.down_ref
  32.6 5.8 %collective-permute-done.up_ref = bf16[16,8,256]{2,1,0:T(8,128)(2,1)S(1)} collective-permute-done((bf16[16,8,256]{2,1,0:T(8,128)(2,1)S(1)}, bf16[16,8,256]{2,1,0:T(8,128)(2,1)S(1)}, u32[]{:S(2)}, u32[]{:S(2)}) %collective-permute-start) | collective-permute-done | bytes 65568 | tf_op jit(solution)/shard_map/ppermute | solution.py:145
  38.4 0.0 copy-start
  38.4 2.1 %copy-done = bf16[11,11,128,128]{3,2,1,0:T(8,128)(2,1)S(1)} copy-done((bf16[11,11,128,128]{3,2,1,0:T(8,128)(2,1)S(1)}, bf16[11,11,128,128]{3,2,1,0:T(8,128)(2,1)}, u32[]{:S(2)}) %copy-start) | copy-done | bytes 3964952
  40.5 0.0 copy-start.1
  40.5 1.3 %ratio.1.own_ref = bf16[128,128]{1,0:T(8,128)(2,1)S(1)} custom-call(bf16[16,8,512]{2,1,0:T(8,128)(2,1)S(1)} %all_to_all.10.own_ref, bf16[16,8,256]{2,1,0:T(8,128)(2,1)S(1)} %collective-permute-done.up_ref, bf16[16,8,256]{2,1,0:T(8,128)(2,1)S(1)} %collective-permute-done.1.down_ref, bf16[11,11,128,128]{3,2,1,0:T(8,128)(2,1)S(1)} %copy-done), custom_call_target="tpu_custom_call" | custom-call | tf_op jit(solution)/shard_map/ratio/pallas_call | solution.py:161
  41.8 1.9 %collective-permute-start.3 = (bf16[128,128]{1,0:T(8,128)(2,1)S(1)}, bf16[128,128]{1,0:T(8,128)(2,1)S(1)}, u32[]{:S(2)}, u32[]{:S(2)}) collective-permute-start(bf16[128,128]{1,0:T(8,128)(2,1)S(1)} %ratio.1.own_ref), channel_id=1, source_target_pairs={{1,0},{2,1},{3,2},{4,3},{5,4},{6,5},{7,6},{8,7},{9,8},{10,9},{11,1... | collective-permute-start | bytes 98312 | tf_op jit(solution)/shard_map/ppermute | solution.py:146
  43.7 2.4 %collective-permute-start.2 = (bf16[128,128]{1,0:T(8,128)(2,1)S(1)}, bf16[128,128]{1,0:T(8,128)(2,1)S(1)}, u32[]{:S(2)}, u32[]{:S(2)}) collective-permute-start(bf16[128,128]{1,0:T(8,128)(2,1)S(1)} %ratio.1.own_ref), channel_id=1, source_target_pairs={{0,1},{1,2},{2,3},{3,4},{4,5},{5,6},{6,7},{7,8},{8,9},{9,10},{10,1... | collective-permute-start | bytes 98312 | tf_op jit(solution)/shard_map/ppermute | solution.py:145
  46.1 0.0 collective-permute-done.3.down_ref
  46.2 4.9 %collective-permute-done.2.up_ref = bf16[128,128]{1,0:T(8,128)(2,1)S(1)} collective-permute-done((bf16[128,128]{1,0:T(8,128)(2,1)S(1)}, bf16[128,128]{1,0:T(8,128)(2,1)S(1)}, u32[]{:S(2)}, u32[]{:S(2)}) %collective-permute-start.2) | collective-permute-done | bytes 32800 | tf_op jit(solution)/shard_map/ppermute | solution.py:145
  51.1 0.0 copy-done.1
  51.1 2.5 %back.1 = f32[16,8,256]{2,1,0:T(8,128)S(1)} custom-call(bf16[128,128]{1,0:T(8,128)(2,1)S(1)} %ratio.1.own_ref, bf16[128,128]{1,0:T(8,128)(2,1)S(1)} %collective-permute-done.2.up_ref, bf16[128,128]{1,0:T(8,128)(2,1)S(1)} %collective-permute-done.3.down_ref, bf16[11,11,128,128]{3,2,1,0:T(8,128)(2,1)S(1)} %copy-done.1), custom_call_target="tpu_custom_call" | custom-call | tf_op jit(solution)/shard_map/back/pallas_call | solution.py:174
  53.6 13.9 %all_to_all.11.parts_ref = f32[16,8,256]{2,1,0:T(8,128)S(1)} all-to-all(f32[16,8,256]{2,1,0:T(8,128)S(1)} %back.1), channel_id=1, replica_groups=mesh['depth'=16,'tile'=32] {'depth'}, dimensions={0} | all-to-all | bytes 262144 | tf_op jit(solution)/shard_map/all_to_all | solution.py:186
  67.5 0.8 %final.1 = f32[8,8,256]{2,1,0:T(8,128)} custom-call(f32[16,8,256]{2,1,0:T(8,128)S(1)} %all_to_all.11.parts_ref, f32[8,8,256]{2,1,0:T(8,128)S(1)} %copy-done.2), custom_call_target="tpu_custom_call" | custom-call | tf_op jit(solution)/shard_map/final/pallas_call | solution.py:187
  (1 shorter events, 0.0 us)
Async XLA Ops:
  0.0 0.8 %copy-start.2 = (f32[8,8,256]{2,1,0:T(8,128)S(1)}, f32[8,8,256]{2,1,0:T(8,128)}, u32[]{:S(2)}) copy-start(f32[8,8,256]{2,1,0:T(8,128)} %vol_ref.3) | copy-start | bytes 196612
  0.8 0.8 %copy-start.3 = (f32[8,8,256]{2,1,0:T(8,128)S(1)}, f32[8,8,256]{2,1,0:T(8,128)}, u32[]{:S(2)}) copy-start(f32[8,8,256]{2,1,0:T(8,128)} %meas_ref.1) | copy-start | bytes 196612
  21.0 11.5 %collective-permute-start.1 = (bf16[16,8,256]{2,1,0:T(8,128)(2,1)S(1)}, bf16[16,8,256]{2,1,0:T(8,128)(2,1)S(1)}, u32[]{:S(2)}, u32[]{:S(2)}) collective-permute-start(bf16[16,8,256]{2,1,0:T(8,128)(2,1)S(1)} %slice.4), channel_id=1, source_target_pairs={{1,0},{2,1},{3,2},{4,3},{5,4},{6,5},{7,6},{8,7},{9,8},{10,9},{11,1... | collective-permute-start | bytes 196616 | tf_op jit(solution)/shard_map/ppermute | solution.py:146
  30.7 7.7 %collective-permute-start = (bf16[16,8,256]{2,1,0:T(8,128)(2,1)S(1)}, bf16[16,8,256]{2,1,0:T(8,128)(2,1)S(1)}, u32[]{:S(2)}, u32[]{:S(2)}) collective-permute-start(bf16[16,8,256]{2,1,0:T(8,128)(2,1)S(1)} %slice.4), channel_id=1, source_target_pairs={{0,1},{1,2},{2,3},{3,4},{4,5},{5,6},{6,7},{7,8},{8,9},{9,10},{10,1... | collective-permute-start | bytes 196616 | tf_op jit(solution)/shard_map/ppermute | solution.py:145
  38.4 2.1 %copy-start = (bf16[11,11,128,128]{3,2,1,0:T(8,128)(2,1)S(1)}, bf16[11,11,128,128]{3,2,1,0:T(8,128)(2,1)}, u32[]{:S(2)}) copy-start(bf16[11,11,128,128]{3,2,1,0:T(8,128)(2,1)} %psf_ref.3) | copy-start | bytes 11894788
  40.5 10.6 %copy-start.1 = (bf16[11,11,128,128]{3,2,1,0:T(8,128)(2,1)S(1)}, bf16[11,11,128,128]{3,2,1,0:T(8,128)(2,1)}, u32[]{:S(2)}) copy-start(bf16[11,11,128,128]{3,2,1,0:T(8,128)(2,1)} %psf_ref.3) | copy-start | bytes 11894788
  41.8 4.3 %collective-permute-start.3 = (bf16[128,128]{1,0:T(8,128)(2,1)S(1)}, bf16[128,128]{1,0:T(8,128)(2,1)S(1)}, u32[]{:S(2)}, u32[]{:S(2)}) collective-permute-start(bf16[128,128]{1,0:T(8,128)(2,1)S(1)} %ratio.1.own_ref), channel_id=1, source_target_pairs={{1,0},{2,1},{3,2},{4,3},{5,4},{6,5},{7,6},{8,7},{9,8},{10,9},{11,1... | collective-permute-start | bytes 98312 | tf_op jit(solution)/shard_map/ppermute | solution.py:146
  43.7 7.3 %collective-permute-start.2 = (bf16[128,128]{1,0:T(8,128)(2,1)S(1)}, bf16[128,128]{1,0:T(8,128)(2,1)S(1)}, u32[]{:S(2)}, u32[]{:S(2)}) collective-permute-start(bf16[128,128]{1,0:T(8,128)(2,1)S(1)} %ratio.1.own_ref), channel_id=1, source_target_pairs={{0,1},{1,2},{2,3},{3,4},{4,5},{5,6},{6,7},{7,8},{8,9},{9,10},{10,1... | collective-permute-start | bytes 98312 | tf_op jit(solution)/shard_map/ppermute | solution.py:145

commit v2 on v1

--- a/solution.py
+++ b/solution.py
@@ -15,6 +15,7 @@
 F32 = jnp.float32
 BF16 = jnp.bfloat16
 VM = pl.BlockSpec(memory_space=pltpu.VMEM)
+HBM = pl.BlockSpec(memory_space=pl.ANY)
 PARAMS = pltpu.CompilerParams(vmem_limit_bytes=40 * 1024 * 1024)
 
 
@@ -22,7 +23,14 @@
     return lax.broadcasted_iota(jnp.int32, shape, 1)
 
 
-def pack_kernel(vol_ref, meas_ref, out_ref):
+def pack_kernel(vol_hbm, meas_hbm, out_ref, vol_ref, meas_ref, sems):
+    copies = [
+        pltpu.make_async_copy(vol_hbm, vol_ref, sems.at[0]),
+        pltpu.make_async_copy(meas_hbm, meas_ref, sems.at[1]),
+    ]
+    for copy in copies:
+        copy.start()
+    copies[0].wait()
     lane = lanes()
     slot = lane // S
     inside = lane % S
@@ -54,6 +62,8 @@
             for s in range(1, 4):
                 value = jnp.where(slot < s, value, window(t, 4 * g + s))
             out_ref[t, :, g * 128 : g * 128 + 128] = value.astype(BF16)
+    copies[1].wait()
+    for t in range(TILES):
         value = turned(meas_ref, 1, 0, t // 8, -W * t)
         for y in range(1, H):
             value = jnp.where(lane < W * y, value, turned(meas_ref, 1, y, t // 8, W * y - W * t))
@@ -62,13 +72,21 @@
         out_ref[t, :, 384:512] = (value - head.astype(F32)).astype(BF16)
 
 
-def ratio_kernel(own_ref, up_ref, down_ref, psf_ref, out_ref, rows_ref, taps_ref):
+def ratio_kernel(own_ref, mate_ref, next_ref, psf_ref, out_ref, rows_ref, taps_ref):
     def group(ref, g):
         return ref[:, :, g * 128 : g * 128 + 128].astype(F32).reshape(Z, 128)
 
+    even = lax.axis_index("tile") % 2 == 0
+
+    def above(g):
+        return jnp.where(even, group(next_ref, g), group(mate_ref, g))
+
+    def below(g):
+        return jnp.where(even, group(mate_ref, g), group(next_ref, g))
+
     lane = lanes((Z, 128))
-    mixed = jnp.where(lane < S, group(down_ref, 1), group(up_ref, 0))
-    blocks = [mixed, group(up_ref, 1), group(own_ref, 0), group(own_ref, 1), group(down_ref, 0)]
+    mixed = jnp.where(lane < S, below(1), above(0))
+    blocks = [mixed, above(1), group(own_ref, 0), group(own_ref, 1), below(0)]
     for i, block in enumerate(blocks):
         rows_ref[i * 128 : i * 128 + 128, :] = block.T
     for y in range(H + 2 * R):
@@ -84,17 +102,20 @@
     out_ref[...] = (measured / total).astype(BF16)
 
 
-def back_kernel(own_ref, up_ref, down_ref, psf_ref, out_ref, rows_ref, taps_ref):
+def back_kernel(own_ref, mate_ref, next_ref, psf_ref, out_ref, rows_ref, taps_ref):
     rows = H + 2 * R
     pitch = 48
     zeros = jnp.zeros((16, 128), F32)
+    even = lax.axis_index("tile") % 2 == 0
     for y in range(rows):
         if y < R:
-            value = up_ref[(y + H - R) * W : (y + H - R) * W + W, :]
+            here = slice((y + H - R) * W, (y + H - R) * W + W)
+            value = jnp.where(even, next_ref[here, :].astype(F32), mate_ref[here, :].astype(F32))
         elif y < R + H:
             value = own_ref[(y - R) * W : (y - R) * W + W, :]
         else:
-            value = down_ref[(y - R - H) * W : (y - R - H) * W + W, :]
+            here = slice((y - R - H) * W, (y - R - H) * W + W)
+            value = jnp.where(even, mate_ref[here, :].astype(F32), next_ref[here, :].astype(F32))
         rows_ref[y * pitch : y * pitch + 16, :] = zeros
         rows_ref[y * pitch + 16 : y * pitch + 32, :] = value.astype(F32)
         rows_ref[y * pitch + 32 : y * pitch + 48, :] = zeros
@@ -140,24 +161,30 @@
             out_ref[:, y, here] = vol_ref[:, y, here] * (sums[0] + sums[1]) / weight
 
 
-def both_ways(x, axis):
-    count = lax.axis_size(axis)
-    down = lax.ppermute(x, axis, [(i, i + 1) for i in range(count - 1)])
-    up = lax.ppermute(x, axis, [(i + 1, i) for i in range(count - 1)])
-    return down, up
+def neighbours(x):
+    count = lax.axis_size("tile")
+    chips = [(i, i + 1) for i in range(1, count - 1, 2)] + [(i, i - 1) for i in range(2, count, 2)]
+    cores = [(i, i + 1) for i in range(0, count, 2)] + [(i, i - 1) for i in range(1, count, 2)]
+    return lax.ppermute(x, "tile", cores), lax.ppermute(x, "tile", chips)
 
 
 def body(volume, measured, point_spread):
     packed = pl.pallas_call(
         pack_kernel,
         out_shape=jax.ShapeDtypeStruct((TILES, 8, 512), BF16),
-        in_specs=[VM, VM],
-        out_specs=VM,
-        compiler_params=PARAMS,
+        in_specs=[HBM] * 2,
+        out_specs=VM,
+        scratch_shapes=[
+            pltpu.VMEM(volume.shape, F32),
+            pltpu.VMEM(measured.shape, F32),
+            pltpu.SemaphoreType.DMA((2,)),
+        ],
+        compiler_params=pltpu.CompilerParams(vmem_limit_bytes=56 * 1024 * 1024),
+        cost_estimate=pl.CostEstimate(flops=20_000_000_000, bytes_accessed=2**20, transcendentals=0),
         name="pack",
     )(volume, measured)
     own = lax.all_to_all(packed, "depth", 0, 0, tiled=True)
-    above, below = both_ways(own[:, :, :256], "tile")
+    mate, beyond = neighbours(own[:, :, :256])
     ratio = pl.pallas_call(
         ratio_kernel,
         out_shape=jax.ShapeDtypeStruct((H * W, Z), BF16),
@@ -169,8 +196,8 @@
         ],
         compiler_params=PARAMS,
         name="ratio",
-    )(own, above, below, point_spread)
-    above, below = both_ways(ratio, "tile")
+    )(own, mate, beyond, point_spread)
+    mate, beyond = neighbours(ratio)
     shares = pl.pallas_call(
         back_kernel,
         out_shape=jax.ShapeDtypeStruct((TILES, 8, H * S), F32),
@@ -182,7 +209,7 @@
         ],
         compiler_params=PARAMS,
         name="back",
-    )(ratio, above, below, point_spread)
+    )(ratio, mate, beyond, point_spread)
     parts = lax.all_to_all(shares, "depth", 0, 0, tiled=True)
     return pl.pallas_call(
         final_kernel,

time: 68.8 us -> 60.8 us (0.88)
  waiting for transfers between devices: 10.7 us -> 2.39 us
  local copies, waits for them, and re-layouts: 3.81 us -> 0.01 us
  starting transfers between devices: 15.9 us -> 18.1 us
  Pallas kernels: 4.94 us -> 6.6 us
    ppermute x4, waiting for transfers between devices: 10.7 us -> 2.39 us  [neighbours(): return (lax.ppermute(x, 'tile', cores), lax.ppermute(x, 'tile', chips))]
    unnamed x8 -> x4, local copies, waits for them, and re-layouts: 3.8 us -> 0.01 us
    ppermute x4, starting transfers between devices: 15.9 us -> 18.1 us  [neighbours(): return (lax.ppermute(x, 'tile', cores), lax.ppermute(x, 'tile', chips))]
    pallas_call x1, Pallas kernels: 0.27 us -> 2 us  [body(): pl.pallas_call(pack_kernel, out_shape=jax.ShapeDtypeStruct((TILES, 8, 512...]
  transfers between devices with their start and end apart: 4 -> 4, of which waited for: 2 -> 3; matrix products, arithmetic and copies ran while one was open for 0% -> 0% of each run, Pallas kernels for 0% -> 0%
where the time goes in v2:
time: 60.8 us; the launch traced here: 60.4 us
  blocking collectives  33.2 us (55%)
  starting transfers between devices  18.1 us (30%)
  Pallas kernels  6.6 us (11%)
  waiting for transfers between devices  2.39 us (4%)
    all_to_all x1, blocking collectives, body(): own = lax.all_to_all(packed, 'depth', 0, 0, tiled=True)  19.3 us
    ppermute x4, starting transfers between devices, neighbours(): return (lax.ppermute(x, 'tile', cores), lax.ppermute(x, 'tile', chips))  18.1 us
    all_to_all x1, blocking collectives, body(): parts = lax.all_to_all(shares, 'depth', 0, 0, tiled=True)  13.9 us
    pallas_call x1, Pallas kernels, body(): pl.pallas_call(back_kernel, out_shape=jax.ShapeDtypeStruct((TILES, 8, H *...  2.45 us
    ppermute x4, waiting for transfers between devices, neighbours(): return (lax.ppermute(x, 'tile', cores), lax.ppermute(x, 'tile', chips))  2.39 us
    pallas_call x1, Pallas kernels, body(): pl.pallas_call(pack_kernel, out_shape=jax.ShapeDtypeStruct((TILES, 8, 512...  2 us
    pallas_call x1, Pallas kernels, body(): pl.pallas_call(ratio_kernel, out_shape=jax.ShapeDtypeStruct((H * W, Z), B...  1.31 us
  transfers between devices with their start and end apart: 4, of which 3 were waited for; matrix products, arithmetic and copies ran while one was open for 0% of the time, Pallas kernels for 0%

profile of v2, /device:TPU:8, one launch (start us, length us, event | category | flops | bytes accessed | tf_op | source)
XLA Modules:
  0.0 60.4 jit_solution(16848820225922252860)
XLA Ops:
  0.0 0.0 copy-start
  0.0 2.0 %pack.1 = bf16[16,8,512]{2,1,0:T(8,128)(2,1)} custom-call(f32[8,8,256]{2,1,0:T(8,128)} %vol_ref.1, f32[8,8,256]{2,1,0:T(8,128)} %meas_hbm.1), custom_call_target="tpu_custom_call" | custom-call | flops 20000000000 | bytes 1048576 | tf_op jit(solution)/shard_map/pack/pallas_call | solution.py:172
  2.0 19.3 %all_to_all.10.own_ref = bf16[16,8,512]{2,1,0:T(8,128)(2,1)S(1)} all-to-all(bf16[16,8,512]{2,1,0:T(8,128)(2,1)} %pack.1), channel_id=1, replica_groups=mesh['depth'=16,'tile'=32] {'depth'}, dimensions={0} | all-to-all | bytes 262144 | tf_op jit(solution)/shard_map/all_to_all | solution.py:186
  21.3 0.0 copy-start.1
  21.3 9.8 %collective-permute-start.1 = (bf16[16,8,256]{2,1,0:T(8,128)(2,1)S(1)}, bf16[16,8,256]{2,1,0:T(8,128)(2,1)S(1)}, u32[]{:S(2)}, u32[]{:S(2)}) collective-permute-start(bf16[16,8,256]{2,1,0:T(8,128)(2,1)S(1)} %slice.4), channel_id=1, source_target_pairs={{1,2},{3,4},{5,6},{7,8},{9,10},{11,12},{13,14},{15,16},{17,18},{19... | collective-permute-start | bytes 196616 | tf_op jit(solution)/shard_map/ppermute | solution.py:168
  31.1 1.9 %collective-permute-start = (bf16[16,8,256]{2,1,0:T(8,128)(2,1)S(1)}, bf16[16,8,256]{2,1,0:T(8,128)(2,1)S(1)}, u32[]{:S(2)}, u32[]{:S(2)}) collective-permute-start(bf16[16,8,256]{2,1,0:T(8,128)(2,1)S(1)} %slice.4), channel_id=1, source_target_pairs={{0,1},{2,3},{4,5},{6,7},{8,9},{10,11},{12,13},{14,15},{16,17},{18,... | collective-permute-start | bytes 196616 | tf_op jit(solution)/shard_map/ppermute | solution.py:168
  33.0 0.0 collective-permute-done.1.next_ref
  33.0 1.2 %collective-permute-done.mate_ref = bf16[16,8,256]{2,1,0:T(8,128)(2,1)S(1)} collective-permute-done((bf16[16,8,256]{2,1,0:T(8,128)(2,1)S(1)}, bf16[16,8,256]{2,1,0:T(8,128)(2,1)S(1)}, u32[]{:S(2)}, u32[]{:S(2)}) %collective-permute-start) | collective-permute-done | bytes 65568 | tf_op jit(solution)/shard_map/ppermute | solution.py:168
  34.2 0.0 copy-done
  34.2 1.3 %ratio.1.own_ref = bf16[128,128]{1,0:T(8,128)(2,1)S(1)} custom-call(bf16[16,8,512]{2,1,0:T(8,128)(2,1)S(1)} %all_to_all.10.own_ref, bf16[16,8,256]{2,1,0:T(8,128)(2,1)S(1)} %collective-permute-done.mate_ref, bf16[16,8,256]{2,1,0:T(8,128)(2,1)S(1)} %collective-permute-done.1.next_ref, bf16[11,11,128,128]{3,2,1,0:T(8,128)(2,1)S(1)} %copy-done), custom_call_target="tpu_custom_call" | custom-call | tf_op jit(solution)/shard_map/ratio/pallas_call | solution.py:188
  35.5 4.5 %collective-permute-start.3 = (bf16[128,128]{1,0:T(8,128)(2,1)S(1)}, bf16[128,128]{1,0:T(8,128)(2,1)S(1)}, u32[]{:S(2)}, u32[]{:S(2)}) collective-permute-start(bf16[128,128]{1,0:T(8,128)(2,1)S(1)} %ratio.1.own_ref), channel_id=1, source_target_pairs={{1,2},{3,4},{5,6},{7,8},{9,10},{11,12},{13,14},{15,16},{17,18},{19... | collective-permute-start | bytes 98312 | tf_op jit(solution)/shard_map/ppermute | solution.py:168
  40.1 1.9 %collective-permute-start.2 = (bf16[128,128]{1,0:T(8,128)(2,1)S(1)}, bf16[128,128]{1,0:T(8,128)(2,1)S(1)}, u32[]{:S(2)}, u32[]{:S(2)}) collective-permute-start(bf16[128,128]{1,0:T(8,128)(2,1)S(1)} %ratio.1.own_ref), channel_id=1, source_target_pairs={{0,1},{2,3},{4,5},{6,7},{8,9},{10,11},{12,13},{14,15},{16,17},{18,... | collective-permute-start | bytes 98312 | tf_op jit(solution)/shard_map/ppermute | solution.py:168
  42.0 0.9 %collective-permute-done.3.next_ref = bf16[128,128]{1,0:T(8,128)(2,1)S(1)} collective-permute-done((bf16[128,128]{1,0:T(8,128)(2,1)S(1)}, bf16[128,128]{1,0:T(8,128)(2,1)S(1)}, u32[]{:S(2)}, u32[]{:S(2)}) %collective-permute-start.3) | collective-permute-done | bytes 32800 | tf_op jit(solution)/shard_map/ppermute | solution.py:168
  42.9 0.3 collective-permute-done.2.mate_ref
  43.2 2.5 %back.1 = f32[16,8,256]{2,1,0:T(8,128)S(1)} custom-call(bf16[128,128]{1,0:T(8,128)(2,1)S(1)} %ratio.1.own_ref, bf16[128,128]{1,0:T(8,128)(2,1)S(1)} %collective-permute-done.2.mate_ref, bf16[128,128]{1,0:T(8,128)(2,1)S(1)} %collective-permute-done.3.next_ref, bf16[11,11,128,128]{3,2,1,0:T(8,128)(2,1)S(1)} %copy-done), custom_call_target="tpu_custom_call" | custom-call | tf_op jit(solution)/shard_map/back/pallas_call | solution.py:201
  45.7 13.9 %all_to_all.11.parts_ref = f32[16,8,256]{2,1,0:T(8,128)S(1)} all-to-all(f32[16,8,256]{2,1,0:T(8,128)S(1)} %back.1), channel_id=1, replica_groups=mesh['depth'=16,'tile'=32] {'depth'}, dimensions={0} | all-to-all | bytes 262144 | tf_op jit(solution)/shard_map/all_to_all | solution.py:213
  59.6 0.0 copy-done.1
  59.6 0.8 %final.1 = f32[8,8,256]{2,1,0:T(8,128)} custom-call(f32[16,8,256]{2,1,0:T(8,128)S(1)} %all_to_all.11.parts_ref, f32[8,8,256]{2,1,0:T(8,128)S(1)} %copy-done.1), custom_call_target="tpu_custom_call" | custom-call | tf_op jit(solution)/shard_map/final/pallas_call | solution.py:214
  (1 shorter events, 0.0 us)
Async XLA Ops:
  0.0 34.2 %copy-start = (bf16[11,11,128,128]{3,2,1,0:T(8,128)(2,1)S(1)}, bf16[11,11,128,128]{3,2,1,0:T(8,128)(2,1)}, u32[]{:S(2)}) copy-start(bf16[11,11,128,128]{3,2,1,0:T(8,128)(2,1)} %psf_ref.3) | copy-start | bytes 11894788
  21.3 38.3 %copy-start.1 = (f32[8,8,256]{2,1,0:T(8,128)S(1)}, f32[8,8,256]{2,1,0:T(8,128)}, u32[]{:S(2)}) copy-start(f32[8,8,256]{2,1,0:T(8,128)} %vol_ref.1) | copy-start | bytes 196612
  21.3 11.7 %collective-permute-start.1 = (bf16[16,8,256]{2,1,0:T(8,128)(2,1)S(1)}, bf16[16,8,256]{2,1,0:T(8,128)(2,1)S(1)}, u32[]{:S(2)}, u32[]{:S(2)}) collective-permute-start(bf16[16,8,256]{2,1,0:T(8,128)(2,1)S(1)} %slice.4), channel_id=1, source_target_pairs={{1,2},{3,4},{5,6},{7,8},{9,10},{11,12},{13,14},{15,16},{17,18},{19... | collective-permute-start | bytes 196616 | tf_op jit(solution)/shard_map/ppermute | solution.py:168
  31.1 3.1 %collective-permute-start = (bf16[16,8,256]{2,1,0:T(8,128)(2,1)S(1)}, bf16[16,8,256]{2,1,0:T(8,128)(2,1)S(1)}, u32[]{:S(2)}, u32[]{:S(2)}) collective-permute-start(bf16[16,8,256]{2,1,0:T(8,128)(2,1)S(1)} %slice.4), channel_id=1, source_target_pairs={{0,1},{2,3},{4,5},{6,7},{8,9},{10,11},{12,13},{14,15},{16,17},{18,... | collective-permute-start | bytes 196616 | tf_op jit(solution)/shard_map/ppermute | solution.py:168
  35.5 7.3 %collective-permute-start.3 = (bf16[128,128]{1,0:T(8,128)(2,1)S(1)}, bf16[128,128]{1,0:T(8,128)(2,1)S(1)}, u32[]{:S(2)}, u32[]{:S(2)}) collective-permute-start(bf16[128,128]{1,0:T(8,128)(2,1)S(1)} %ratio.1.own_ref), channel_id=1, source_target_pairs={{1,2},{3,4},{5,6},{7,8},{9,10},{11,12},{13,14},{15,16},{17,18},{19... | collective-permute-start | bytes 98312 | tf_op jit(solution)/shard_map/ppermute | solution.py:168
  40.1 3.1 %collective-permute-start.2 = (bf16[128,128]{1,0:T(8,128)(2,1)S(1)}, bf16[128,128]{1,0:T(8,128)(2,1)S(1)}, u32[]{:S(2)}, u32[]{:S(2)}) collective-permute-start(bf16[128,128]{1,0:T(8,128)(2,1)S(1)} %ratio.1.own_ref), channel_id=1, source_target_pairs={{0,1},{2,3},{4,5},{6,7},{8,9},{10,11},{12,13},{14,15},{16,17},{18,... | collective-permute-start | bytes 98312 | tf_op jit(solution)/shard_map/ppermute | solution.py:168

commit v3 on v2

--- a/solution.py
+++ b/solution.py
@@ -72,7 +72,7 @@
         out_ref[t, :, 384:512] = (value - head.astype(F32)).astype(BF16)
 
 
-def ratio_kernel(own_ref, mate_ref, next_ref, psf_ref, out_ref, rows_ref, taps_ref):
+def update_kernel(own_ref, mate_ref, next_ref, far_up_ref, far_down_ref, psf_ref, out_ref, rows_ref, taps_ref, ratio_ref, back_ref):
     def group(ref, g):
         return ref[:, :, g * 128 : g * 128 + 128].astype(F32).reshape(Z, 128)
 
@@ -84,53 +84,44 @@
     def below(g):
         return jnp.where(even, group(mate_ref, g), group(next_ref, g))
 
-    lane = lanes((Z, 128))
-    mixed = jnp.where(lane < S, below(1), above(0))
-    blocks = [mixed, above(1), group(own_ref, 0), group(own_ref, 1), below(0)]
+    blocks = [group(far_up_ref, 0), above(0), above(1), group(own_ref, 0)]
+    blocks += [group(own_ref, 1), below(0), below(1), group(far_down_ref, 0)]
     for i, block in enumerate(blocks):
         rows_ref[i * 128 : i * 128 + 128, :] = block.T
-    for y in range(H + 2 * R):
-        at = S * ((3 + y) % 20)
+    for y in range(H + 4 * R):
+        at = S * (y + 2)
         for b in range(E):
             taps_ref[y * W : y * W + W, b * 128 : b * 128 + 128] = rows_ref[at + b : at + b + W, :].astype(BF16)
-    total = jnp.zeros((H * W, Z), F32)
+    rows = H + 2 * R
+    total = jnp.zeros((rows * W, Z), F32)
     for a in range(E):
         total = total + jnp.dot(
-            taps_ref[a * W : a * W + H * W, :], psf_ref[a].reshape(E * Z, Z), preferred_element_type=F32
+            taps_ref[a * W : a * W + rows * W, :], psf_ref[a].reshape(E * Z, Z), preferred_element_type=F32
         )
-    measured = (group(own_ref, 2) + group(own_ref, 3)).T
-    out_ref[...] = (measured / total).astype(BF16)
-
-
-def back_kernel(own_ref, mate_ref, next_ref, psf_ref, out_ref, rows_ref, taps_ref):
-    rows = H + 2 * R
+
     pitch = 48
     zeros = jnp.zeros((16, 128), F32)
-    even = lax.axis_index("tile") % 2 == 0
+    measured_up = (above(2) + above(3)).T
+    measured_own = (group(own_ref, 2) + group(own_ref, 3)).T
+    measured_down = (below(2) + below(3)).T
+    measured = jnp.concatenate([measured_up[(H - R) * W :], measured_own, measured_down[: R * W]], axis=0)
+    ratio = (measured / total).astype(BF16).astype(F32)
     for y in range(rows):
-        if y < R:
-            here = slice((y + H - R) * W, (y + H - R) * W + W)
-            value = jnp.where(even, next_ref[here, :].astype(F32), mate_ref[here, :].astype(F32))
-        elif y < R + H:
-            value = own_ref[(y - R) * W : (y - R) * W + W, :]
-        else:
-            here = slice((y - R - H) * W, (y - R - H) * W + W)
-            value = jnp.where(even, mate_ref[here, :].astype(F32), next_ref[here, :].astype(F32))
-        rows_ref[y * pitch : y * pitch + 16, :] = zeros
-        rows_ref[y * pitch + 16 : y * pitch + 32, :] = value.astype(F32)
-        rows_ref[y * pitch + 32 : y * pitch + 48, :] = zeros
+        ratio_ref[y * pitch : y * pitch + 16, :] = zeros
+        ratio_ref[y * pitch + 16 : y * pitch + 32, :] = ratio[y * W : y * W + W]
+        ratio_ref[y * pitch + 32 : y * pitch + 48, :] = zeros
     last = lax.broadcasted_iota(jnp.int32, (S, 128), 0) == S - 1
     for y in range(rows):
         for b in range(E):
             start = y * pitch + 16 - b
-            value = jnp.where(last, 1.0, rows_ref[start : start + S, :])
-            taps_ref[y * S : y * S + S, b * 128 : b * 128 + 128] = value.astype(BF16)
+            value = jnp.where(last, 1.0, ratio_ref[start : start + S, :])
+            back_ref[y * S : y * S + S, b * 128 : b * 128 + 128] = value.astype(BF16)
     total = jnp.zeros((Z, H * S), F32)
     for a in range(E):
         kernel = jnp.concatenate([psf_ref[a, b] for b in range(E)], axis=1)
         start = (2 * R - a) * S
         total = total + lax.dot_general(
-            kernel, taps_ref[start : start + H * S, :], (((1,), (1,)), ((), ())), preferred_element_type=F32
+            kernel, back_ref[start : start + H * S, :], (((1,), (1,)), ((), ())), preferred_element_type=F32
         )
     out_ref[...] = total.reshape(TILES, 8, H * S)
 
@@ -165,7 +156,11 @@
     count = lax.axis_size("tile")
     chips = [(i, i + 1) for i in range(1, count - 1, 2)] + [(i, i - 1) for i in range(2, count, 2)]
     cores = [(i, i + 1) for i in range(0, count, 2)] + [(i, i - 1) for i in range(1, count, 2)]
-    return lax.ppermute(x, "tile", cores), lax.ppermute(x, "tile", chips)
+    mate = lax.ppermute(x, "tile", cores)
+    far_down = lax.ppermute(x[:, :, :128], "tile", [(i + 2, i) for i in range(count - 2)])
+    far_up = lax.ppermute(x[:, :, 128:256], "tile", [(i, i + 2) for i in range(count - 2)])
+    beyond = lax.ppermute(x, "tile", chips)
+    return mate, beyond, far_up, far_down
 
 
 def body(volume, measured, point_spread):
@@ -184,32 +179,20 @@
         name="pack",
     )(volume, measured)
     own = lax.all_to_all(packed, "depth", 0, 0, tiled=True)
-    mate, beyond = neighbours(own[:, :, :256])
-    ratio = pl.pallas_call(
-        ratio_kernel,
-        out_shape=jax.ShapeDtypeStruct((H * W, Z), BF16),
-        in_specs=[VM] * 4,
+    shares = pl.pallas_call(
+        update_kernel,
+        out_shape=jax.ShapeDtypeStruct((TILES, 8, H * S), F32),
+        in_specs=[VM] * 6,
         out_specs=VM,
         scratch_shapes=[
-            pltpu.VMEM((5 * 128, 128), F32),
-            pltpu.VMEM(((H + 2 * R) * W, E * Z), BF16),
-        ],
-        compiler_params=PARAMS,
-        name="ratio",
-    )(own, mate, beyond, point_spread)
-    mate, beyond = neighbours(ratio)
-    shares = pl.pallas_call(
-        back_kernel,
-        out_shape=jax.ShapeDtypeStruct((TILES, 8, H * S), F32),
-        in_specs=[VM] * 4,
-        out_specs=VM,
-        scratch_shapes=[
+            pltpu.VMEM((8 * 128, 128), F32),
+            pltpu.VMEM(((H + 4 * R) * W, E * Z), BF16),
             pltpu.VMEM(((H + 2 * R) * 48, 128), F32),
             pltpu.VMEM(((H + 2 * R) * S, E * Z), BF16),
         ],
         compiler_params=PARAMS,
-        name="back",
-    )(ratio, mate, beyond, point_spread)
+        name="update",
+    )(own, *neighbours(own), point_spread)
     parts = lax.all_to_all(shares, "depth", 0, 0, tiled=True)
     return pl.pallas_call(
         final_kernel,

time: 60.8 us -> 68.5 us (1.13)
  Pallas kernels: 6.6 us -> 11.8 us
  waiting for transfers between devices: 2.39 us -> 5.97 us
  starting transfers between devices: 18.1 us -> 17.4 us
    pallas_call x2 -> x1, Pallas kernels: 3.76 us -> 8.96 us  [body(): pl.pallas_call(update_kernel, out_shape=jax.ShapeDtypeStruct((TILES, 8, H...]
    ppermute x4, waiting for transfers between devices: 2.39 us -> 5.97 us  [the longest x1 5.96 us: neighbours(): lax.ppermute(x[:, :, 128:256], 'tile', [(i, i + 2) for i in range(count -...]
    ppermute x4, starting transfers between devices: 18.1 us -> 17.4 us  [the longest x1 9.61 us: neighbours(): beyond = lax.ppermute(x, 'tile', chips)]
  transfers between devices with their start and end apart: 4 -> 4, of which waited for: 3 -> 1; matrix products, arithmetic and copies ran while one was open for 0% -> 0% of each run, Pallas kernels for 0% -> 0%
where the time goes in v3:
time: 68.5 us; the launch traced here: 68.2 us
  blocking collectives  32.9 us (48%)
  starting transfers between devices  17.4 us (25%)
  Pallas kernels  11.8 us (17%)
  waiting for transfers between devices  5.97 us (9%)
    all_to_all x1, blocking collectives, body(): own = lax.all_to_all(packed, 'depth', 0, 0, tiled=True)  19.3 us
    all_to_all x1, blocking collectives, body(): parts = lax.all_to_all(shares, 'depth', 0, 0, tiled=True)  13.7 us
    ppermute x1, starting transfers between devices, neighbours(): beyond = lax.ppermute(x, 'tile', chips)  9.61 us
    pallas_call x1, Pallas kernels, body(): pl.pallas_call(update_kernel, out_shape=jax.ShapeDtypeStruct((TILES, 8, H...  8.96 us
    ppermute x1, waiting for transfers between devices, neighbours(): lax.ppermute(x[:, :, 128:256], 'tile', [(i, i + 2) for i in range(count -...  5.96 us
    ppermute x1, starting transfers between devices, neighbours(): lax.ppermute(x[:, :, :128], 'tile', [(i + 2, i) for i in range(count - 2)])  3.91 us
    pallas_call x1, Pallas kernels, body(): pl.pallas_call(pack_kernel, out_shape=jax.ShapeDtypeStruct((TILES, 8, 512...  2 us
    ppermute x1, starting transfers between devices, neighbours(): lax.ppermute(x[:, :, 128:256], 'tile', [(i, i + 2) for i in range(count -...  1.94 us
  transfers between devices with their start and end apart: 4, of which 1 were waited for; matrix products, arithmetic and copies ran while one was open for 0% of the time, Pallas kernels for 0%

profile of v3, /device:TPU:8, one launch (start us, length us, event | category | flops | bytes accessed | tf_op | source)
XLA Modules:
  0.0 68.2 jit_solution(3089010316540764951)
XLA Ops:
  0.0 0.0 copy-start
  0.0 2.0 %pack.1 = bf16[16,8,512]{2,1,0:T(8,128)(2,1)} custom-call(f32[8,8,256]{2,1,0:T(8,128)} %vol_ref.1, f32[8,8,256]{2,1,0:T(8,128)} %meas_hbm.1), custom_call_target="tpu_custom_call" | custom-call | flops 20000000000 | bytes 1048576 | tf_op jit(solution)/shard_map/pack/pallas_call | solution.py:167
  2.0 0.0 copy-start.1
  2.0 19.3 %all_to_all.10.own_ref = bf16[16,8,512]{2,1,0:T(8,128)(2,1)S(1)} all-to-all(bf16[16,8,512]{2,1,0:T(8,128)(2,1)} %pack.1), channel_id=1, replica_groups=mesh['depth'=16,'tile'=32] {'depth'}, dimensions={0} | all-to-all | bytes 262144 | tf_op jit(solution)/shard_map/all_to_all | solution.py:181
  21.3 9.6 %collective-permute-start.1 = (bf16[16,8,512]{2,1,0:T(8,128)(2,1)S(1)}, bf16[16,8,512]{2,1,0:T(8,128)(2,1)S(1)}, u32[]{:S(2)}, u32[]{:S(2)}) collective-permute-start(bf16[16,8,512]{2,1,0:T(8,128)(2,1)S(1)} %all_to_all.10.own_ref), channel_id=1, source_target_pairs={{1,2},{3,4},{5,6},{7,8},{9,10},{11,12},{13,14},{15,16},{17,18},{19... | collective-permute-start | bytes 393224 | tf_op jit(solution)/shard_map/ppermute | solution.py:162
  30.9 1.9 %collective-permute-start = (bf16[16,8,512]{2,1,0:T(8,128)(2,1)S(1)}, bf16[16,8,512]{2,1,0:T(8,128)(2,1)S(1)}, u32[]{:S(2)}, u32[]{:S(2)}) collective-permute-start(bf16[16,8,512]{2,1,0:T(8,128)(2,1)S(1)} %all_to_all.10.own_ref), channel_id=1, source_target_pairs={{0,1},{2,3},{4,5},{6,7},{8,9},{10,11},{12,13},{14,15},{16,17},{18,... | collective-permute-start | bytes 393224 | tf_op jit(solution)/shard_map/ppermute | solution.py:159
  32.9 3.9 %collective-permute-start.3 = (bf16[16,8,128]{2,1,0:T(8,128)(2,1)S(1)}, bf16[16,8,128]{2,1,0:T(8,128)(2,1)S(1)}, u32[]{:S(2)}, u32[]{:S(2)}) collective-permute-start(bf16[16,8,128]{2,1,0:T(8,128)(2,1)S(1)} %get-tuple-element.5), channel_id=1, source_target_pairs={{2,0},{3,1},{4,2},{5,3},{6,4},{7,5},{8,6},{9,7},{10,8},{11,9},{12,... | collective-permute-start | bytes 98312 | tf_op jit(solution)/shard_map/ppermute | solution.py:160
  36.8 1.9 %collective-permute-start.2 = (bf16[16,8,128]{2,1,0:T(8,128)(2,1)S(1)}, bf16[16,8,128]{2,1,0:T(8,128)(2,1)S(1)}, u32[]{:S(2)}, u32[]{:S(2)}) collective-permute-start(bf16[16,8,128]{2,1,0:T(8,128)(2,1)S(1)} %get-tuple-element.6), channel_id=1, source_target_pairs={{0,2},{1,3},{2,4},{3,5},{4,6},{5,7},{6,8},{7,9},{8,10},{9,11},{10,... | collective-permute-start | bytes 98312 | tf_op jit(solution)/shard_map/ppermute | solution.py:161
  38.7 0.0 collective-permute-done.3.far_down_ref
  38.7 6.0 %collective-permute-done.2.far_up_ref = bf16[16,8,128]{2,1,0:T(8,128)(2,1)S(1)} collective-permute-done((bf16[16,8,128]{2,1,0:T(8,128)(2,1)S(1)}, bf16[16,8,128]{2,1,0:T(8,128)(2,1)S(1)}, u32[]{:S(2)}, u32[]{:S(2)}) %collective-permute-start.2) | collective-permute-done | bytes 32800 | tf_op jit(solution)/shard_map/ppermute | solution.py:161
  44.7 0.0 collective-permute-done.1.next_ref
  44.7 0.0 collective-permute-done.mate_ref
  44.7 0.0 copy-done
  44.7 9.0 %update.1 = f32[16,8,256]{2,1,0:T(8,128)S(1)} custom-call(bf16[16,8,512]{2,1,0:T(8,128)(2,1)S(1)} %all_to_all.10.own_ref, bf16[16,8,512]{2,1,0:T(8,128)(2,1)S(1)} %collective-permute-done.mate_ref, bf16[16,8,512]{2,1,0:T(8,128)(2,1)S(1)} %collective-permute-done.1.next_ref, bf16[16,8,128]{2,1,0:T(8,128)(2,1)S(1)} %collective-permute-done.2.far_up_ref, ...), custom_call_target="tpu_custom_call" | custom-call | tf_op jit(solution)/shard_map/update/pallas_call | solution.py:182
  53.7 13.7 %all_to_all.11.parts_ref = f32[16,8,256]{2,1,0:T(8,128)S(1)} all-to-all(f32[16,8,256]{2,1,0:T(8,128)S(1)} %update.1), channel_id=1, replica_groups=mesh['depth'=16,'tile'=32] {'depth'}, dimensions={0} | all-to-all | bytes 262144 | tf_op jit(solution)/shard_map/all_to_all | solution.py:196
  67.3 0.0 copy-done.1
  67.3 0.8 %final.1 = f32[8,8,256]{2,1,0:T(8,128)} custom-call(f32[16,8,256]{2,1,0:T(8,128)S(1)} %all_to_all.11.parts_ref, f32[8,8,256]{2,1,0:T(8,128)S(1)} %copy-done.1), custom_call_target="tpu_custom_call" | custom-call | tf_op jit(solution)/shard_map/final/pallas_call | solution.py:197
  (1 shorter events, 0.0 us)
Async XLA Ops:
  0.0 44.7 %copy-start = (bf16[11,11,128,128]{3,2,1,0:T(8,128)(2,1)S(1)}, bf16[11,11,128,128]{3,2,1,0:T(8,128)(2,1)}, u32[]{:S(2)}) copy-start(bf16[11,11,128,128]{3,2,1,0:T(8,128)(2,1)} %psf_ref.1) | copy-start | bytes 11894788
  2.0 65.3 %copy-start.1 = (f32[8,8,256]{2,1,0:T(8,128)S(1)}, f32[8,8,256]{2,1,0:T(8,128)}, u32[]{:S(2)}) copy-start(f32[8,8,256]{2,1,0:T(8,128)} %vol_ref.1) | copy-start | bytes 196612
  21.3 23.4 %collective-permute-start.1 = (bf16[16,8,512]{2,1,0:T(8,128)(2,1)S(1)}, bf16[16,8,512]{2,1,0:T(8,128)(2,1)S(1)}, u32[]{:S(2)}, u32[]{:S(2)}) collective-permute-start(bf16[16,8,512]{2,1,0:T(8,128)(2,1)S(1)} %all_to_all.10.own_ref), channel_id=1, source_target_pairs={{1,2},{3,4},{5,6},{7,8},{9,10},{11,12},{13,14},{15,16},{17,18},{19... | collective-permute-start | bytes 393224 | tf_op jit(solution)/shard_map/ppermute | solution.py:162
  30.9 13.8 %collective-permute-start = (bf16[16,8,512]{2,1,0:T(8,128)(2,1)S(1)}, bf16[16,8,512]{2,1,0:T(8,128)(2,1)S(1)}, u32[]{:S(2)}, u32[]{:S(2)}) collective-permute-start(bf16[16,8,512]{2,1,0:T(8,128)(2,1)S(1)} %all_to_all.10.own_ref), channel_id=1, source_target_pairs={{0,1},{2,3},{4,5},{6,7},{8,9},{10,11},{12,13},{14,15},{16,17},{18,... | collective-permute-start | bytes 393224 | tf_op jit(solution)/shard_map/ppermute | solution.py:159
  32.9 5.9 %collective-permute-start.3 = (bf16[16,8,128]{2,1,0:T(8,128)(2,1)S(1)}, bf16[16,8,128]{2,1,0:T(8,128)(2,1)S(1)}, u32[]{:S(2)}, u32[]{:S(2)}) collective-permute-start(bf16[16,8,128]{2,1,0:T(8,128)(2,1)S(1)} %get-tuple-element.5), channel_id=1, source_target_pairs={{2,0},{3,1},{4,2},{5,3},{6,4},{7,5},{8,6},{9,7},{10,8},{11,9},{12,... | collective-permute-start | bytes 98312 | tf_op jit(solution)/shard_map/ppermute | solution.py:160
  36.8 7.9 %collective-permute-start.2 = (bf16[16,8,128]{2,1,0:T(8,128)(2,1)S(1)}, bf16[16,8,128]{2,1,0:T(8,128)(2,1)S(1)}, u32[]{:S(2)}, u32[]{:S(2)}) collective-permute-start(bf16[16,8,128]{2,1,0:T(8,128)(2,1)S(1)} %get-tuple-element.6), channel_id=1, source_target_pairs={{0,2},{1,3},{2,4},{3,5},{4,6},{5,7},{6,8},{7,9},{8,10},{9,11},{10,... | collective-permute-start | bytes 98312 | tf_op jit(solution)/shard_map/ppermute | solution.py:161

commit v4 on v2

--- a/solution.py
+++ b/solution.py
@@ -3,6 +3,7 @@
 from jax import lax
 from jax.experimental import pallas as pl
 from jax.experimental.pallas import tpu as pltpu
+from jax.sharding import Mesh
 from jax.sharding import PartitionSpec as P
 
 R = 5
@@ -72,11 +73,13 @@
         out_ref[t, :, 384:512] = (value - head.astype(F32)).astype(BF16)
 
 
-def ratio_kernel(own_ref, mate_ref, next_ref, psf_ref, out_ref, rows_ref, taps_ref):
+def ratio_kernel(own_ref, chip_ref, next_ref, psf_ref, out_ref, rows_ref, taps_ref):
     def group(ref, g):
         return ref[:, :, g * 128 : g * 128 + 128].astype(F32).reshape(Z, 128)
 
-    even = lax.axis_index("tile") % 2 == 0
+    core = lax.axis_index("core")
+    even = core == 0
+    mate_ref = chip_ref.at[1 - core]
 
     def above(g):
         return jnp.where(even, group(next_ref, g), group(mate_ref, g))
@@ -102,37 +105,41 @@
     out_ref[...] = (measured / total).astype(BF16)
 
 
-def back_kernel(own_ref, mate_ref, next_ref, psf_ref, out_ref, rows_ref, taps_ref):
-    rows = H + 2 * R
-    pitch = 48
-    zeros = jnp.zeros((16, 128), F32)
-    even = lax.axis_index("tile") % 2 == 0
-    for y in range(rows):
+def back_kernel(own_ref, chip_ref, next_ref, psf_ref, out_ref, rows_ref, sum_ref):
+    core = lax.axis_index("core")
+    even = core == 0
+    mate_ref = chip_ref.at[1 - core]
+    for y in range(H + 2 * R):
         if y < R:
             here = slice((y + H - R) * W, (y + H - R) * W + W)
-            value = jnp.where(even, next_ref[here, :].astype(F32), mate_ref[here, :].astype(F32))
+            value = jnp.where(even, next_ref[here, :].astype(F32), mate_ref[here, :].astype(F32)).astype(BF16)
         elif y < R + H:
             value = own_ref[(y - R) * W : (y - R) * W + W, :]
         else:
             here = slice((y - R - H) * W, (y - R - H) * W + W)
-            value = jnp.where(even, mate_ref[here, :].astype(F32), next_ref[here, :].astype(F32))
-        rows_ref[y * pitch : y * pitch + 16, :] = zeros
-        rows_ref[y * pitch + 16 : y * pitch + 32, :] = value.astype(F32)
-        rows_ref[y * pitch + 32 : y * pitch + 48, :] = zeros
-    last = lax.broadcasted_iota(jnp.int32, (S, 128), 0) == S - 1
-    for y in range(rows):
-        for b in range(E):
-            start = y * pitch + 16 - b
-            value = jnp.where(last, 1.0, rows_ref[start : start + S, :])
-            taps_ref[y * S : y * S + S, b * 128 : b * 128 + 128] = value.astype(BF16)
-    total = jnp.zeros((Z, H * S), F32)
-    for a in range(E):
-        kernel = jnp.concatenate([psf_ref[a, b] for b in range(E)], axis=1)
-        start = (2 * R - a) * S
-        total = total + lax.dot_general(
-            kernel, taps_ref[start : start + H * S, :], (((1,), (1,)), ((), ())), preferred_element_type=F32
+            value = jnp.where(even, mate_ref[here, :].astype(F32), next_ref[here, :].astype(F32)).astype(BF16)
+        for a in range(E):
+            row = y + a - 2 * R
+            if 0 <= row < H:
+                rows_ref[row * W : row * W + W, a * 128 : a * 128 + 128] = value
+    rows_ref[H * W : H * W + W, :] = jnp.ones((W, E * Z), BF16)
+    sum_ref[...] = jnp.zeros((H * S, Z), F32)
+    weight = jnp.zeros((1, Z), F32)
+    for first in range(0, E, 2):
+        pair = range(first, min(first + 2, E))
+        kernel = jnp.concatenate(
+            [psf_ref[a, first : first + len(pair)].reshape(len(pair) * Z, Z) for a in range(E)], axis=1
         )
-    out_ref[...] = total.reshape(TILES, 8, H * S)
+        product = lax.dot_general(rows_ref[...], kernel, (((1,), (1,)), ((), ())), preferred_element_type=F32)
+        for i, b in enumerate(pair):
+            part = product[:, i * Z : i * Z + Z]
+            for y in range(H):
+                here = slice(y * S + b, y * S + b + W)
+                sum_ref[here, :] = sum_ref[here, :] + part[y * W : y * W + W]
+            weight = weight + part[H * W : H * W + 1]
+    sum_ref[S - 1 : S, :] = weight
+    for g in range(2):
+        out_ref[:, :, g * 128 : g * 128 + 128] = sum_ref[g * 128 : g * 128 + 128, :].T.reshape(TILES, 8, 128)
 
 
 def final_kernel(parts_ref, vol_ref, out_ref):
@@ -162,10 +169,11 @@
 
 
 def neighbours(x):
-    count = lax.axis_size("tile")
+    tile = ("pair", "core")
+    count = lax.axis_size(tile)
     chips = [(i, i + 1) for i in range(1, count - 1, 2)] + [(i, i - 1) for i in range(2, count, 2)]
-    cores = [(i, i + 1) for i in range(0, count, 2)] + [(i, i - 1) for i in range(1, count, 2)]
-    return lax.ppermute(x, "tile", cores), lax.ppermute(x, "tile", chips)
+    beyond = lax.ppermute(x, tile, chips)
+    return lax.all_gather(x, "core"), beyond
 
 
 def body(volume, measured, point_spread):
@@ -184,7 +192,7 @@
         name="pack",
     )(volume, measured)
     own = lax.all_to_all(packed, "depth", 0, 0, tiled=True)
-    mate, beyond = neighbours(own[:, :, :256])
+    chip, beyond = neighbours(own[:, :, :256])
     ratio = pl.pallas_call(
         ratio_kernel,
         out_shape=jax.ShapeDtypeStruct((H * W, Z), BF16),
@@ -196,20 +204,20 @@
         ],
         compiler_params=PARAMS,
         name="ratio",
-    )(own, mate, beyond, point_spread)
-    mate, beyond = neighbours(ratio)
+    )(own, chip, beyond, point_spread)
+    chip, beyond = neighbours(ratio)
     shares = pl.pallas_call(
         back_kernel,
         out_shape=jax.ShapeDtypeStruct((TILES, 8, H * S), F32),
         in_specs=[VM] * 4,
         out_specs=VM,
         scratch_shapes=[
-            pltpu.VMEM(((H + 2 * R) * 48, 128), F32),
-            pltpu.VMEM(((H + 2 * R) * S, E * Z), BF16),
+            pltpu.VMEM((H * W + W, E * Z), BF16),
+            pltpu.VMEM((H * S, Z), F32),
         ],
         compiler_params=PARAMS,
         name="back",
-    )(ratio, mate, beyond, point_spread)
+    )(ratio, chip, beyond, point_spread)
     parts = lax.all_to_all(shares, "depth", 0, 0, tiled=True)
     return pl.pallas_call(
         final_kernel,
@@ -222,6 +230,7 @@
 
 
 def solution(mesh):
-    in_specs = (P("depth", "tile", None), P("depth", "tile", None), P())
-    out_specs = P("depth", "tile", None)
-    return jax.shard_map(body, mesh=mesh, in_specs=in_specs, out_specs=out_specs, check_vma=False)
+    depth, tile = mesh.devices.shape
+    split = Mesh(mesh.devices.reshape(depth, tile // 2, 2), ("depth", "pair", "core"))
+    spec = P("depth", ("pair", "core"), None)
+    return jax.shard_map(body, mesh=split, in_specs=(spec, spec, P()), out_specs=spec, check_vma=False)

time: 60.8 us -> 58.4 us (0.961)
  blocking collectives: 33.2 us -> 37 us
  starting transfers between devices: 18.1 us -> 15.4 us
  waiting for transfers between devices: 2.39 us -> 0.04 us
  Pallas kernels: 6.6 us -> 5.67 us
    all_gather x0 -> x2, blocking collectives: none -> 3.75 us  [neighbours(): return (lax.all_gather(x, 'core'), beyond)]
    ppermute x4 -> x2, starting transfers between devices: 18.1 us -> 15.4 us  [neighbours(): beyond = lax.ppermute(x, tile, chips)]
    ppermute x4 -> x2, waiting for transfers between devices: 2.39 us -> 0.04 us  [neighbours(): beyond = lax.ppermute(x, tile, chips)]
    pallas_call x1, Pallas kernels: 2.45 us -> 1.5 us  [body(): pl.pallas_call(back_kernel, out_shape=jax.ShapeDtypeStruct((TILES, 8, H *...]
  transfers between devices with their start and end apart: 4 -> 2, of which waited for: 3 -> 0; matrix products, arithmetic and copies ran while one was open for 0% -> 0% of each run, Pallas kernels for 0% -> 0%
where the time goes in v4:
time: 58.4 us; the launch traced here: 58.1 us
  blocking collectives  37 us (63%)
  starting transfers between devices  15.4 us (26%)
  Pallas kernels  5.67 us (10%)
    all_to_all x1, blocking collectives, body(): own = lax.all_to_all(packed, 'depth', 0, 0, tiled=True)  19.3 us
    ppermute x2, starting transfers between devices, neighbours(): beyond = lax.ppermute(x, tile, chips)  15.4 us
    all_to_all x1, blocking collectives, body(): parts = lax.all_to_all(shares, 'depth', 0, 0, tiled=True)  13.9 us
    all_gather x2, blocking collectives, neighbours(): return (lax.all_gather(x, 'core'), beyond)  3.75 us
    pallas_call x1, Pallas kernels, body(): pl.pallas_call(pack_kernel, out_shape=jax.ShapeDtypeStruct((TILES, 8, 512...  2 us
    pallas_call x1, Pallas kernels, body(): pl.pallas_call(back_kernel, out_shape=jax.ShapeDtypeStruct((TILES, 8, H *...  1.5 us
    pallas_call x1, Pallas kernels, body(): pl.pallas_call(ratio_kernel, out_shape=jax.ShapeDtypeStruct((H * W, Z), B...  1.32 us
  transfers between devices with their start and end apart: 2, of which 0 were waited for; matrix products, arithmetic and copies ran while one was open for 0% of the time, Pallas kernels for 0%

profile of v4, /device:TPU:8, one launch (start us, length us, event | category | flops | bytes accessed | tf_op | source)
XLA Modules:
  0.0 58.1 jit_solution(11137270022837108162)
XLA Ops:
  0.0 0.0 copy-start
  0.0 2.0 %pack.1 = bf16[16,8,512]{2,1,0:T(8,128)(2,1)} custom-call(f32[8,8,256]{2,1,0:T(8,128)} %vol_ref.1, f32[8,8,256]{2,1,0:T(8,128)} %meas_hbm.1), custom_call_target="tpu_custom_call" | custom-call | flops 20000000000 | bytes 1048576 | tf_op jit(solution)/shard_map/pack/pallas_call | solution.py:180
  2.0 19.3 %all_to_all.10.own_ref = bf16[16,8,512]{2,1,0:T(8,128)(2,1)S(1)} all-to-all(bf16[16,8,512]{2,1,0:T(8,128)(2,1)} %pack.1), channel_id=1, replica_groups=mesh['depth'=16,'pair'=16,'core'=2] {'depth'}, dimensions={0} | all-to-all | bytes 262144 | tf_op jit(solution)/shard_map/all_to_all | solution.py:194
  21.3 9.6 %collective-permute-start = (bf16[16,8,256]{2,1,0:T(8,128)(2,1)S(1)}, bf16[16,8,256]{2,1,0:T(8,128)(2,1)S(1)}, u32[]{:S(2)}, u32[]{:S(2)}) collective-permute-start(bf16[16,8,256]{2,1,0:T(8,128)(2,1)S(1)} %slice.4), channel_id=1, source_target_pairs={{1,2},{3,4},{5,6},{7,8},{9,10},{11,12},{13,14},{15,16},{17,18},{19... | collective-permute-start | bytes 196616 | tf_op jit(solution)/shard_map/ppermute | solution.py:175
  30.9 1.9 %all-gather = bf16[32,8,256]{2,1,0:T(8,128)(2,1)S(1)} all-gather(bf16[16,8,256]{2,1,0:T(8,128)(2,1)S(1)} %slice.4), channel_id=2, replica_groups=mesh['depth'=16,'pair'=16,'core'=2] {'core'}, dimensions={0}, use_global_device_ids=true | all-gather | bytes 196608 | tf_op jit(solution)/shard_map/all_gather | solution.py:176
  32.8 0.0 collective-permute-done.next_ref
  32.9 0.0 copy-done
  32.9 0.0 copy-start.1
  32.9 1.3 %ratio.1.own_ref = bf16[128,128]{1,0:T(8,128)(2,1)S(1)} custom-call(bf16[16,8,512]{2,1,0:T(8,128)(2,1)S(1)} %all_to_all.10.own_ref, bf16[2,16,8,256]{3,2,1,0:T(8,128)(2,1)S(1)} %bitcast.2, bf16[16,8,256]{2,1,0:T(8,128)(2,1)S(1)} %collective-permute-done.next_ref, bf16[11,11,128,128]{3,2,1,0:T(8,128)(2,1)S(1)} %copy-done), custom_call_target="tpu_custom_call" | custom-call | tf_op jit(solution)/shard_map/ratio/pallas_call | solution.py:196
  34.2 5.8 %collective-permute-start.1 = (bf16[128,128]{1,0:T(8,128)(2,1)S(1)}, bf16[128,128]{1,0:T(8,128)(2,1)S(1)}, u32[]{:S(2)}, u32[]{:S(2)}) collective-permute-start(bf16[128,128]{1,0:T(8,128)(2,1)S(1)} %ratio.1.own_ref), channel_id=1, source_target_pairs={{1,2},{3,4},{5,6},{7,8},{9,10},{11,12},{13,14},{15,16},{17,18},{19... | collective-permute-start | bytes 98312 | tf_op jit(solution)/shard_map/ppermute | solution.py:175
  40.0 1.9 %all-gather.1 = bf16[256,128]{1,0:T(8,128)(2,1)S(1)} all-gather(bf16[128,128]{1,0:T(8,128)(2,1)S(1)} %ratio.1.own_ref), channel_id=3, replica_groups=mesh['depth'=16,'pair'=16,'core'=2] {'core'}, dimensions={0}, use_global_device_ids=true | all-gather | bytes 98304 | tf_op jit(solution)/shard_map/all_gather | solution.py:176
  41.8 0.0 collective-permute-done.1.next_ref
  41.8 1.5 %back.1 = f32[16,8,256]{2,1,0:T(8,128)S(1)} custom-call(bf16[128,128]{1,0:T(8,128)(2,1)S(1)} %ratio.1.own_ref, bf16[2,128,128]{2,1,0:T(8,128)(2,1)S(1)} %bitcast.3, bf16[128,128]{1,0:T(8,128)(2,1)S(1)} %collective-permute-done.1.next_ref, bf16[11,11,128,128]{3,2,1,0:T(8,128)(2,1)S(1)} %copy-done), custom_call_target="tpu_custom_call" | custom-call | tf_op jit(solution)/shard_map/back/pallas_call | solution.py:209
  43.3 13.9 %all_to_all.11.parts_ref = f32[16,8,256]{2,1,0:T(8,128)S(1)} all-to-all(f32[16,8,256]{2,1,0:T(8,128)S(1)} %back.1), channel_id=1, replica_groups=mesh['depth'=16,'pair'=16,'core'=2] {'depth'}, dimensions={0} | all-to-all | bytes 262144 | tf_op jit(solution)/shard_map/all_to_all | solution.py:221
  57.3 0.0 copy-done.1
  57.3 0.8 %final.1 = f32[8,8,256]{2,1,0:T(8,128)} custom-call(f32[16,8,256]{2,1,0:T(8,128)S(1)} %all_to_all.11.parts_ref, f32[8,8,256]{2,1,0:T(8,128)S(1)} %copy-done.1), custom_call_target="tpu_custom_call" | custom-call | tf_op jit(solution)/shard_map/final/pallas_call | solution.py:222
  (1 shorter events, 0.0 us)
Async XLA Ops:
  0.0 32.9 %copy-start = (bf16[11,11,128,128]{3,2,1,0:T(8,128)(2,1)S(1)}, bf16[11,11,128,128]{3,2,1,0:T(8,128)(2,1)}, u32[]{:S(2)}) copy-start(bf16[11,11,128,128]{3,2,1,0:T(8,128)(2,1)} %psf_ref.3) | copy-start | bytes 11894788
  21.3 11.6 %collective-permute-start = (bf16[16,8,256]{2,1,0:T(8,128)(2,1)S(1)}, bf16[16,8,256]{2,1,0:T(8,128)(2,1)S(1)}, u32[]{:S(2)}, u32[]{:S(2)}) collective-permute-start(bf16[16,8,256]{2,1,0:T(8,128)(2,1)S(1)} %slice.4), channel_id=1, source_target_pairs={{1,2},{3,4},{5,6},{7,8},{9,10},{11,12},{13,14},{15,16},{17,18},{19... | collective-permute-start | bytes 196616 | tf_op jit(solution)/shard_map/ppermute | solution.py:175
  32.9 24.4 %copy-start.1 = (f32[8,8,256]{2,1,0:T(8,128)S(1)}, f32[8,8,256]{2,1,0:T(8,128)}, u32[]{:S(2)}) copy-start(f32[8,8,256]{2,1,0:T(8,128)} %vol_ref.1) | copy-start | bytes 196612
  34.2 7.6 %collective-permute-start.1 = (bf16[128,128]{1,0:T(8,128)(2,1)S(1)}, bf16[128,128]{1,0:T(8,128)(2,1)S(1)}, u32[]{:S(2)}, u32[]{:S(2)}) collective-permute-start(bf16[128,128]{1,0:T(8,128)(2,1)S(1)} %ratio.1.own_ref), channel_id=1, source_target_pairs={{1,2},{3,4},{5,6},{7,8},{9,10},{11,12},{13,14},{15,16},{17,18},{19... | collective-permute-start | bytes 98312 | tf_op jit(solution)/shard_map/ppermute | solution.py:175

commit v5 on v4

--- a/solution.py
+++ b/solution.py
@@ -13,6 +13,7 @@
 W = 16
 H = 8
 S = 32
+CHUNKS = ((0, 13),)
 F32 = jnp.float32
 BF16 = jnp.bfloat16
 VM = pl.BlockSpec(memory_space=pltpu.VMEM)
@@ -73,51 +74,54 @@
         out_ref[t, :, 384:512] = (value - head.astype(F32)).astype(BF16)
 
 
-def ratio_kernel(own_ref, chip_ref, next_ref, psf_ref, out_ref, rows_ref, taps_ref):
-    def group(ref, g):
-        return ref[:, :, g * 128 : g * 128 + 128].astype(F32).reshape(Z, 128)
-
+def join_kernel(own_ref, chip_ref, out_ref):
+    even = lax.axis_index("core") == 0
+    out_ref[:, :, :512] = own_ref[...]
+    upper, lower = chip_ref[1, :, :, :128], chip_ref[0, :, :, 128:]
+    out_ref[:, :, 512:] = jnp.where(even, upper.astype(F32), lower.astype(F32)).astype(BF16)
+
+
+def ratio_kernel(own_ref, chip_ref, next_ref, psf_ref, out_ref, rows_ref, taps_ref, meas_ref):
     core = lax.axis_index("core")
     even = core == 0
-    mate_ref = chip_ref.at[1 - core]
-
-    def above(g):
-        return jnp.where(even, group(next_ref, g), group(mate_ref, g))
-
-    def below(g):
-        return jnp.where(even, group(mate_ref, g), group(next_ref, g))
-
-    lane = lanes((Z, 128))
-    mixed = jnp.where(lane < S, below(1), above(0))
-    blocks = [mixed, above(1), group(own_ref, 0), group(own_ref, 1), below(0)]
-    for i, block in enumerate(blocks):
-        rows_ref[i * 128 : i * 128 + 128, :] = block.T
-    for y in range(H + 2 * R):
-        at = S * ((3 + y) % 20)
+
+    def group(value, g):
+        return value[:, :, g * 128 : g * 128 + 128].astype(F32).reshape(Z, 128)
+
+    upper, lower = chip_ref[0], chip_ref[1]
+    chip = [group(upper, 0), group(upper, 1), group(lower, 0), group(lower, 1)]
+    beyond = [group(next_ref, 0), group(next_ref, 1), group(next_ref, 4)]
+    when_even = [beyond[2], beyond[0], beyond[1], *chip]
+    when_odd = [*chip, *beyond]
+    shift = S * (1 - core)
+    for i, (a, b) in enumerate(zip(when_even, when_odd)):
+        rows_ref[pl.ds(pl.multiple_of(i * 128 + shift, S), 128), :] = jnp.where(even, a, b).T
+    rows = H + R
+    for y in range(rows + 2 * R):
+        at = S * (y + 3)
         for b in range(E):
             taps_ref[y * W : y * W + W, b * 128 : b * 128 + 128] = rows_ref[at + b : at + b + W, :].astype(BF16)
-    total = jnp.zeros((H * W, Z), F32)
-    for a in range(E):
-        total = total + jnp.dot(
-            taps_ref[a * W : a * W + H * W, :], psf_ref[a].reshape(E * Z, Z), preferred_element_type=F32
-        )
-    measured = (group(own_ref, 2) + group(own_ref, 3)).T
-    out_ref[...] = (measured / total).astype(BF16)
-
-
-def back_kernel(own_ref, chip_ref, next_ref, psf_ref, out_ref, rows_ref, sum_ref):
-    core = lax.axis_index("core")
-    even = core == 0
-    mate_ref = chip_ref.at[1 - core]
+    here = (group(own_ref, 2) + group(own_ref, 3)).T
+    there = (group(next_ref, 2) + group(next_ref, 3)).T
+    skip = (H - R) * W
+    meas_ref[pl.ds(pl.multiple_of(jnp.where(even, H * W, skip), 16), H * W), :] = here
+    meas_ref[pl.ds(pl.multiple_of(jnp.where(even, 0, skip + H * W), 16), H * W), :] = there
+    for first, count in CHUNKS:
+        total = jnp.zeros((count * W, Z), F32)
+        for a in range(E):
+            total = total + jnp.dot(
+                taps_ref[(first + a) * W : (first + a + count) * W, :],
+                psf_ref[a].reshape(E * Z, Z),
+                preferred_element_type=F32,
+            )
+        part = slice(first * W, (first + count) * W)
+        out_ref[part, :] = (meas_ref[skip + first * W : skip + (first + count) * W, :] / total).astype(BF16)
+
+
+def back_kernel(chip_ref, psf_ref, out_ref, rows_ref, sum_ref):
+    first_row = lax.axis_index("core") * (H * W)
     for y in range(H + 2 * R):
-        if y < R:
-            here = slice((y + H - R) * W, (y + H - R) * W + W)
-            value = jnp.where(even, next_ref[here, :].astype(F32), mate_ref[here, :].astype(F32)).astype(BF16)
-        elif y < R + H:
-            value = own_ref[(y - R) * W : (y - R) * W + W, :]
-        else:
-            here = slice((y - R - H) * W, (y - R - H) * W + W)
-            value = jnp.where(even, mate_ref[here, :].astype(F32), next_ref[here, :].astype(F32)).astype(BF16)
+        value = chip_ref[pl.ds(pl.multiple_of(first_row + y * W, W), W), :]
         for a in range(E):
             row = y + a - 2 * R
             if 0 <= row < H:
@@ -168,14 +172,6 @@
             out_ref[:, y, here] = vol_ref[:, y, here] * (sums[0] + sums[1]) / weight
 
 
-def neighbours(x):
-    tile = ("pair", "core")
-    count = lax.axis_size(tile)
-    chips = [(i, i + 1) for i in range(1, count - 1, 2)] + [(i, i - 1) for i in range(2, count, 2)]
-    beyond = lax.ppermute(x, tile, chips)
-    return lax.all_gather(x, "core"), beyond
-
-
 def body(volume, measured, point_spread):
     packed = pl.pallas_call(
         pack_kernel,
@@ -192,24 +188,37 @@
         name="pack",
     )(volume, measured)
     own = lax.all_to_all(packed, "depth", 0, 0, tiled=True)
-    chip, beyond = neighbours(own[:, :, :256])
+    chip = lax.all_gather(own[:, :, :256], "core")
+    joined = pl.pallas_call(
+        join_kernel,
+        out_shape=jax.ShapeDtypeStruct((TILES, 8, 640), BF16),
+        in_specs=[VM] * 2,
+        out_specs=VM,
+        compiler_params=PARAMS,
+        name="join",
+    )(own, chip)
+    tile = ("pair", "core")
+    count = lax.axis_size(tile)
+    pairs = [(i, i + 1) for i in range(1, count - 1, 2)] + [(i, i - 1) for i in range(2, count, 2)]
+    beyond = lax.ppermute(joined, tile, pairs)
     ratio = pl.pallas_call(
         ratio_kernel,
-        out_shape=jax.ShapeDtypeStruct((H * W, Z), BF16),
+        out_shape=jax.ShapeDtypeStruct(((H + R) * W, Z), BF16),
         in_specs=[VM] * 4,
         out_specs=VM,
         scratch_shapes=[
-            pltpu.VMEM((5 * 128, 128), F32),
-            pltpu.VMEM(((H + 2 * R) * W, E * Z), BF16),
+            pltpu.VMEM((7 * 128 + S, 128), F32),
+            pltpu.VMEM(((H + 3 * R) * W, E * Z), BF16),
+            pltpu.VMEM((2 * H * W + (H - R) * W, Z), F32),
         ],
         compiler_params=PARAMS,
         name="ratio",
     )(own, chip, beyond, point_spread)
-    chip, beyond = neighbours(ratio)
+    chip_ratio = lax.all_gather(ratio, "core", tiled=True)
     shares = pl.pallas_call(
         back_kernel,
         out_shape=jax.ShapeDtypeStruct((TILES, 8, H * S), F32),
-        in_specs=[VM] * 4,
+        in_specs=[VM] * 2,
         out_specs=VM,
         scratch_shapes=[
             pltpu.VMEM((H * W + W, E * Z), BF16),
@@ -217,7 +226,7 @@
         ],
         compiler_params=PARAMS,
         name="back",
-    )(ratio, chip, beyond, point_spread)
+    )(chip_ratio, point_spread)
     parts = lax.all_to_all(shares, "depth", 0, 0, tiled=True)
     return pl.pallas_call(
         final_kernel,

time: 58.4 us -> 58.1 us (level)
  starting transfers between devices: 15.4 us -> 11.5 us
  waiting for transfers between devices: 0.04 us -> 2.99 us
  Pallas kernels: 5.67 us -> 6.55 us
    ppermute x2 -> x1, starting transfers between devices: 15.4 us -> 11.5 us  [body(): beyond = lax.ppermute(joined, tile, pairs)]
    ppermute x2 -> x1, waiting for transfers between devices: 0.04 us -> 2.99 us  [body(): beyond = lax.ppermute(joined, tile, pairs)]
    pallas_call x1 -> x2, Pallas kernels: 1.32 us -> 2.21 us  [the longest x1 2.19 us: body(): pl.pallas_call(ratio_kernel, out_shape=jax.ShapeDtypeStruct(((H + R) * W,...]
  transfers between devices with their start and end apart: 2 -> 1, of which waited for: 0 -> 1; matrix products, arithmetic and copies ran while one was open for 0% -> 0% of each run, Pallas kernels for 0% -> 0%
where the time goes in v5:
time: 58.1 us; the launch traced here: 57.8 us
  blocking collectives  36.7 us (63%)
  starting transfers between devices  11.5 us (20%)
  Pallas kernels  6.55 us (11%)
  waiting for transfers between devices  2.99 us (5%)
    all_to_all x1, blocking collectives, body(): own = lax.all_to_all(packed, 'depth', 0, 0, tiled=True)  19.3 us
    all_to_all x1, blocking collectives, body(): parts = lax.all_to_all(shares, 'depth', 0, 0, tiled=True)  13.7 us
    ppermute x1, starting transfers between devices, body(): beyond = lax.ppermute(joined, tile, pairs)  11.5 us
    ppermute x1, waiting for transfers between devices, body(): beyond = lax.ppermute(joined, tile, pairs)  2.99 us
    pallas_call x1, Pallas kernels, body(): pl.pallas_call(ratio_kernel, out_shape=jax.ShapeDtypeStruct(((H + R) * W,...  2.19 us
    pallas_call x1, Pallas kernels, body(): pl.pallas_call(pack_kernel, out_shape=jax.ShapeDtypeStruct((TILES, 8, 512...  2 us
    all_gather x1, blocking collectives, body(): chip = lax.all_gather(own[:, :, :256], 'core')  1.89 us
    all_gather x1, blocking collectives, body(): chip_ratio = lax.all_gather(ratio, 'core', tiled=True)  1.88 us
  transfers between devices with their start and end apart: 1, of which 1 were waited for; matrix products, arithmetic and copies ran while one was open for 0% of the time, Pallas kernels for 0%

profile of v5, /device:TPU:8, one launch (start us, length us, event | category | flops | bytes accessed | tf_op | source)
XLA Modules:
  0.0 57.8 jit_solution(5184260605305699387)
XLA Ops:
  0.0 0.0 copy-start
  0.0 2.0 %pack.1 = bf16[16,8,512]{2,1,0:T(8,128)(2,1)} custom-call(f32[8,8,256]{2,1,0:T(8,128)} %vol_ref.1, f32[8,8,256]{2,1,0:T(8,128)} %meas_hbm.1), custom_call_target="tpu_custom_call" | custom-call | flops 20000000000 | bytes 1048576 | tf_op jit(solution)/shard_map/pack/pallas_call | solution.py:176
  2.0 19.3 %all_to_all.10.own_ref = bf16[16,8,512]{2,1,0:T(8,128)(2,1)S(1)} all-to-all(bf16[16,8,512]{2,1,0:T(8,128)(2,1)} %pack.1), channel_id=1, replica_groups=mesh['depth'=16,'pair'=16,'core'=2] {'depth'}, dimensions={0} | all-to-all | bytes 262144 | tf_op jit(solution)/shard_map/all_to_all | solution.py:190
  21.3 1.9 %all-gather = bf16[32,8,256]{2,1,0:T(8,128)(2,1)S(1)} all-gather(bf16[16,8,256]{2,1,0:T(8,128)(2,1)S(1)} %slice.4), channel_id=2, replica_groups=mesh['depth'=16,'pair'=16,'core'=2] {'core'}, dimensions={0}, use_global_device_ids=true | all-gather | bytes 196608 | tf_op jit(solution)/shard_map/all_gather | solution.py:191
  23.2 0.0 copy-start.1
  23.2 11.5 %collective-permute-start = (bf16[16,8,640]{2,1,0:T(8,128)(2,1)S(1)}, bf16[16,8,640]{2,1,0:T(8,128)(2,1)S(1)}, u32[]{:S(2)}, u32[]{:S(2)}) collective-permute-start(bf16[16,8,640]{2,1,0:T(8,128)(2,1)S(1)} %join.1), channel_id=1, source_target_pairs={{1,2},{3,4},{5,6},{7,8},{9,10},{11,12},{13,14},{15,16},{17,18},{19... | collective-permute-start | bytes 491528 | tf_op jit(solution)/shard_map/ppermute | solution.py:203
  34.7 3.0 %collective-permute-done.next_ref = bf16[16,8,640]{2,1,0:T(8,128)(2,1)S(1)} collective-permute-done((bf16[16,8,640]{2,1,0:T(8,128)(2,1)S(1)}, bf16[16,8,640]{2,1,0:T(8,128)(2,1)S(1)}, u32[]{:S(2)}, u32[]{:S(2)}) %collective-permute-start) | collective-permute-done | bytes 163872 | tf_op jit(solution)/shard_map/ppermute | solution.py:203
  37.7 0.0 copy-done
  37.7 2.2 %ratio.1 = bf16[208,128]{1,0:T(8,128)(2,1)S(1)} custom-call(bf16[16,8,512]{2,1,0:T(8,128)(2,1)S(1)} %all_to_all.10.own_ref, bf16[2,16,8,256]{3,2,1,0:T(8,128)(2,1)S(1)} %bitcast.2, bf16[16,8,640]{2,1,0:T(8,128)(2,1)S(1)} %collective-permute-done.next_ref, bf16[11,11,128,128]{3,2,1,0:T(8,128)(2,1)S(1)} %copy-done), custom_call_target="tpu_custom_call" | custom-call | tf_op jit(solution)/shard_map/ratio/pallas_call | solution.py:204
  39.9 1.9 %all_gather.11.chip_ref = bf16[416,128]{1,0:T(8,128)(2,1)S(1)} all-gather(bf16[208,128]{1,0:T(8,128)(2,1)S(1)} %ratio.1), channel_id=1, replica_groups=mesh['depth'=16,'pair'=16,'core'=2] {'core'}, dimensions={0}, use_global_device_ids=true | all-gather | bytes 159744 | tf_op jit(solution)/shard_map/all_gather | solution.py:217
  41.8 1.5 %back.1 = f32[16,8,256]{2,1,0:T(8,128)S(1)} custom-call(bf16[416,128]{1,0:T(8,128)(2,1)S(1)} %all_gather.11.chip_ref, bf16[11,11,128,128]{3,2,1,0:T(8,128)(2,1)S(1)} %copy-done), custom_call_target="tpu_custom_call" | custom-call | tf_op jit(solution)/shard_map/back/pallas_call | solution.py:218
  43.3 13.7 %all_to_all.11.parts_ref = f32[16,8,256]{2,1,0:T(8,128)S(1)} all-to-all(f32[16,8,256]{2,1,0:T(8,128)S(1)} %back.1), channel_id=1, replica_groups=mesh['depth'=16,'pair'=16,'core'=2] {'depth'}, dimensions={0} | all-to-all | bytes 262144 | tf_op jit(solution)/shard_map/all_to_all | solution.py:230
  57.0 0.0 copy-done.1
  57.0 0.8 %final.1 = f32[8,8,256]{2,1,0:T(8,128)} custom-call(f32[16,8,256]{2,1,0:T(8,128)S(1)} %all_to_all.11.parts_ref, f32[8,8,256]{2,1,0:T(8,128)S(1)} %copy-done.1), custom_call_target="tpu_custom_call" | custom-call | tf_op jit(solution)/shard_map/final/pallas_call | solution.py:231
  (2 shorter events, 0.0 us)
Async XLA Ops:
  0.0 37.7 %copy-start = (bf16[11,11,128,128]{3,2,1,0:T(8,128)(2,1)S(1)}, bf16[11,11,128,128]{3,2,1,0:T(8,128)(2,1)}, u32[]{:S(2)}) copy-start(bf16[11,11,128,128]{3,2,1,0:T(8,128)(2,1)} %psf_ref.3) | copy-start | bytes 11894788
  23.2 33.7 %copy-start.1 = (f32[8,8,256]{2,1,0:T(8,128)S(1)}, f32[8,8,256]{2,1,0:T(8,128)}, u32[]{:S(2)}) copy-start(f32[8,8,256]{2,1,0:T(8,128)} %vol_ref.1) | copy-start | bytes 196612
  23.2 14.5 %collective-permute-start = (bf16[16,8,640]{2,1,0:T(8,128)(2,1)S(1)}, bf16[16,8,640]{2,1,0:T(8,128)(2,1)S(1)}, u32[]{:S(2)}, u32[]{:S(2)}) collective-permute-start(bf16[16,8,640]{2,1,0:T(8,128)(2,1)S(1)} %join.1), channel_id=1, source_target_pairs={{1,2},{3,4},{5,6},{7,8},{9,10},{11,12},{13,14},{15,16},{17,18},{19... | collective-permute-start | bytes 491528 | tf_op jit(solution)/shard_map/ppermute | solution.py:203

commit v6 on v5

--- a/solution.py
+++ b/solution.py
@@ -13,11 +13,9 @@
 W = 16
 H = 8
 S = 32
-CHUNKS = ((0, 13),)
 F32 = jnp.float32
 BF16 = jnp.bfloat16
 VM = pl.BlockSpec(memory_space=pltpu.VMEM)
-HBM = pl.BlockSpec(memory_space=pl.ANY)
 PARAMS = pltpu.CompilerParams(vmem_limit_bytes=40 * 1024 * 1024)
 
 
@@ -25,14 +23,8 @@
     return lax.broadcasted_iota(jnp.int32, shape, 1)
 
 
-def pack_kernel(vol_hbm, meas_hbm, out_ref, vol_ref, meas_ref, sems):
-    copies = [
-        pltpu.make_async_copy(vol_hbm, vol_ref, sems.at[0]),
-        pltpu.make_async_copy(meas_hbm, meas_ref, sems.at[1]),
-    ]
-    for copy in copies:
-        copy.start()
-    copies[0].wait()
+def pack_kernel(both_ref, out_ref):
+    vol_ref, meas_ref = both_ref.at[0], both_ref.at[1]
     lane = lanes()
     slot = lane // S
     inside = lane % S
@@ -64,7 +56,6 @@
             for s in range(1, 4):
                 value = jnp.where(slot < s, value, window(t, 4 * g + s))
             out_ref[t, :, g * 128 : g * 128 + 128] = value.astype(BF16)
-    copies[1].wait()
     for t in range(TILES):
         value = turned(meas_ref, 1, 0, t // 8, -W * t)
         for y in range(1, H):
@@ -74,48 +65,78 @@
         out_ref[t, :, 384:512] = (value - head.astype(F32)).astype(BF16)
 
 
+def group(value, g):
+    return value[:, :, g * 128 : g * 128 + 128].astype(F32).reshape(Z, 128)
+
+
 def join_kernel(own_ref, chip_ref, out_ref):
-    even = lax.axis_index("core") == 0
-    out_ref[:, :, :512] = own_ref[...]
-    upper, lower = chip_ref[1, :, :, :128], chip_ref[0, :, :, 128:]
-    out_ref[:, :, 512:] = jnp.where(even, upper.astype(F32), lower.astype(F32)).astype(BF16)
-
-
-def ratio_kernel(own_ref, chip_ref, next_ref, psf_ref, out_ref, rows_ref, taps_ref, meas_ref):
     core = lax.axis_index("core")
     even = core == 0
-
-    def group(value, g):
-        return value[:, :, g * 128 : g * 128 + 128].astype(F32).reshape(Z, 128)
-
-    upper, lower = chip_ref[0], chip_ref[1]
-    chip = [group(upper, 0), group(upper, 1), group(lower, 0), group(lower, 1)]
-    beyond = [group(next_ref, 0), group(next_ref, 1), group(next_ref, 4)]
-    when_even = [beyond[2], beyond[0], beyond[1], *chip]
-    when_odd = [*chip, *beyond]
-    shift = S * (1 - core)
-    for i, (a, b) in enumerate(zip(when_even, when_odd)):
-        rows_ref[pl.ds(pl.multiple_of(i * 128 + shift, S), 128), :] = jnp.where(even, a, b).T
-    rows = H + R
-    for y in range(rows + 2 * R):
-        at = S * (y + 3)
+    lane = lanes((Z, 128))
+    keep = (lane >= 48 * core) & (lane < 80 + 48 * core)
+    mate = jnp.where(even, group(chip_ref[1], 0), group(chip_ref[0], 1))
+    half = pltpu.roll(mate, 64, 1)
+    one = jnp.where(even, pltpu.roll(mate, 96, 1), half)
+    two = jnp.where(even, half, pltpu.roll(mate, 32, 1))
+    out_ref[:, :, :256] = own_ref[:, :, :256]
+    out_ref[:, :, 256:384] = jnp.where(keep, group(own_ref, 2), one).astype(BF16).reshape(TILES, 8, 128)
+    out_ref[:, :, 384:] = jnp.where(keep, group(own_ref, 3), two).astype(BF16).reshape(TILES, 8, 128)
+
+
+def spread_rows(rows_ref, taps_ref, count):
+    for y in range(count):
         for b in range(E):
-            taps_ref[y * W : y * W + W, b * 128 : b * 128 + 128] = rows_ref[at + b : at + b + W, :].astype(BF16)
-    here = (group(own_ref, 2) + group(own_ref, 3)).T
-    there = (group(next_ref, 2) + group(next_ref, 3)).T
-    skip = (H - R) * W
-    meas_ref[pl.ds(pl.multiple_of(jnp.where(even, H * W, skip), 16), H * W), :] = here
-    meas_ref[pl.ds(pl.multiple_of(jnp.where(even, 0, skip + H * W), 16), H * W), :] = there
-    for first, count in CHUNKS:
-        total = jnp.zeros((count * W, Z), F32)
-        for a in range(E):
-            total = total + jnp.dot(
-                taps_ref[(first + a) * W : (first + a + count) * W, :],
-                psf_ref[a].reshape(E * Z, Z),
-                preferred_element_type=F32,
-            )
-        part = slice(first * W, (first + count) * W)
-        out_ref[part, :] = (meas_ref[skip + first * W : skip + (first + count) * W, :] / total).astype(BF16)
+            start = y * S + b
+            taps_ref[y * W : y * W + W, b * 128 : b * 128 + 128] = rows_ref[start : start + W, :].astype(BF16)
+
+
+def add_products(taps_ref, psf_ref, sum_ref, offset, count, taps_row, sum_row):
+    part = jnp.dot(
+        taps_ref[pl.ds(pl.multiple_of(taps_row * W, W), count * W), :],
+        psf_ref[offset].reshape(E * Z, Z),
+        preferred_element_type=F32,
+    )
+    here = pl.ds(pl.multiple_of(sum_row * W, W), count * W)
+    sum_ref[here, :] = sum_ref[here, :] + part
+
+
+def inner_kernel(own_ref, chip_ref, psf_ref, sum_ref, meas_ref, rows_ref, taps_ref):
+    core = lax.axis_index("core")
+    for i in range(4):
+        rows_ref[i * 128 : i * 128 + 128, :] = group(chip_ref[i // 2], i % 2).T
+    meas_ref[...] = (group(own_ref, 2) + group(own_ref, 3)).T
+    spread_rows(rows_ref, taps_ref, 2 * H)
+    sum_ref[...] = jnp.zeros(sum_ref.shape, F32)
+    for k in range(-R, R + 1):
+        count = H + k
+        add_products(
+            taps_ref, psf_ref, sum_ref, R + k * (1 - 2 * core), count, (2 * H - count) * core, (H + R - count) * (1 - core)
+        )
+
+
+def ratio_kernel(inner_ref, meas_ref, next_ref, psf_ref, out_ref, rows_ref, taps_ref, sum_ref):
+    core = lax.axis_index("core")
+    even = core == 0
+    first, second = group(next_ref, 2).T, group(next_ref, 3).T
+    shift = 2 * S * (1 - core)
+    for g in range(2):
+        rows_ref[pl.ds(pl.multiple_of(g * 128 + shift, S), 128), :] = group(next_ref, g).T
+    for i, block in enumerate((first, second)):
+        at = pl.multiple_of(i * S + 8 * S * core, S)
+        rows_ref[pl.ds(at, S), :] = jnp.where(even, block[:S], block[128 - S :])
+    spread_rows(rows_ref, taps_ref, 2 * R)
+    sum_ref[...] = inner_ref[...]
+    for k in range(-R, R):
+        count = R - k
+        add_products(
+            taps_ref, psf_ref, sum_ref, R + k * (1 - 2 * core), count, (2 * R - count) * (1 - core), (H + R - count) * core
+        )
+    here = pl.ds(pl.multiple_of(R * W * (1 - core), W), H * W)
+    out_ref[here, :] = (meas_ref[...] / sum_ref[here, :]).astype(BF16)
+    there = pl.ds(pl.multiple_of(H * W * core, W), R * W)
+    beyond = first + second
+    beyond = jnp.where(even, beyond[(H - R) * W :], beyond[: R * W])
+    out_ref[there, :] = (beyond / sum_ref[there, :]).astype(BF16)
 
 
 def back_kernel(chip_ref, psf_ref, out_ref, rows_ref, sum_ref):
@@ -176,22 +197,17 @@
     packed = pl.pallas_call(
         pack_kernel,
         out_shape=jax.ShapeDtypeStruct((TILES, 8, 512), BF16),
-        in_specs=[HBM] * 2,
-        out_specs=VM,
-        scratch_shapes=[
-            pltpu.VMEM(volume.shape, F32),
-            pltpu.VMEM(measured.shape, F32),
-            pltpu.SemaphoreType.DMA((2,)),
-        ],
-        compiler_params=pltpu.CompilerParams(vmem_limit_bytes=56 * 1024 * 1024),
+        in_specs=[VM],
+        out_specs=VM,
+        compiler_params=PARAMS,
         cost_estimate=pl.CostEstimate(flops=20_000_000_000, bytes_accessed=2**20, transcendentals=0),
         name="pack",
-    )(volume, measured)
+    )(jnp.stack([volume, measured]))
     own = lax.all_to_all(packed, "depth", 0, 0, tiled=True)
     chip = lax.all_gather(own[:, :, :256], "core")
     joined = pl.pallas_call(
         join_kernel,
-        out_shape=jax.ShapeDtypeStruct((TILES, 8, 640), BF16),
+        out_shape=jax.ShapeDtypeStruct((TILES, 8, 512), BF16),
         in_specs=[VM] * 2,
         out_specs=VM,
         compiler_params=PARAMS,
@@ -201,19 +217,33 @@
     count = lax.axis_size(tile)
     pairs = [(i, i + 1) for i in range(1, count - 1, 2)] + [(i, i - 1) for i in range(2, count, 2)]
     beyond = lax.ppermute(joined, tile, pairs)
+    rows = H + R
+    inner, near = pl.pallas_call(
+        inner_kernel,
+        out_shape=[jax.ShapeDtypeStruct((rows * W, Z), F32), jax.ShapeDtypeStruct((H * W, Z), F32)],
+        in_specs=[VM] * 3,
+        out_specs=[VM] * 2,
+        scratch_shapes=[
+            pltpu.VMEM((2 * H * S, Z), F32),
+            pltpu.VMEM((2 * H * W, E * Z), BF16),
+        ],
+        compiler_params=PARAMS,
+        cost_estimate=pl.CostEstimate(flops=2 * 88 * W * E * Z * Z, bytes_accessed=2**22, transcendentals=0),
+        name="inner",
+    )(own, chip, point_spread)
     ratio = pl.pallas_call(
         ratio_kernel,
-        out_shape=jax.ShapeDtypeStruct(((H + R) * W, Z), BF16),
+        out_shape=jax.ShapeDtypeStruct((rows * W, Z), BF16),
         in_specs=[VM] * 4,
         out_specs=VM,
         scratch_shapes=[
-            pltpu.VMEM((7 * 128 + S, 128), F32),
-            pltpu.VMEM(((H + 3 * R) * W, E * Z), BF16),
-            pltpu.VMEM((2 * H * W + (H - R) * W, Z), F32),
+            pltpu.VMEM((2 * R * S, Z), F32),
+            pltpu.VMEM((2 * R * W, E * Z), BF16),
+            pltpu.VMEM((rows * W, Z), F32),
         ],
         compiler_params=PARAMS,
         name="ratio",
-    )(own, chip, beyond, point_spread)
+    )(inner, near, beyond, point_spread)
     chip_ratio = lax.all_gather(ratio, "core", tiled=True)
     shares = pl.pallas_call(
         back_kernel,

time: 58.1 us -> 55.8 us (0.960)
  waiting for transfers between devices: 2.99 us -> 1.08 us
  Pallas kernels: 6.55 us -> 5.38 us
  other arithmetic: 0 us -> 0.88 us
    ppermute x1, waiting for transfers between devices: 2.99 us -> 1.08 us  [body(): beyond = lax.ppermute(joined, tile, pairs)]
    pallas_call x1, Pallas kernels: 2 us -> 0.26 us  [body(): pl.pallas_call(pack_kernel, out_shape=jax.ShapeDtypeStruct((TILES, 8, 512...]
    another operation x0 -> x1, other arithmetic: none -> 0.88 us  [body(): jnp.stack([volume, measured])]
    pallas_call x2 -> x3, Pallas kernels: 2.21 us -> 2.75 us  [the longest x1 1.54 us: body(): pl.pallas_call(inner_kernel, out_shape=[jax.ShapeDtypeStruct((rows * W, Z...]
  transfers between devices with their start and end apart: 1 -> 1, of which waited for: 1 -> 1; matrix products, arithmetic and copies ran while one was open for 0% -> 0% of each run, Pallas kernels for 0% -> 3%
where the time goes in v6:
time: 55.8 us; the launch traced here: 55.6 us
  blocking collectives  36.8 us (66%)
  starting transfers between devices  11.4 us (20%)
  Pallas kernels  5.38 us (10%)
  waiting for transfers between devices  1.08 us (2%)
  other arithmetic  0.88 us (2%)
    all_to_all x1, blocking collectives, body(): own = lax.all_to_all(packed, 'depth', 0, 0, tiled=True)  19.4 us
    all_to_all x1, blocking collectives, body(): parts = lax.all_to_all(shares, 'depth', 0, 0, tiled=True)  13.7 us
    ppermute x1, starting transfers between devices, body(): beyond = lax.ppermute(joined, tile, pairs)  11.4 us
    all_gather x1, blocking collectives, body(): chip = lax.all_gather(own[:, :, :256], 'core')  1.89 us
    all_gather x1, blocking collectives, body(): chip_ratio = lax.all_gather(ratio, 'core', tiled=True)  1.88 us
    pallas_call x1, Pallas kernels, body(): pl.pallas_call(inner_kernel, out_shape=[jax.ShapeDtypeStruct((rows * W, Z...  1.54 us
    pallas_call x1, Pallas kernels, body(): pl.pallas_call(back_kernel, out_shape=jax.ShapeDtypeStruct((TILES, 8, H *...  1.52 us
  transfers between devices with their start and end apart: 1, of which 1 were waited for; matrix products, arithmetic and copies ran while one was open for 0% of the time, Pallas kernels for 3%

profile of v6, /device:TPU:8, one launch (start us, length us, event | category | flops | bytes accessed | tf_op | source)
XLA Modules:
  0.0 55.6 jit_solution(6089889140838820042)
XLA Ops:
  0.0 0.9 %pad_maximum_fusion.both_ref = f32[2,8,8,256]{3,2,1,0:T(8,128)S(1)} fusion(f32[1,8,8,256]{3,2,1,0:T(8,128)} %bitcast.6, f32[1,8,8,256]{3,2,1,0:T(8,128)} %bitcast.5), kind=kLoop, calls=%fused_computation | loop fusion | flops 32768 | bytes 262144 | tf_op jit(solution)/shard_map/stack | solution.py:205
  0.9 0.0 copy-start
  0.9 0.3 pack.1
  1.2 19.4 %all_to_all.10.own_ref = bf16[16,8,512]{2,1,0:T(8,128)(2,1)S(1)} all-to-all(bf16[16,8,512]{2,1,0:T(8,128)(2,1)S(1)} %pack.1), channel_id=1, replica_groups=mesh['depth'=16,'pair'=16,'core'=2] {'depth'}, dimensions={0} | all-to-all | bytes 262144 | tf_op jit(solution)/shard_map/all_to_all | solution.py:206
  20.5 1.9 %all-gather = bf16[32,8,256]{2,1,0:T(8,128)(2,1)S(1)} all-gather(bf16[16,8,256]{2,1,0:T(8,128)(2,1)S(1)} %slice.4), channel_id=2, replica_groups=mesh['depth'=16,'pair'=16,'core'=2] {'core'}, dimensions={0}, use_global_device_ids=true | all-gather | bytes 196608 | tf_op jit(solution)/shard_map/all_gather | solution.py:207
  22.4 0.1 join.1
  22.5 11.4 %collective-permute-start = (bf16[16,8,512]{2,1,0:T(8,128)(2,1)S(1)}, bf16[16,8,512]{2,1,0:T(8,128)(2,1)S(1)}, u32[]{:S(2)}, u32[]{:S(2)}) collective-permute-start(bf16[16,8,512]{2,1,0:T(8,128)(2,1)S(1)} %join.1), channel_id=1, source_target_pairs={{1,2},{3,4},{5,6},{7,8},{9,10},{11,12},{13,14},{15,16},{17,18},{19... | collective-permute-start | bytes 393224 | tf_op jit(solution)/shard_map/ppermute | solution.py:219
  33.9 0.0 copy-done
  33.9 1.5 %inner.1 = (f32[208,128]{1,0:T(8,128)S(1)}, f32[128,128]{1,0:T(8,128)S(1)}) custom-call(bf16[16,8,512]{2,1,0:T(8,128)(2,1)S(1)} %all_to_all.10.own_ref, bf16[2,16,8,256]{3,2,1,0:T(8,128)(2,1)S(1)} %bitcast.4, bf16[11,11,128,128]{3,2,1,0:T(8,128)(2,1)S(1)} %copy-done), custom_call_target="tpu_custom_call" | custom-call | flops 507510784 | bytes 4194304 | tf_op jit(solution)/shard_map/inner/pallas_call | solution.py:221
  35.5 1.1 %collective-permute-done.next_ref = bf16[16,8,512]{2,1,0:T(8,128)(2,1)S(1)} collective-permute-done((bf16[16,8,512]{2,1,0:T(8,128)(2,1)S(1)}, bf16[16,8,512]{2,1,0:T(8,128)(2,1)S(1)}, u32[]{:S(2)}, u32[]{:S(2)}) %collective-permute-start) | collective-permute-done | bytes 131104 | tf_op jit(solution)/shard_map/ppermute | solution.py:219
  36.5 0.0 copy-start.1
  36.5 1.1 %ratio.1 = bf16[208,128]{1,0:T(8,128)(2,1)S(1)} custom-call(f32[208,128]{1,0:T(8,128)S(1)} %get-tuple-element.7.inner_ref, f32[128,128]{1,0:T(8,128)S(1)} %get-tuple-element.8.meas_ref, bf16[16,8,512]{2,1,0:T(8,128)(2,1)S(1)} %collective-permute-done.next_ref, bf16[11,11,128,128]{3,2,1,0:T(8,128)(2,1)S(1)} %copy-done), custom_call_target="tpu_custom_call" | custom-call | tf_op jit(solution)/shard_map/ratio/pallas_call | solution.py:234
  37.7 1.9 %all_gather.11.chip_ref = bf16[416,128]{1,0:T(8,128)(2,1)S(1)} all-gather(bf16[208,128]{1,0:T(8,128)(2,1)S(1)} %ratio.1), channel_id=1, replica_groups=mesh['depth'=16,'pair'=16,'core'=2] {'core'}, dimensions={0}, use_global_device_ids=true | all-gather | bytes 159744 | tf_op jit(solution)/shard_map/all_gather | solution.py:247
  39.5 1.5 %back.1 = f32[16,8,256]{2,1,0:T(8,128)S(1)} custom-call(bf16[416,128]{1,0:T(8,128)(2,1)S(1)} %all_gather.11.chip_ref, bf16[11,11,128,128]{3,2,1,0:T(8,128)(2,1)S(1)} %copy-done), custom_call_target="tpu_custom_call" | custom-call | tf_op jit(solution)/shard_map/back/pallas_call | solution.py:248
  41.1 13.7 %all_to_all.11.parts_ref = f32[16,8,256]{2,1,0:T(8,128)S(1)} all-to-all(f32[16,8,256]{2,1,0:T(8,128)S(1)} %back.1), channel_id=1, replica_groups=mesh['depth'=16,'pair'=16,'core'=2] {'depth'}, dimensions={0} | all-to-all | bytes 262144 | tf_op jit(solution)/shard_map/all_to_all | solution.py:260
  54.7 0.0 copy-done.1
  54.7 0.8 %final.1 = f32[8,8,256]{2,1,0:T(8,128)} custom-call(f32[16,8,256]{2,1,0:T(8,128)S(1)} %all_to_all.11.parts_ref, f32[8,8,256]{2,1,0:T(8,128)S(1)} %copy-done.1), custom_call_target="tpu_custom_call" | custom-call | tf_op jit(solution)/shard_map/final/pallas_call | solution.py:261
  (1 shorter events, 0.0 us)
Async XLA Ops:
  0.9 33.0 %copy-start = (bf16[11,11,128,128]{3,2,1,0:T(8,128)(2,1)S(1)}, bf16[11,11,128,128]{3,2,1,0:T(8,128)(2,1)}, u32[]{:S(2)}) copy-start(bf16[11,11,128,128]{3,2,1,0:T(8,128)(2,1)} %psf_ref.5) | copy-start | bytes 11894788
  22.5 14.0 %collective-permute-start = (bf16[16,8,512]{2,1,0:T(8,128)(2,1)S(1)}, bf16[16,8,512]{2,1,0:T(8,128)(2,1)S(1)}, u32[]{:S(2)}, u32[]{:S(2)}) collective-permute-start(bf16[16,8,512]{2,1,0:T(8,128)(2,1)S(1)} %join.1), channel_id=1, source_target_pairs={{1,2},{3,4},{5,6},{7,8},{9,10},{11,12},{13,14},{15,16},{17,18},{19... | collective-permute-start | bytes 393224 | tf_op jit(solution)/shard_map/ppermute | solution.py:219
  36.5 18.2 %copy-start.1 = (f32[8,8,256]{2,1,0:T(8,128)S(1)}, f32[8,8,256]{2,1,0:T(8,128)}, u32[]{:S(2)}) copy-start(f32[8,8,256]{2,1,0:T(8,128)} %vol_ref.1) | copy-start | bytes 196612

commit v7 on v6

--- a/solution.py
+++ b/solution.py
@@ -23,8 +23,7 @@
     return lax.broadcasted_iota(jnp.int32, shape, 1)
 
 
-def pack_kernel(both_ref, out_ref):
-    vol_ref, meas_ref = both_ref.at[0], both_ref.at[1]
+def pack_kernel(vol_ref, meas_ref, out_ref):
     lane = lanes()
     slot = lane // S
     inside = lane % S
@@ -33,7 +32,7 @@
     def turned(ref, key, y, half, shift):
         name = (key, y, half, shift % 128)
         if name not in rolled:
-            part = ref[:, y, half * 128 : half * 128 + 128]
+            part = ref[*key, :, y, half * 128 : half * 128 + 128]
             rolled[name] = pltpu.roll(part, shift % 128, 1) if shift % 128 else part
         return rolled[name]
 
@@ -41,9 +40,10 @@
         start = W * t - R
         shift = S * (y % 4) - start
         low, high = max(start, 0) // 128, min(start + W + 2 * R - 1, 255) // 128
-        value = turned(vol_ref, 0, y, low, shift)
+        tile, y = (y // H,), y % H
+        value = turned(vol_ref, tile, y, low, shift)
         if high != low:
-            value = jnp.where(inside < 128 - start, value, turned(vol_ref, 0, y, high, shift))
+            value = jnp.where(inside < 128 - start, value, turned(vol_ref, tile, y, high, shift))
         if start < 0:
             value = jnp.where(inside < -start, 0.0, value)
         if start + W + 2 * R > 256:
@@ -51,36 +51,38 @@
         return value
 
     for t in range(TILES):
-        for g in range(2):
+        for g in range(4):
             value = window(t, 4 * g)
             for s in range(1, 4):
                 value = jnp.where(slot < s, value, window(t, 4 * g + s))
             out_ref[t, :, g * 128 : g * 128 + 128] = value.astype(BF16)
     for t in range(TILES):
-        value = turned(meas_ref, 1, 0, t // 8, -W * t)
+        value = turned(meas_ref, (), 0, t // 8, -W * t)
         for y in range(1, H):
-            value = jnp.where(lane < W * y, value, turned(meas_ref, 1, y, t // 8, W * y - W * t))
+            value = jnp.where(lane < W * y, value, turned(meas_ref, (), y, t // 8, W * y - W * t))
         head = value.astype(BF16)
-        out_ref[t, :, 256:384] = head
-        out_ref[t, :, 384:512] = (value - head.astype(F32)).astype(BF16)
+        out_ref[t, :, 512:640] = head
+        out_ref[t, :, 640:768] = (value - head.astype(F32)).astype(BF16)
 
 
 def group(value, g):
     return value[:, :, g * 128 : g * 128 + 128].astype(F32).reshape(Z, 128)
 
 
-def join_kernel(own_ref, chip_ref, out_ref):
+def join_kernel(own_ref, out_ref):
     core = lax.axis_index("core")
     even = core == 0
     lane = lanes((Z, 128))
     keep = (lane >= 48 * core) & (lane < 80 + 48 * core)
-    mate = jnp.where(even, group(chip_ref[1], 0), group(chip_ref[0], 1))
+    upper, lower = [[group(own_ref, 2 * i + g) for g in range(2)] for i in range(2)]
+    mate = jnp.where(even, lower[0], upper[1])
     half = pltpu.roll(mate, 64, 1)
     one = jnp.where(even, pltpu.roll(mate, 96, 1), half)
     two = jnp.where(even, half, pltpu.roll(mate, 32, 1))
-    out_ref[:, :, :256] = own_ref[:, :, :256]
-    out_ref[:, :, 256:384] = jnp.where(keep, group(own_ref, 2), one).astype(BF16).reshape(TILES, 8, 128)
-    out_ref[:, :, 384:] = jnp.where(keep, group(own_ref, 3), two).astype(BF16).reshape(TILES, 8, 128)
+    parts = [jnp.where(even, upper[g], lower[g]) for g in range(2)]
+    parts += [jnp.where(keep, group(own_ref, 4), one), jnp.where(keep, group(own_ref, 5), two)]
+    for g, part in enumerate(parts):
+        out_ref[:, :, g * 128 : g * 128 + 128] = part.astype(BF16).reshape(TILES, 8, 128)
 
 
 def spread_rows(rows_ref, taps_ref, count):
@@ -100,11 +102,11 @@
     sum_ref[here, :] = sum_ref[here, :] + part
 
 
-def inner_kernel(own_ref, chip_ref, psf_ref, sum_ref, meas_ref, rows_ref, taps_ref):
+def inner_kernel(own_ref, psf_ref, sum_ref, meas_ref, rows_ref, taps_ref):
     core = lax.axis_index("core")
     for i in range(4):
-        rows_ref[i * 128 : i * 128 + 128, :] = group(chip_ref[i // 2], i % 2).T
-    meas_ref[...] = (group(own_ref, 2) + group(own_ref, 3)).T
+        rows_ref[i * 128 : i * 128 + 128, :] = group(own_ref, i).T
+    meas_ref[...] = (group(own_ref, 4) + group(own_ref, 5)).T
     spread_rows(rows_ref, taps_ref, 2 * H)
     sum_ref[...] = jnp.zeros(sum_ref.shape, F32)
     for k in range(-R, R + 1):
@@ -196,23 +198,22 @@
 def body(volume, measured, point_spread):
     packed = pl.pallas_call(
         pack_kernel,
-        out_shape=jax.ShapeDtypeStruct((TILES, 8, 512), BF16),
-        in_specs=[VM],
+        out_shape=jax.ShapeDtypeStruct((TILES, 8, 768), BF16),
+        in_specs=[VM] * 2,
         out_specs=VM,
         compiler_params=PARAMS,
         cost_estimate=pl.CostEstimate(flops=20_000_000_000, bytes_accessed=2**20, transcendentals=0),
         name="pack",
-    )(jnp.stack([volume, measured]))
+    )(lax.all_gather(volume, "core"), measured)
     own = lax.all_to_all(packed, "depth", 0, 0, tiled=True)
-    chip = lax.all_gather(own[:, :, :256], "core")
     joined = pl.pallas_call(
         join_kernel,
         out_shape=jax.ShapeDtypeStruct((TILES, 8, 512), BF16),
-        in_specs=[VM] * 2,
+        in_specs=[VM],
         out_specs=VM,
         compiler_params=PARAMS,
         name="join",
-    )(own, chip)
+    )(own)
     tile = ("pair", "core")
     count = lax.axis_size(tile)
     pairs = [(i, i + 1) for i in range(1, count - 1, 2)] + [(i, i - 1) for i in range(2, count, 2)]
@@ -221,7 +222,7 @@
     inner, near = pl.pallas_call(
         inner_kernel,
         out_shape=[jax.ShapeDtypeStruct((rows * W, Z), F32), jax.ShapeDtypeStruct((H * W, Z), F32)],
-        in_specs=[VM] * 3,
+        in_specs=[VM] * 2,
         out_specs=[VM] * 2,
         scratch_shapes=[
             pltpu.VMEM((2 * H * S, Z), F32),
@@ -230,7 +231,7 @@
         compiler_params=PARAMS,
         cost_estimate=pl.CostEstimate(flops=2 * 88 * W * E * Z * Z, bytes_accessed=2**22, transcendentals=0),
         name="inner",
-    )(own, chip, point_spread)
+    )(own, point_spread)
     ratio = pl.pallas_call(
         ratio_kernel,
         out_shape=jax.ShapeDtypeStruct((rows * W, Z), BF16),

time: 55.8 us -> 57.2 us (1.025)
  blocking collectives: 36.8 us -> 40 us
  starting transfers between devices: 11.4 us -> 9.56 us
  other arithmetic: 0.88 us -> 0 us
  local copies, waits for them, and re-layouts: 0.02 us -> 0.85 us
    all_to_all x1, blocking collectives: 13.7 us -> 15.8 us  [body(): parts = lax.all_to_all(shares, 'depth', 0, 0, tiled=True)]
    ppermute x1, starting transfers between devices: 11.4 us -> 9.56 us  [body(): beyond = lax.ppermute(joined, tile, pairs)]
    another operation x1 -> x0, other arithmetic: 0.88 us -> none  [body(): jnp.stack([volume, measured])]
    all_to_all x1, blocking collectives: 19.4 us -> 20.2 us  [body(): own = lax.all_to_all(packed, 'depth', 0, 0, tiled=True)]
    unnamed x4 -> x6, local copies, waits for them, and re-layouts: 0.01 us -> 0.85 us
where the time goes in v7:
time: 57.2 us; the launch traced here: 57 us
  blocking collectives  40 us (70%)
  starting transfers between devices  9.56 us (17%)
  Pallas kernels  5.51 us (10%)
  waiting for transfers between devices  1.09 us (2%)
  local copies, waits for them, and re-layouts  0.85 us (1%)
    all_to_all x1, blocking collectives, body(): own = lax.all_to_all(packed, 'depth', 0, 0, tiled=True)  20.2 us
    all_to_all x1, blocking collectives, body(): parts = lax.all_to_all(shares, 'depth', 0, 0, tiled=True)  15.8 us
    ppermute x1, starting transfers between devices, body(): beyond = lax.ppermute(joined, tile, pairs)  9.56 us
    all_gather x1, blocking collectives, body(): lax.all_gather(volume, 'core')  2.1 us
    all_gather x1, blocking collectives, body(): chip_ratio = lax.all_gather(ratio, 'core', tiled=True)  1.88 us
    pallas_call x1, Pallas kernels, body(): pl.pallas_call(inner_kernel, out_shape=[jax.ShapeDtypeStruct((rows * W, Z...  1.53 us
    pallas_call x1, Pallas kernels, body(): pl.pallas_call(back_kernel, out_shape=jax.ShapeDtypeStruct((TILES, 8, H *...  1.52 us
  transfers between devices with their start and end apart: 1, of which 1 were waited for; matrix products, arithmetic and copies ran while one was open for 0% of the time, Pallas kernels for 3%

profile of v7, /device:TPU:8, one launch (start us, length us, event | category | flops | bytes accessed | tf_op | source)
XLA Modules:
  0.0 57.0 jit_solution(18054773575024396730)
XLA Ops:
  0.0 2.1 %all-gather = f32[16,8,256]{2,1,0:T(8,128)S(1)} all-gather(f32[8,8,256]{2,1,0:T(8,128)} %vol_ref.1), channel_id=2, replica_groups=mesh['depth'=16,'pair'=16,'core'=2] {'core'}, dimensions={0}, use_global_device_ids=true | all-gather | bytes 196608 | tf_op jit(solution)/shard_map/all_gather | solution.py:207
  2.1 0.0 copy-start.2
  2.1 0.8 %copy-done.2 = f32[8,8,256]{2,1,0:T(8,128)S(1)} copy-done((f32[8,8,256]{2,1,0:T(8,128)S(1)}, f32[8,8,256]{2,1,0:T(8,128)}, u32[]{:S(2)}) %copy-start.2) | copy-done | bytes 65560
  2.9 0.0 copy-start
  2.9 0.4 pack.1
  3.3 20.2 %all_to_all.10.own_ref = bf16[16,8,768]{2,1,0:T(8,128)(2,1)S(1)} all-to-all(bf16[16,8,768]{2,1,0:T(8,128)(2,1)S(1)} %pack.1), channel_id=1, replica_groups=mesh['depth'=16,'pair'=16,'core'=2] {'depth'}, dimensions={0} | all-to-all | bytes 393216 | tf_op jit(solution)/shard_map/all_to_all | solution.py:208
  23.5 0.1 join.1
  23.7 9.6 %collective-permute-start = (bf16[16,8,512]{2,1,0:T(8,128)(2,1)S(1)}, bf16[16,8,512]{2,1,0:T(8,128)(2,1)S(1)}, u32[]{:S(2)}, u32[]{:S(2)}) collective-permute-start(bf16[16,8,512]{2,1,0:T(8,128)(2,1)S(1)} %join.1), channel_id=1, source_target_pairs={{1,2},{3,4},{5,6},{7,8},{9,10},{11,12},{13,14},{15,16},{17,18},{19... | collective-permute-start | bytes 393224 | tf_op jit(solution)/shard_map/ppermute | solution.py:220
  33.2 0.0 copy-done
  33.2 1.5 %inner.1 = (f32[208,128]{1,0:T(8,128)S(1)}, f32[128,128]{1,0:T(8,128)S(1)}) custom-call(bf16[16,8,768]{2,1,0:T(8,128)(2,1)S(1)} %all_to_all.10.own_ref, bf16[11,11,128,128]{3,2,1,0:T(8,128)(2,1)S(1)} %copy-done), custom_call_target="tpu_custom_call" | custom-call | flops 507510784 | bytes 4194304 | tf_op jit(solution)/shard_map/inner/pallas_call | solution.py:222
  34.8 1.1 %collective-permute-done.next_ref = bf16[16,8,512]{2,1,0:T(8,128)(2,1)S(1)} collective-permute-done((bf16[16,8,512]{2,1,0:T(8,128)(2,1)S(1)}, bf16[16,8,512]{2,1,0:T(8,128)(2,1)S(1)}, u32[]{:S(2)}, u32[]{:S(2)}) %collective-permute-start) | collective-permute-done | bytes 131104 | tf_op jit(solution)/shard_map/ppermute | solution.py:220
  35.9 0.0 copy-start.1
  35.9 1.1 %ratio.1 = bf16[208,128]{1,0:T(8,128)(2,1)S(1)} custom-call(f32[208,128]{1,0:T(8,128)S(1)} %get-tuple-element.7.inner_ref, f32[128,128]{1,0:T(8,128)S(1)} %get-tuple-element.8.meas_ref, bf16[16,8,512]{2,1,0:T(8,128)(2,1)S(1)} %collective-permute-done.next_ref, bf16[11,11,128,128]{3,2,1,0:T(8,128)(2,1)S(1)} %copy-done), custom_call_target="tpu_custom_call" | custom-call | tf_op jit(solution)/shard_map/ratio/pallas_call | solution.py:235
  37.0 1.9 %all_gather.11.chip_ref = bf16[416,128]{1,0:T(8,128)(2,1)S(1)} all-gather(bf16[208,128]{1,0:T(8,128)(2,1)S(1)} %ratio.1), channel_id=1, replica_groups=mesh['depth'=16,'pair'=16,'core'=2] {'core'}, dimensions={0}, use_global_device_ids=true | all-gather | bytes 159744 | tf_op jit(solution)/shard_map/all_gather | solution.py:248
  38.9 1.5 %back.1 = f32[16,8,256]{2,1,0:T(8,128)S(1)} custom-call(bf16[416,128]{1,0:T(8,128)(2,1)S(1)} %all_gather.11.chip_ref, bf16[11,11,128,128]{3,2,1,0:T(8,128)(2,1)S(1)} %copy-done), custom_call_target="tpu_custom_call" | custom-call | tf_op jit(solution)/shard_map/back/pallas_call | solution.py:249
  40.4 15.8 %all_to_all.11.parts_ref = f32[16,8,256]{2,1,0:T(8,128)S(1)} all-to-all(f32[16,8,256]{2,1,0:T(8,128)S(1)} %back.1), channel_id=1, replica_groups=mesh['depth'=16,'pair'=16,'core'=2] {'depth'}, dimensions={0} | all-to-all | bytes 262144 | tf_op jit(solution)/shard_map/all_to_all | solution.py:261
  56.2 0.0 copy-done.1
  56.2 0.8 %final.1 = f32[8,8,256]{2,1,0:T(8,128)} custom-call(f32[16,8,256]{2,1,0:T(8,128)S(1)} %all_to_all.11.parts_ref, f32[8,8,256]{2,1,0:T(8,128)S(1)} %copy-done.1), custom_call_target="tpu_custom_call" | custom-call | tf_op jit(solution)/shard_map/final/pallas_call | solution.py:262
Async XLA Ops:
  2.1 0.8 %copy-start.2 = (f32[8,8,256]{2,1,0:T(8,128)S(1)}, f32[8,8,256]{2,1,0:T(8,128)}, u32[]{:S(2)}) copy-start(f32[8,8,256]{2,1,0:T(8,128)} %meas_ref.1) | copy-start | bytes 196612
  2.9 30.3 %copy-start = (bf16[11,11,128,128]{3,2,1,0:T(8,128)(2,1)S(1)}, bf16[11,11,128,128]{3,2,1,0:T(8,128)(2,1)}, u32[]{:S(2)}) copy-start(bf16[11,11,128,128]{3,2,1,0:T(8,128)(2,1)} %psf_ref.5) | copy-start | bytes 11894788
  23.7 12.2 %collective-permute-start = (bf16[16,8,512]{2,1,0:T(8,128)(2,1)S(1)}, bf16[16,8,512]{2,1,0:T(8,128)(2,1)S(1)}, u32[]{:S(2)}, u32[]{:S(2)}) collective-permute-start(bf16[16,8,512]{2,1,0:T(8,128)(2,1)S(1)} %join.1), channel_id=1, source_target_pairs={{1,2},{3,4},{5,6},{7,8},{9,10},{11,12},{13,14},{15,16},{17,18},{19... | collective-permute-start | bytes 393224 | tf_op jit(solution)/shard_map/ppermute | solution.py:220
  35.9 20.3 %copy-start.1 = (f32[8,8,256]{2,1,0:T(8,128)S(1)}, f32[8,8,256]{2,1,0:T(8,128)}, u32[]{:S(2)}) copy-start(f32[8,8,256]{2,1,0:T(8,128)} %vol_ref.1) | copy-start | bytes 196612

commit v8 on v6

--- a/solution.py
+++ b/solution.py
@@ -13,6 +13,7 @@
 W = 16
 H = 8
 S = 32
+SCALE = 8.0
 F32 = jnp.float32
 BF16 = jnp.bfloat16
 VM = pl.BlockSpec(memory_space=pltpu.VMEM)
@@ -90,14 +91,19 @@
             taps_ref[y * W : y * W + W, b * 128 : b * 128 + 128] = rows_ref[start : start + W, :].astype(BF16)
 
 
-def add_products(taps_ref, psf_ref, sum_ref, offset, count, taps_row, sum_row):
-    part = jnp.dot(
-        taps_ref[pl.ds(pl.multiple_of(taps_row * W, W), count * W), :],
-        psf_ref[offset].reshape(E * Z, Z),
-        preferred_element_type=F32,
+def add_products(taps_ref, psf_ref, sum_ref, offsets, count, taps_row, sum_rows, first):
+    kernel = jnp.concatenate([psf_ref[offset].reshape(E * Z, Z) for offset in offsets], axis=1)
+    product = jnp.dot(
+        taps_ref[pl.ds(pl.multiple_of(taps_row * W, W), count * W), :], kernel, preferred_element_type=F32
     )
-    here = pl.ds(pl.multiple_of(sum_row * W, W), count * W)
-    sum_ref[here, :] = sum_ref[here, :] + part
+    for i, sum_row in enumerate(sum_rows):
+        part = product[:, i * Z : i * Z + Z]
+        if i and count == 1:
+            break
+        if i:
+            part = jnp.where(first, part[W:], part[:-W])
+        here = pl.ds(pl.multiple_of(sum_row * W, W), (count - i) * W)
+        sum_ref[here, :] = sum_ref[here, :] + part
 
 
 def inner_kernel(own_ref, chip_ref, psf_ref, sum_ref, meas_ref, rows_ref, taps_ref):
@@ -107,10 +113,17 @@
     meas_ref[...] = (group(own_ref, 2) + group(own_ref, 3)).T
     spread_rows(rows_ref, taps_ref, 2 * H)
     sum_ref[...] = jnp.zeros(sum_ref.shape, F32)
-    for k in range(-R, R + 1):
-        count = H + k
+    for k in range(R, -R - 1, -2):
+        steps = range(k, max(k - 2, -R - 1), -1)
         add_products(
-            taps_ref, psf_ref, sum_ref, R + k * (1 - 2 * core), count, (2 * H - count) * core, (H + R - count) * (1 - core)
+            taps_ref,
+            psf_ref,
+            sum_ref,
+            [R + i * (1 - 2 * core) for i in steps],
+            H + k,
+            (H - k) * core,
+            [(R - i) * (1 - core) for i in steps],
+            core == 1,
         )
 
 
@@ -126,10 +139,17 @@
         rows_ref[pl.ds(at, S), :] = jnp.where(even, block[:S], block[128 - S :])
     spread_rows(rows_ref, taps_ref, 2 * R)
     sum_ref[...] = inner_ref[...]
-    for k in range(-R, R):
-        count = R - k
+    for k in range(-R, R, 2):
+        steps = (k, k + 1)
         add_products(
-            taps_ref, psf_ref, sum_ref, R + k * (1 - 2 * core), count, (2 * R - count) * (1 - core), (H + R - count) * core
+            taps_ref,
+            psf_ref,
+            sum_ref,
+            [R + i * (1 - 2 * core) for i in steps],
+            R - k,
+            (R + k) * (1 - core),
+            [(H + i) * core for i in steps],
+            even,
         )
     here = pl.ds(pl.multiple_of(R * W * (1 - core), W), H * W)
     out_ref[here, :] = (meas_ref[...] / sum_ref[here, :]).astype(BF16)
@@ -162,15 +182,14 @@
                 here = slice(y * S + b, y * S + b + W)
                 sum_ref[here, :] = sum_ref[here, :] + part[y * W : y * W + W]
             weight = weight + part[H * W : H * W + 1]
-    sum_ref[S - 1 : S, :] = weight
+    factor = SCALE / weight
     for g in range(2):
-        out_ref[:, :, g * 128 : g * 128 + 128] = sum_ref[g * 128 : g * 128 + 128, :].T.reshape(TILES, 8, 128)
+        share = (sum_ref[g * 128 : g * 128 + 128, :] * factor).T
+        out_ref[:, :, g * 128 : g * 128 + 128] = share.reshape(TILES, 8, 128)
 
 
 def final_kernel(parts_ref, vol_ref, out_ref):
     lane = lanes()
-    weight = parts_ref[0, :, S - 1 : S]
-
     for y in range(H):
         g, s = y // 4, y % 4
         turned = []
@@ -190,7 +209,7 @@
                     (lane >= start) & (lane < stop), turned[t], 0.0 if before is None else before
                 )
             here = slice(half * 128, half * 128 + 128)
-            out_ref[:, y, here] = vol_ref[:, y, here] * (sums[0] + sums[1]) / weight
+            out_ref[:, y, here] = vol_ref[:, y, here] * ((sums[0] + sums[1]) * (1 / SCALE))
 
 
 def body(volume, measured, point_spread):
@@ -257,7 +276,7 @@
         compiler_params=PARAMS,
         name="back",
     )(chip_ratio, point_spread)
-    parts = lax.all_to_all(shares, "depth", 0, 0, tiled=True)
+    parts = lax.all_to_all(shares.astype(jnp.float16), "depth", 0, 0, tiled=True).astype(F32)
     return pl.pallas_call(
         final_kernel,
         out_shape=jax.ShapeDtypeStruct(volume.shape, F32),

time: 55.8 us -> 55.4 us (level)
  transfers between devices with their start and end apart: 1 -> 1, of which waited for: 1 -> 1; matrix products, arithmetic and copies ran while one was open for 0% -> 0% of each run, Pallas kernels for 3% -> 2%
where the time goes in v8:
time: 55.4 us; the launch traced here: 55.2 us
  blocking collectives  36.5 us (66%)
  starting transfers between devices  11.4 us (21%)
  Pallas kernels  4.85 us (9%)
  waiting for transfers between devices  1.49 us (3%)
  other arithmetic  0.9 us (2%)
    all_to_all x1, blocking collectives, body(): own = lax.all_to_all(packed, 'depth', 0, 0, tiled=True)  19.4 us
    all_to_all x1, blocking collectives, body(): lax.all_to_all(shares.astype(jnp.float16), 'depth', 0, 0, tiled=True)  13.4 us
    ppermute x1, starting transfers between devices, body(): beyond = lax.ppermute(joined, tile, pairs)  11.4 us
    all_gather x1, blocking collectives, body(): chip = lax.all_gather(own[:, :, :256], 'core')  1.89 us
    all_gather x1, blocking collectives, body(): chip_ratio = lax.all_gather(ratio, 'core', tiled=True)  1.88 us
    pallas_call x1, Pallas kernels, body(): pl.pallas_call(back_kernel, out_shape=jax.ShapeDtypeStruct((TILES, 8, H *...  1.53 us
    ppermute x1, waiting for transfers between devices, body(): beyond = lax.ppermute(joined, tile, pairs)  1.49 us
    pallas_call x1, Pallas kernels, body(): pl.pallas_call(inner_kernel, out_shape=[jax.ShapeDtypeStruct((rows * W, Z...  1.13 us
  transfers between devices with their start and end apart: 1, of which 1 were waited for; matrix products, arithmetic and copies ran while one was open for 0% of the time, Pallas kernels for 2%

profile of v8, /device:TPU:8, one launch (start us, length us, event | category | flops | bytes accessed | tf_op | source)
XLA Modules:
  0.0 55.2 jit_solution(4233437819126260989)
XLA Ops:
  0.0 0.9 %pad_maximum_fusion.both_ref = f32[2,8,8,256]{3,2,1,0:T(8,128)S(1)} fusion(f32[1,8,8,256]{3,2,1,0:T(8,128)} %bitcast.6, f32[1,8,8,256]{3,2,1,0:T(8,128)} %bitcast.5), kind=kLoop, calls=%fused_computation | loop fusion | flops 32768 | bytes 262144 | tf_op jit(solution)/shard_map/stack | solution.py:224
  0.9 0.0 copy-start
  0.9 0.3 pack.1
  1.2 19.4 %all_to_all.10.own_ref = bf16[16,8,512]{2,1,0:T(8,128)(2,1)S(1)} all-to-all(bf16[16,8,512]{2,1,0:T(8,128)(2,1)S(1)} %pack.1), channel_id=1, replica_groups=mesh['depth'=16,'pair'=16,'core'=2] {'depth'}, dimensions={0} | all-to-all | bytes 262144 | tf_op jit(solution)/shard_map/all_to_all | solution.py:225
  20.5 1.9 %all-gather = bf16[32,8,256]{2,1,0:T(8,128)(2,1)S(1)} all-gather(bf16[16,8,256]{2,1,0:T(8,128)(2,1)S(1)} %slice.4), channel_id=2, replica_groups=mesh['depth'=16,'pair'=16,'core'=2] {'core'}, dimensions={0}, use_global_device_ids=true | all-gather | bytes 196608 | tf_op jit(solution)/shard_map/all_gather | solution.py:226
  22.4 0.1 join.1
  22.5 11.4 %collective-permute-start = (bf16[16,8,512]{2,1,0:T(8,128)(2,1)S(1)}, bf16[16,8,512]{2,1,0:T(8,128)(2,1)S(1)}, u32[]{:S(2)}, u32[]{:S(2)}) collective-permute-start(bf16[16,8,512]{2,1,0:T(8,128)(2,1)S(1)} %join.1), channel_id=1, source_target_pairs={{1,2},{3,4},{5,6},{7,8},{9,10},{11,12},{13,14},{15,16},{17,18},{19... | collective-permute-start | bytes 393224 | tf_op jit(solution)/shard_map/ppermute | solution.py:238
  33.9 0.0 copy-done
  33.9 1.1 %inner.1 = (f32[208,128]{1,0:T(8,128)S(1)}, f32[128,128]{1,0:T(8,128)S(1)}) custom-call(bf16[16,8,512]{2,1,0:T(8,128)(2,1)S(1)} %all_to_all.10.own_ref, bf16[2,16,8,256]{3,2,1,0:T(8,128)(2,1)S(1)} %bitcast.4, bf16[11,11,128,128]{3,2,1,0:T(8,128)(2,1)S(1)} %copy-done), custom_call_target="tpu_custom_call" | custom-call | flops 507510784 | bytes 4194304 | tf_op jit(solution)/shard_map/inner/pallas_call | solution.py:240
  35.0 1.5 %collective-permute-done.next_ref = bf16[16,8,512]{2,1,0:T(8,128)(2,1)S(1)} collective-permute-done((bf16[16,8,512]{2,1,0:T(8,128)(2,1)S(1)}, bf16[16,8,512]{2,1,0:T(8,128)(2,1)S(1)}, u32[]{:S(2)}, u32[]{:S(2)}) %collective-permute-start) | collective-permute-done | bytes 131104 | tf_op jit(solution)/shard_map/ppermute | solution.py:238
  36.5 0.0 copy-start.1
  36.5 1.0 %ratio.1 = bf16[208,128]{1,0:T(8,128)(2,1)S(1)} custom-call(f32[208,128]{1,0:T(8,128)S(1)} %get-tuple-element.7.inner_ref, f32[128,128]{1,0:T(8,128)S(1)} %get-tuple-element.8.meas_ref, bf16[16,8,512]{2,1,0:T(8,128)(2,1)S(1)} %collective-permute-done.next_ref, bf16[11,11,128,128]{3,2,1,0:T(8,128)(2,1)S(1)} %copy-done), custom_call_target="tpu_custom_call" | custom-call | tf_op jit(solution)/shard_map/ratio/pallas_call | solution.py:253
  37.5 1.9 %all_gather.11.chip_ref = bf16[416,128]{1,0:T(8,128)(2,1)S(1)} all-gather(bf16[208,128]{1,0:T(8,128)(2,1)S(1)} %ratio.1), channel_id=1, replica_groups=mesh['depth'=16,'pair'=16,'core'=2] {'core'}, dimensions={0}, use_global_device_ids=true | all-gather | bytes 159744 | tf_op jit(solution)/shard_map/all_gather | solution.py:266
  39.4 1.5 %back.1 = f32[16,8,256]{2,1,0:T(8,128)S(1)} custom-call(bf16[416,128]{1,0:T(8,128)(2,1)S(1)} %all_gather.11.chip_ref, bf16[11,11,128,128]{3,2,1,0:T(8,128)(2,1)S(1)} %copy-done), custom_call_target="tpu_custom_call" | custom-call | tf_op jit(solution)/shard_map/back/pallas_call | solution.py:267
  41.0 13.4 %all_to_all.11 = f16[16,8,256]{2,1,0:T(8,128)(2,1)S(1)} all-to-all(f16[16,8,256]{2,1,0:T(8,128)(2,1)S(1)} %convert_element_type.6), channel_id=1, replica_groups=mesh['depth'=16,'pair'=16,'core'=2] {'depth'}, dimensions={0} | all-to-all | bytes 131072 | tf_op jit(solution)/shard_map/all_to_all | solution.py:279
  54.4 0.0 copy-done.1
  54.4 0.8 %final.1 = f32[8,8,256]{2,1,0:T(8,128)} custom-call(f32[16,8,256]{2,1,0:T(8,128)S(1)} %convert_element_type.7.parts_ref, f32[8,8,256]{2,1,0:T(8,128)S(1)} %copy-done.1), custom_call_target="tpu_custom_call" | custom-call | tf_op jit(solution)/shard_map/final/pallas_call | solution.py:280
  (3 shorter events, 0.0 us)
Async XLA Ops:
  0.9 33.0 %copy-start = (bf16[11,11,128,128]{3,2,1,0:T(8,128)(2,1)S(1)}, bf16[11,11,128,128]{3,2,1,0:T(8,128)(2,1)}, u32[]{:S(2)}) copy-start(bf16[11,11,128,128]{3,2,1,0:T(8,128)(2,1)} %psf_ref.5) | copy-start | bytes 11894788
  22.5 14.0 %collective-permute-start = (bf16[16,8,512]{2,1,0:T(8,128)(2,1)S(1)}, bf16[16,8,512]{2,1,0:T(8,128)(2,1)S(1)}, u32[]{:S(2)}, u32[]{:S(2)}) collective-permute-start(bf16[16,8,512]{2,1,0:T(8,128)(2,1)S(1)} %join.1), channel_id=1, source_target_pairs={{1,2},{3,4},{5,6},{7,8},{9,10},{11,12},{13,14},{15,16},{17,18},{19... | collective-permute-start | bytes 393224 | tf_op jit(solution)/shard_map/ppermute | solution.py:238
  36.5 17.8 %copy-start.1 = (f32[8,8,256]{2,1,0:T(8,128)S(1)}, f32[8,8,256]{2,1,0:T(8,128)}, u32[]{:S(2)}) copy-start(f32[8,8,256]{2,1,0:T(8,128)} %vol_ref.1) | copy-start | bytes 196612

commit v9 on v8

v9 whole, which is shorter than its diff:
```python
import jax
import jax.numpy as jnp
from jax import lax
from jax.experimental import pallas as pl
from jax.experimental.pallas import tpu as pltpu
from jax.sharding import Mesh
from jax.sharding import PartitionSpec as P

R = 5
E = 11
Z = 128
TILES = 16
W = 16
H = 8
C = 26
S = 32
SCALE = 8.0
F32 = jnp.float32
BF16 = jnp.bfloat16
F16 = jnp.float16
VM = pl.BlockSpec(memory_space=pltpu.VMEM)
PARAMS = pltpu.CompilerParams(vmem_limit_bytes=40 * 1024 * 1024)


def lanes(shape=(8, 128)):
    return lax.broadcasted_iota(jnp.int32, shape, 1)


def pack_kernel(vol_ref, meas_ref, out_ref):
    even = lax.axis_index("core") == 0
    lane = lanes()
    rows = {}
    rolled = {}

    def row(i, half):
        if (i, half) not in rows:
            here = slice(half * 128, half * 128 + 128)
            a, b = [vol_ref[r // H, :, r % H, here] for r in (i, i + H - R)]
            rows[i, half] = jnp.where(even, a, b).astype(BF16).astype(F32)
        return rows[i, half]

    def turned(part, name, shift):
        name = (*name, shift % 128)
        if name not in rolled:
            rolled[name] = pltpu.roll(part, shift % 128, 1) if shift % 128 else part
        return rolled[name]

    def window(t, i, at):
        start = W * t - R
        low, high = max(start, 0) // 128, min(start + C - 1, 255) // 128
        value = turned(row(i, low), (i, low), at - start)
        if high != low:
            value = jnp.where(lane - at < 128 - start, value, turned(row(i, high), (i, high), at - start))
        if start < 0:
            value = jnp.where(lane - at < -start, 0.0, value)
        if start + C > 256:
            value = jnp.where(lane - at < 256 - start, value, 0.0)
        return value

    def measured(y, half):
        part = meas_ref[:, y, half * 128 : half * 128 + 128]
        return part * part * part * part

    for t in range(TILES):
        for g in range(3):
            value = window(t, 4 * g, 0)
            for s in range(1, 4):
                value = jnp.where(lane < C * s, value, window(t, 4 * g + s, C * s))
            if g < 2:
                value = jnp.where(lane < 4 * C, value, window(t, H + R - 1, 4 * C - 24 * g))
            out_ref[t, :, g * 128 : g * 128 + 128] = value
        half = t // 8
        value = turned(measured(0, half), ("m", 0, half), -W * t)
        for y in range(1, H):
            value = jnp.where(lane < W * y, value, turned(measured(y, half), ("m", y, half), W * y - W * t))
        out_ref[t, :, 384:512] = value


def group(value, g):
    return value[:, :, g * 128 : g * 128 + 128].reshape(Z, 128)


def fill_rows(packed_ref, rows_ref):
    for g in range(3):
        block = group(packed_ref, g).T
        rows_ref[g * 4 * C : (g + 1) * 4 * C, :] = block[: 4 * C]
        if g == 0:
            rows_ref[12 * C : 12 * C + 24, :] = block[4 * C :]
        if g == 1:
            rows_ref[12 * C + 24 : 12 * C + 32, :] = block[4 * C : 4 * C + 8]
    coded = group(packed_ref, 3)
    return jnp.where(coded > 0.0, jnp.sqrt(jnp.sqrt(coded)), 0.0).T


def spread_rows(rows_ref, taps_ref):
    for y in range(H + R):
        for b in range(E):
            start = y * C + b
            taps_ref[y * W : y * W + W, b * 128 : b * 128 + 128] = rows_ref[start : start + W, :].astype(BF16)


def add_products(taps_ref, psf_ref, sum_ref, offsets, count, taps_row, sum_rows, first):
    kernel = jnp.concatenate([psf_ref[offset].reshape(E * Z, Z) for offset in offsets], axis=1)
    product = jnp.dot(
        taps_ref[pl.ds(pl.multiple_of(taps_row * W, W), count * W), :], kernel, preferred_element_type=F32
    )
    for i, sum_row in enumerate(sum_rows):
        part = product[:, i * Z : i * Z + Z]
        if i and count == 1:
            break
        if i:
            part = jnp.where(first, part[W:], part[:-W])
        here = pl.ds(pl.multiple_of(sum_row * W, W), (count - i) * W)
        sum_ref[here, :] = sum_ref[here, :] + part


def inner_kernel(own_ref, psf_ref, sum_ref, meas_ref, rows_ref, taps_ref):
    core = lax.axis_index("core")
    meas_ref[...] = fill_rows(own_ref, rows_ref)
    spread_rows(rows_ref, taps_ref)
    sum_ref[...] = jnp.zeros(sum_ref.shape, F32)
    for k in range(R, -R - 1, -2):
        steps = range(k, max(k - 2, -R - 1), -1)
        add_products(
            taps_ref,
            psf_ref,
            sum_ref,
            [R + i * (1 - 2 * core) for i in steps],
            H + k,
            (R - k) * core,
            [(R - i) * (1 - core) for i in steps],
            core == 1,
        )


def ratio_kernel(inner_ref, meas_ref, next_ref, psf_ref, out_ref, rows_ref, taps_ref, sum_ref):
    core = lax.axis_index("core")
    even = core == 0
    beyond = fill_rows(next_ref, rows_ref)
    spread_rows(rows_ref, taps_ref)
    sum_ref[...] = inner_ref[...]
    for k in range(-R, R, 2):
        steps = (k, k + 1)
        add_products(
            taps_ref,
            psf_ref,
            sum_ref,
            [R + i * (1 - 2 * core) for i in steps],
            R - k,
            (H + k) * (1 - core),
            [(H + i) * core for i in steps],
            even,
        )
    here = pl.ds(pl.multiple_of(R * W * (1 - core), W), H * W)
    out_ref[here, :] = (meas_ref[...] / sum_ref[here, :]).astype(BF16)
    there = pl.ds(pl.multiple_of(H * W * core, W), R * W)
    beyond = jnp.where(even, beyond[(H - R) * W :], beyond[: R * W])
    out_ref[there, :] = (beyond / sum_ref[there, :]).astype(BF16)


def back_kernel(chip_ref, psf_ref, out_ref, rows_ref, sum_ref):
    first_row = lax.axis_index("core") * (H * W)
    for y in range(H + 2 * R):
        value = chip_ref[pl.ds(pl.multiple_of(first_row + y * W, W), W), :]
        for a in range(E):
            row = y + a - 2 * R
            if 0 <= row < H:
                rows_ref[row * W : row * W + W, a * 128 : a * 128 + 128] = value
    rows_ref[H * W : H * W + W, :] = jnp.ones((W, E * Z), BF16)
    sum_ref[...] = jnp.zeros((H * S, Z), F32)
    weight = jnp.zeros((1, Z), F32)
    for first in range(0, E, 2):
        pair = range(first, min(first + 2, E))
        kernel = jnp.concatenate(
            [psf_ref[a, first : first + len(pair)].reshape(len(pair) * Z, Z) for a in range(E)], axis=1
        )
        product = lax.dot_general(rows_ref[...], kernel, (((1,), (1,)), ((), ())), preferred_element_type=F32)
        for i, b in enumerate(pair):
            part = product[:, i * Z : i * Z + Z]
            for y in range(H):
                here = slice(y * S + b, y * S + b + W)
                sum_ref[here, :] = sum_ref[here, :] + part[y * W : y * W + W]
            weight = weight + part[H * W : H * W + 1]
    factor = SCALE / weight
    for g in range(2):
        share = (sum_ref[g * 128 : g * 128 + 128, :] * factor).T
        out_ref[:, :, g * 128 : g * 128 + 128] = share.reshape(TILES, 8, 128)


def final_kernel(parts_ref, vol_ref, out_ref):
    lane = lanes()
    for y in range(H):
        g, s = y // 4, y % 4
        turned = []
        for t in range(TILES):
            part = parts_ref[t, :, g * 128 : g * 128 + 128]
            shift = (W * t - R - S * s) % 128
            turned.append(pltpu.roll(part, shift, 1) if shift else part)
        for half in range(2):
            sums = [None, None]
            for t in range(TILES):
                start, stop = W * t - R - 128 * half, W * t + W + R - 128 * half
                start, stop = max(start, 0), min(stop, 128)
                if start >= stop:
                    continue
                before = sums[t % 2]
                sums[t % 2] = jnp.where(
                    (lane >= start) & (lane < stop), turned[t], 0.0 if before is None else before
                )
            here = slice(half * 128, half * 128 + 128)
            out_ref[:, y, here] = vol_ref[:, y, here] * ((sums[0] + sums[1]) * (1 / SCALE))


def body(volume, measured, point_spread):
    packed = pl.pallas_call(
        pack_kernel,
        out_shape=jax.ShapeDtypeStruct((TILES, 8, 512), F32),
        in_specs=[VM] * 2,
        out_specs=VM,
        compiler_params=PARAMS,
        cost_estimate=pl.CostEstimate(flops=20_000_000_000, bytes_accessed=2**20, transcendentals=0),
        name="pack",
    )(lax.all_gather(volume, "core"), measured)
    own = lax.all_to_all(packed.astype(F16), "depth", 0, 0, tiled=True)
    tile = ("pair", "core")
    count = lax.axis_size(tile)
    pairs = [(i, i + 1) for i in range(1, count - 1, 2)] + [(i, i - 1) for i in range(2, count, 2)]
    beyond = lax.ppermute(own, tile, pairs)
    rows = H + R
    scratch = [pltpu.VMEM((rows * C + 14, Z), F32), pltpu.VMEM((rows * W, E * Z), BF16)]
    inner, near = pl.pallas_call(
        inner_kernel,
        out_shape=[jax.ShapeDtypeStruct((rows * W, Z), F32), jax.ShapeDtypeStruct((H * W, Z), F32)],
        in_specs=[VM] * 2,
        out_specs=[VM] * 2,
        scratch_shapes=scratch,
        compiler_params=PARAMS,
        cost_estimate=pl.CostEstimate(flops=2 * 88 * W * E * Z * Z, bytes_accessed=2**22, transcendentals=0),
        name="inner",
    )(own.astype(F32), point_spread)
    ratio = pl.pallas_call(
        ratio_kernel,
        out_shape=jax.ShapeDtypeStruct((rows * W, Z), BF16),
        in_specs=[VM] * 4,
        out_specs=VM,
        scratch_shapes=[*scratch, pltpu.VMEM((rows * W, Z), F32)],
        compiler_params=PARAMS,
        name="ratio",
    )(inner, near, beyond.astype(F32), point_spread)
    chip_ratio = lax.all_gather(ratio, "core", tiled=True)
    shares = pl.pallas_call(
        back_kernel,
        out_shape=jax.ShapeDtypeStruct((TILES, 8, H * S), F32),
        in_specs=[VM] * 2,
        out_specs=VM,
        scratch_shapes=[
            pltpu.VMEM((H * W + W, E * Z), BF16),
            pltpu.VMEM((H * S, Z), F32),
        ],
        compiler_params=PARAMS,
        name="back",
    )(chip_ratio, point_spread)
    parts = lax.all_to_all(shares.astype(F16), "depth", 0, 0, tiled=True).astype(F32)
    return pl.pallas_call(
        final_kernel,
        out_shape=jax.ShapeDtypeStruct(volume.shape, F32),
        in_specs=[VM, VM],
        out_specs=VM,
        compiler_params=PARAMS,
        name="final",
    )(parts, volume)


def solution(mesh):
    depth, tile = mesh.devices.shape
    split = Mesh(mesh.devices.reshape(depth, tile // 2, 2), ("depth", "pair", "core"))
    spec = P("depth", ("pair", "core"), None)
    return jax.shard_map(body, mesh=split, in_specs=(spec, spec, P()), out_specs=spec, check_vma=False)
```

time: 55.4 us -> 54.9 us (level)
  starting transfers between devices: 11.4 us -> 9.69 us
  blocking collectives: 36.5 us -> 37.6 us
  local copies, waits for them, and re-layouts: 0.02 us -> 0.85 us
  other arithmetic: 0.9 us -> 0.08 us
    ppermute x1, starting transfers between devices: 11.4 us -> 9.69 us  [body(): beyond = lax.ppermute(own, tile, pairs)]
    another operation x1 -> x0, other arithmetic: 0.88 us -> none  [body(): jnp.stack([volume, measured])]
    unnamed x4 -> x6, local copies, waits for them, and re-layouts: 0.01 us -> 0.85 us
    all_to_all x2, blocking collectives: 32.7 us -> 33.6 us  [the longest x1 19.6 us: body(): own = lax.all_to_all(packed.astype(F16), 'depth', 0, 0, tiled=True)]
where the time goes in v9:
time: 54.9 us; the launch traced here: 54.7 us
  blocking collectives  37.6 us (68%)
  starting transfers between devices  9.69 us (18%)
  Pallas kernels  4.98 us (9%)
  waiting for transfers between devices  1.46 us (3%)
  local copies, waits for them, and re-layouts  0.85 us (2%)
    all_to_all x1, blocking collectives, body(): own = lax.all_to_all(packed.astype(F16), 'depth', 0, 0, tiled=True)  19.6 us
    all_to_all x1, blocking collectives, body(): lax.all_to_all(shares.astype(F16), 'depth', 0, 0, tiled=True).astype(F32)  14 us
    ppermute x1, starting transfers between devices, body(): beyond = lax.ppermute(own, tile, pairs)  9.69 us
    all_gather x1, blocking collectives, body(): lax.all_gather(volume, 'core')  2.1 us
    all_gather x1, blocking collectives, body(): chip_ratio = lax.all_gather(ratio, 'core', tiled=True)  1.88 us
    pallas_call x1, Pallas kernels, body(): pl.pallas_call(back_kernel, out_shape=jax.ShapeDtypeStruct((TILES, 8, H *...  1.53 us
    ppermute x1, waiting for transfers between devices, body(): beyond = lax.ppermute(own, tile, pairs)  1.46 us
    pallas_call x1, Pallas kernels, body(): pl.pallas_call(inner_kernel, out_shape=[jax.ShapeDtypeStruct((rows * W, Z...  1.14 us
  transfers between devices with their start and end apart: 1, of which 1 were waited for; matrix products, arithmetic and copies ran while one was open for 0% of the time, Pallas kernels for 2%

profile of v9, /device:TPU:8, one launch (start us, length us, event | category | flops | bytes accessed | tf_op | source)
XLA Modules:
  0.0 54.7 jit_solution(17127921661056149270)
XLA Ops:
  0.0 2.1 %all-gather = f32[16,8,256]{2,1,0:T(8,128)S(1)} all-gather(f32[8,8,256]{2,1,0:T(8,128)} %vol_ref.1), channel_id=2, replica_groups=mesh['depth'=16,'pair'=16,'core'=2] {'core'}, dimensions={0}, use_global_device_ids=true | all-gather | bytes 196608 | tf_op jit(solution)/shard_map/all_gather | solution.py:223
  2.1 0.0 copy-start.2
  2.1 0.8 %copy-done.2 = f32[8,8,256]{2,1,0:T(8,128)S(1)} copy-done((f32[8,8,256]{2,1,0:T(8,128)S(1)}, f32[8,8,256]{2,1,0:T(8,128)}, u32[]{:S(2)}) %copy-start.2) | copy-done | bytes 65560
  2.9 0.0 copy-start
  2.9 0.5 pack.1
  3.5 19.6 %all_to_all.10 = f16[16,8,512]{2,1,0:T(8,128)(2,1)S(1)} all-to-all(f16[16,8,512]{2,1,0:T(8,128)(2,1)S(1)} %convert_element_type.15), channel_id=1, replica_groups=mesh['depth'=16,'pair'=16,'core'=2] {'depth'}, dimensions={0} | all-to-all | bytes 262144 | tf_op jit(solution)/shard_map/all_to_all | solution.py:224
  23.1 9.7 %collective-permute-start = (f16[16,8,512]{2,1,0:T(8,128)(2,1)S(1)}, f16[16,8,512]{2,1,0:T(8,128)(2,1)S(1)}, u32[]{:S(2)}, u32[]{:S(2)}) collective-permute-start(f16[16,8,512]{2,1,0:T(8,128)(2,1)S(1)} %all_to_all.10), channel_id=1, source_target_pairs={{1,2},{3,4},{5,6},{7,8},{9,10},{11,12},{13,14},{15,16},{17,18},{19... | collective-permute-start | bytes 393224 | tf_op jit(solution)/shard_map/ppermute | solution.py:228
  32.8 0.0 copy-done
  32.8 1.1 %inner.1 = (f32[208,128]{1,0:T(8,128)S(1)}, f32[128,128]{1,0:T(8,128)S(1)}) custom-call(f32[16,8,512]{2,1,0:T(8,128)S(1)} %convert_element_type.16.own_ref, bf16[11,11,128,128]{3,2,1,0:T(8,128)(2,1)S(1)} %copy-done), custom_call_target="tpu_custom_call" | custom-call | flops 507510784 | bytes 4194304 | tf_op jit(solution)/shard_map/inner/pallas_call | solution.py:231
  33.9 1.5 %collective-permute-done = f16[16,8,512]{2,1,0:T(8,128)(2,1)S(1)} collective-permute-done((f16[16,8,512]{2,1,0:T(8,128)(2,1)S(1)}, f16[16,8,512]{2,1,0:T(8,128)(2,1)S(1)}, u32[]{:S(2)}, u32[]{:S(2)}) %collective-permute-start) | collective-permute-done | bytes 131104 | tf_op jit(solution)/shard_map/ppermute | solution.py:228
  35.4 0.0 copy-start.1
  35.4 0.9 %ratio.1 = bf16[208,128]{1,0:T(8,128)(2,1)S(1)} custom-call(f32[208,128]{1,0:T(8,128)S(1)} %get-tuple-element.7.inner_ref, f32[128,128]{1,0:T(8,128)S(1)} %get-tuple-element.8.meas_ref, f32[16,8,512]{2,1,0:T(8,128)S(1)} %convert_element_type.17.next_ref, bf16[11,11,128,128]{3,2,1,0:T(8,128)(2,1)S(1)} %copy-done), custom_call_target="tpu_custom_call" | custom-call | tf_op jit(solution)/shard_map/ratio/pallas_call | solution.py:241
  36.4 1.9 %all_gather.11.chip_ref = bf16[416,128]{1,0:T(8,128)(2,1)S(1)} all-gather(bf16[208,128]{1,0:T(8,128)(2,1)S(1)} %ratio.1), channel_id=1, replica_groups=mesh['depth'=16,'pair'=16,'core'=2] {'core'}, dimensions={0}, use_global_device_ids=true | all-gather | bytes 159744 | tf_op jit(solution)/shard_map/all_gather | solution.py:250
  38.3 1.5 %back.1 = f32[16,8,256]{2,1,0:T(8,128)S(1)} custom-call(bf16[416,128]{1,0:T(8,128)(2,1)S(1)} %all_gather.11.chip_ref, bf16[11,11,128,128]{3,2,1,0:T(8,128)(2,1)S(1)} %copy-done), custom_call_target="tpu_custom_call" | custom-call | tf_op jit(solution)/shard_map/back/pallas_call | solution.py:251
  39.8 14.0 %all_to_all.11 = f16[16,8,256]{2,1,0:T(8,128)(2,1)S(1)} all-to-all(f16[16,8,256]{2,1,0:T(8,128)(2,1)S(1)} %convert_element_type.18), channel_id=1, replica_groups=mesh['depth'=16,'pair'=16,'core'=2] {'depth'}, dimensions={0} | all-to-all | bytes 131072 | tf_op jit(solution)/shard_map/all_to_all | solution.py:263
  53.9 0.0 copy-done.1
  53.9 0.8 %final.1 = f32[8,8,256]{2,1,0:T(8,128)} custom-call(f32[16,8,256]{2,1,0:T(8,128)S(1)} %convert_element_type.19.parts_ref, f32[8,8,256]{2,1,0:T(8,128)S(1)} %copy-done.1), custom_call_target="tpu_custom_call" | custom-call | tf_op jit(solution)/shard_map/final/pallas_call | solution.py:264
  (5 shorter events, 0.1 us)
Async XLA Ops:
  2.1 0.8 %copy-start.2 = (f32[8,8,256]{2,1,0:T(8,128)S(1)}, f32[8,8,256]{2,1,0:T(8,128)}, u32[]{:S(2)}) copy-start(f32[8,8,256]{2,1,0:T(8,128)} %meas_ref.1) | copy-start | bytes 196612
  2.9 29.8 %copy-start = (bf16[11,11,128,128]{3,2,1,0:T(8,128)(2,1)S(1)}, bf16[11,11,128,128]{3,2,1,0:T(8,128)(2,1)}, u32[]{:S(2)}) copy-start(bf16[11,11,128,128]{3,2,1,0:T(8,128)(2,1)} %psf_ref.5) | copy-start | bytes 11894788
  23.1 12.3 %collective-permute-start = (f16[16,8,512]{2,1,0:T(8,128)(2,1)S(1)}, f16[16,8,512]{2,1,0:T(8,128)(2,1)S(1)}, u32[]{:S(2)}, u32[]{:S(2)}) collective-permute-start(f16[16,8,512]{2,1,0:T(8,128)(2,1)S(1)} %all_to_all.10), channel_id=1, source_target_pairs={{1,2},{3,4},{5,6},{7,8},{9,10},{11,12},{13,14},{15,16},{17,18},{19... | collective-permute-start | bytes 393224 | tf_op jit(solution)/shard_map/ppermute | solution.py:228
  35.4 18.4 %copy-start.1 = (f32[8,8,256]{2,1,0:T(8,128)S(1)}, f32[8,8,256]{2,1,0:T(8,128)}, u32[]{:S(2)}) copy-start(f32[8,8,256]{2,1,0:T(8,128)} %vol_ref.1) | copy-start | bytes 196612

commit v10 on v9

--- a/solution.py
+++ b/solution.py
@@ -26,77 +26,82 @@
     return lax.broadcasted_iota(jnp.int32, shape, 1)
 
 
+VOLUME_AT = [(0, C * i) for i in range(4)] + [(1, C * i) for i in range(4)]
+VOLUME_AT += [(2, 64 + C * i) for i in range(2)] + [(3, 48 + C * i) for i in range(3)]
+MEASURED_AT = [(2, W * i) for i in range(4)] + [(0, 4 * C)] + [(3, W * i) for i in range(3)]
+
+
 def pack_kernel(vol_ref, meas_ref, out_ref):
     even = lax.axis_index("core") == 0
     lane = lanes()
     rows = {}
     rolled = {}
 
-    def row(i, half):
-        if (i, half) not in rows:
-            here = slice(half * 128, half * 128 + 128)
-            a, b = [vol_ref[r // H, :, r % H, here] for r in (i, i + H - R)]
-            rows[i, half] = jnp.where(even, a, b).astype(BF16).astype(F32)
-        return rows[i, half]
-
-    def turned(part, name, shift):
-        name = (*name, shift % 128)
-        if name not in rolled:
-            rolled[name] = pltpu.roll(part, shift % 128, 1) if shift % 128 else part
-        return rolled[name]
-
-    def window(t, i, at):
+    def volume_row(j, half):
+        here = slice(half * 128, half * 128 + 128)
+        odd = j + 6 if j < 2 * R else j - 7
+        a, b = [vol_ref[r // H, :, r % H, here] for r in (j, odd)]
+        return jnp.where(even, a, b).astype(BF16).astype(F32)
+
+    def measured_row(j, half):
+        here = slice(half * 128, half * 128 + 128)
+        odd = j + 3 if j < R else j - R
+        part = jnp.where(even, meas_ref[:, j, here], meas_ref[:, odd, here])
+        part = part * part
+        return part * part
+
+    def turned(make, j, half, shift):
+        name = (make, j, half)
+        if name not in rows:
+            rows[name] = make(j, half)
+        shift = shift % 128
+        if (name, shift) not in rolled:
+            rolled[name, shift] = pltpu.roll(rows[name], shift, 1) if shift else rows[name]
+        return rolled[name, shift]
+
+    def window(t, j, at):
         start = W * t - R
         low, high = max(start, 0) // 128, min(start + C - 1, 255) // 128
-        value = turned(row(i, low), (i, low), at - start)
+        value = turned(volume_row, j, low, at - start)
         if high != low:
-            value = jnp.where(lane - at < 128 - start, value, turned(row(i, high), (i, high), at - start))
+            value = jnp.where(lane - at < 128 - start, value, turned(volume_row, j, high, at - start))
         if start < 0:
             value = jnp.where(lane - at < -start, 0.0, value)
         if start + C > 256:
             value = jnp.where(lane - at < 256 - start, value, 0.0)
         return value
 
-    def measured(y, half):
-        part = meas_ref[:, y, half * 128 : half * 128 + 128]
-        return part * part * part * part
-
     for t in range(TILES):
-        for g in range(3):
-            value = window(t, 4 * g, 0)
-            for s in range(1, 4):
-                value = jnp.where(lane < C * s, value, window(t, 4 * g + s, C * s))
-            if g < 2:
-                value = jnp.where(lane < 4 * C, value, window(t, H + R - 1, 4 * C - 24 * g))
+        for g in range(4):
+            parts = [(at, window(t, j, at)) for j, (where, at) in enumerate(VOLUME_AT) if where == g]
+            parts += [
+                (at, turned(measured_row, j, t // 8, at - W * t)) for j, (where, at) in enumerate(MEASURED_AT) if where == g
+            ]
+            parts.sort(key=lambda part: part[0])
+            value = parts[0][1]
+            for at, part in parts[1:]:
+                value = jnp.where(lane < at, value, part)
             out_ref[t, :, g * 128 : g * 128 + 128] = value
-        half = t // 8
-        value = turned(measured(0, half), ("m", 0, half), -W * t)
-        for y in range(1, H):
-            value = jnp.where(lane < W * y, value, turned(measured(y, half), ("m", y, half), W * y - W * t))
-        out_ref[t, :, 384:512] = value
-
-
-def group(value, g):
-    return value[:, :, g * 128 : g * 128 + 128].reshape(Z, 128)
-
-
-def fill_rows(packed_ref, rows_ref):
-    for g in range(3):
-        block = group(packed_ref, g).T
-        rows_ref[g * 4 * C : (g + 1) * 4 * C, :] = block[: 4 * C]
-        if g == 0:
-            rows_ref[12 * C : 12 * C + 24, :] = block[4 * C :]
-        if g == 1:
-            rows_ref[12 * C + 24 : 12 * C + 32, :] = block[4 * C : 4 * C + 8]
-    coded = group(packed_ref, 3)
-    return jnp.where(coded > 0.0, jnp.sqrt(jnp.sqrt(coded)), 0.0).T
-
-
-def spread_rows(rows_ref, taps_ref):
-    for y in range(H + R):
-        for b in range(E):
-            start = y * C + b
-            taps_ref[y * W : y * W + W, b * 128 : b * 128 + 128] = rows_ref[start : start + W, :].astype(BF16)
+
+
+def turned_groups(packed_ref, count):
+    return [packed_ref[:, :, g * 128 : g * 128 + 128].reshape(Z, 128).T for g in range(count)]
+
+
+def decoded(value):
+    return jnp.where(value > 0.0, jnp.sqrt(jnp.sqrt(value)), 0.0)
+
+
+def fill_first_rows(blocks, rows_ref):
+    rows_ref[: 4 * C, :] = blocks[0][: 4 * C]
+    rows_ref[4 * C : 8 * C, :] = blocks[1][: 4 * C]
+    rows_ref[8 * C : 8 * C + 56, :] = blocks[2][64:120]
+
+
+def spread_row(rows_ref, taps_ref, start, row):
+    here = pl.ds(pl.multiple_of(row * W, W), W)
+    for b in range(E):
+        taps_ref[here, b * 128 : b * 128 + 128] = rows_ref[start + b : start + b + W, :].astype(BF16)
 
 
 def add_products(taps_ref, psf_ref, sum_ref, offsets, count, taps_row, sum_rows, first):
@@ -116,8 +121,17 @@
 
 def inner_kernel(own_ref, psf_ref, sum_ref, meas_ref, rows_ref, taps_ref):
     core = lax.axis_index("core")
-    meas_ref[...] = fill_rows(own_ref, rows_ref)
-    spread_rows(rows_ref, taps_ref)
+    blocks = turned_groups(own_ref, 4)
+    fill_first_rows(blocks, rows_ref)
+    rows_ref[264:344, :] = blocks[3][48:]
+    for j in range(H + R):
+        if j < 2 * R:
+            spread_row(rows_ref, taps_ref, j * C, j + 3 * core)
+        else:
+            spread_row(rows_ref, taps_ref, 264 + (j - 2 * R) * C, j - 2 * R * core)
+    for part, even_row, odd_row in ((blocks[2][:64], 0, 3), (blocks[0][4 * C : 4 * C + W], 4, 7), (blocks[3][:48], 5, 0)):
+        row = even_row + (odd_row - even_row) * core
+        meas_ref[pl.ds(pl.multiple_of(row * W, W), part.shape[0]), :] = decoded(part)
     sum_ref[...] = jnp.zeros(sum_ref.shape, F32)
     for k in range(R, -R - 1, -2):
         steps = range(k, max(k - 2, -R - 1), -1)
@@ -136,8 +150,10 @@
 def ratio_kernel(inner_ref, meas_ref, next_ref, psf_ref, out_ref, rows_ref, taps_ref, sum_ref):
     core = lax.axis_index("core")
     even = core == 0
-    beyond = fill_rows(next_ref, rows_ref)
-    spread_rows(rows_ref, taps_ref)
+    blocks = turned_groups(next_ref, 3)
+    fill_first_rows(blocks, rows_ref)
+    for j in range(2 * R):
+        spread_row(rows_ref, taps_ref, j * C, j)
     sum_ref[...] = inner_ref[...]
     for k in range(-R, R, 2):
         steps = (k, k + 1)
@@ -147,15 +163,16 @@
             sum_ref,
             [R + i * (1 - 2 * core) for i in steps],
             R - k,
-            (H + k) * (1 - core),
+            (R + k) * (1 - core),
             [(H + i) * core for i in steps],
             even,
         )
     here = pl.ds(pl.multiple_of(R * W * (1 - core), W), H * W)
     out_ref[here, :] = (meas_ref[...] / sum_ref[here, :]).astype(BF16)
-    there = pl.ds(pl.multiple_of(H * W * core, W), R * W)
-    beyond = jnp.where(even, beyond[(H - R) * W :], beyond[: R * W])
-    out_ref[there, :] = (beyond / sum_ref[there, :]).astype(BF16)
+    there = H * W * core
+    for part, row in ((blocks[2][:64], 0), (blocks[0][4 * C : 4 * C + W], 4)):
+        here = pl.ds(pl.multiple_of(there + row * W, W), part.shape[0])
+        out_ref[here, :] = (decoded(part) / sum_ref[here, :]).astype(BF16)
 
 
 def back_kernel(chip_ref, psf_ref, out_ref, rows_ref, sum_ref):
@@ -225,7 +242,7 @@
     tile = ("pair", "core")
     count = lax.axis_size(tile)
     pairs = [(i, i + 1) for i in range(1, count - 1, 2)] + [(i, i - 1) for i in range(2, count, 2)]
-    beyond = lax.ppermute(own, tile, pairs)
+    beyond = lax.ppermute(own[:, :, :384], tile, pairs)
     rows = H + R
     scratch = [pltpu.VMEM((rows * C + 14, Z), F32), pltpu.VMEM((rows * W, E * Z), BF16)]
     inner, near = pl.pallas_call(

time: 54.9 us -> 54.5 us (level)
  no operation moved by 1% of the time
where the time goes in v10:
time: 54.5 us; the launch traced here: 54.3 us
  blocking collectives  37.7 us (69%)
  starting transfers between devices  9.7 us (18%)
  Pallas kernels  4.83 us (9%)
  waiting for transfers between devices  1.06 us (2%)
  local copies, waits for them, and re-layouts  0.87 us (2%)
    all_to_all x1, blocking collectives, body(): own = lax.all_to_all(packed.astype(F16), 'depth', 0, 0, tiled=True)  19.7 us
    all_to_all x1, blocking collectives, body(): lax.all_to_all(shares.astype(F16), 'depth', 0, 0, tiled=True).astype(F32)  14 us
    ppermute x1, starting transfers between devices, body(): beyond = lax.ppermute(own[:, :, :384], tile, pairs)  9.7 us
    all_gather x1, blocking collectives, body(): lax.all_gather(volume, 'core')  2.1 us
    all_gather x1, blocking collectives, body(): chip_ratio = lax.all_gather(ratio, 'core', tiled=True)  1.88 us
    pallas_call x1, Pallas kernels, body(): pl.pallas_call(back_kernel, out_shape=jax.ShapeDtypeStruct((TILES, 8, H *...  1.52 us
    pallas_call x1, Pallas kernels, body(): pl.pallas_call(inner_kernel, out_shape=[jax.ShapeDtypeStruct((rows * W, Z...  1.19 us
  transfers between devices with their start and end apart: 1, of which 1 were waited for; matrix products, arithmetic and copies ran while one was open for 0% of the time, Pallas kernels for 2%

profile of v10, /device:TPU:8, one launch (start us, length us, event | category | flops | bytes accessed | tf_op | source)
XLA Modules:
  0.0 54.3 jit_solution(11043666559694220353)
XLA Ops:
  0.0 2.1 %all-gather = f32[16,8,256]{2,1,0:T(8,128)S(1)} all-gather(f32[8,8,256]{2,1,0:T(8,128)} %vol_ref.1), channel_id=2, replica_groups=mesh['depth'=16,'pair'=16,'core'=2] {'core'}, dimensions={0}, use_global_device_ids=true | all-gather | bytes 196608 | tf_op jit(solution)/shard_map/all_gather | solution.py:240
  2.1 0.0 copy-start.2
  2.1 0.8 %copy-done.2 = f32[8,8,256]{2,1,0:T(8,128)S(1)} copy-done((f32[8,8,256]{2,1,0:T(8,128)S(1)}, f32[8,8,256]{2,1,0:T(8,128)}, u32[]{:S(2)}) %copy-start.2) | copy-done | bytes 65560
  2.9 0.0 copy-start
  2.9 0.4 pack.1
  3.3 19.7 %all_to_all.10 = f16[16,8,512]{2,1,0:T(8,128)(2,1)S(1)} all-to-all(f16[16,8,512]{2,1,0:T(8,128)(2,1)S(1)} %convert_element_type.15), channel_id=1, replica_groups=mesh['depth'=16,'pair'=16,'core'=2] {'depth'}, dimensions={0} | all-to-all | bytes 262144 | tf_op jit(solution)/shard_map/all_to_all | solution.py:241
  23.1 9.7 %collective-permute-start = (f16[16,8,384]{2,1,0:T(8,128)(2,1)S(1)}, f16[16,8,384]{2,1,0:T(8,128)(2,1)S(1)}, u32[]{:S(2)}, u32[]{:S(2)}) collective-permute-start(f16[16,8,384]{2,1,0:T(8,128)(2,1)S(1)} %slice.4), channel_id=1, source_target_pairs={{1,2},{3,4},{5,6},{7,8},{9,10},{11,12},{13,14},{15,16},{17,18},{19... | collective-permute-start | bytes 294920 | tf_op jit(solution)/shard_map/ppermute | solution.py:245
  32.8 0.0 copy-done
  32.8 1.2 %inner.1 = (f32[208,128]{1,0:T(8,128)S(1)}, f32[128,128]{1,0:T(8,128)S(1)}) custom-call(f32[16,8,512]{2,1,0:T(8,128)S(1)} %convert_element_type.16.own_ref, bf16[11,11,128,128]{3,2,1,0:T(8,128)(2,1)S(1)} %copy-done), custom_call_target="tpu_custom_call" | custom-call | flops 507510784 | bytes 4194304 | tf_op jit(solution)/shard_map/inner/pallas_call | solution.py:248
  34.0 1.1 %collective-permute-done = f16[16,8,384]{2,1,0:T(8,128)(2,1)S(1)} collective-permute-done((f16[16,8,384]{2,1,0:T(8,128)(2,1)S(1)}, f16[16,8,384]{2,1,0:T(8,128)(2,1)S(1)}, u32[]{:S(2)}, u32[]{:S(2)}) %collective-permute-start) | collective-permute-done | bytes 98336 | tf_op jit(solution)/shard_map/ppermute | solution.py:245
  35.1 0.0 copy-start.1
  35.1 0.9 %ratio.1 = bf16[208,128]{1,0:T(8,128)(2,1)S(1)} custom-call(f32[208,128]{1,0:T(8,128)S(1)} %get-tuple-element.7.inner_ref, f32[128,128]{1,0:T(8,128)S(1)} %get-tuple-element.8.meas_ref, f32[16,8,384]{2,1,0:T(8,128)S(1)} %convert_element_type.17.next_ref, bf16[11,11,128,128]{3,2,1,0:T(8,128)(2,1)S(1)} %copy-done), custom_call_target="tpu_custom_call" | custom-call | tf_op jit(solution)/shard_map/ratio/pallas_call | solution.py:258
  36.0 1.9 %all_gather.11.chip_ref = bf16[416,128]{1,0:T(8,128)(2,1)S(1)} all-gather(bf16[208,128]{1,0:T(8,128)(2,1)S(1)} %ratio.1), channel_id=1, replica_groups=mesh['depth'=16,'pair'=16,'core'=2] {'core'}, dimensions={0}, use_global_device_ids=true | all-gather | bytes 159744 | tf_op jit(solution)/shard_map/all_gather | solution.py:267
  37.9 1.5 %back.1 = f32[16,8,256]{2,1,0:T(8,128)S(1)} custom-call(bf16[416,128]{1,0:T(8,128)(2,1)S(1)} %all_gather.11.chip_ref, bf16[11,11,128,128]{3,2,1,0:T(8,128)(2,1)S(1)} %copy-done), custom_call_target="tpu_custom_call" | custom-call | tf_op jit(solution)/shard_map/back/pallas_call | solution.py:268
  39.4 14.0 %all_to_all.11 = f16[16,8,256]{2,1,0:T(8,128)(2,1)S(1)} all-to-all(f16[16,8,256]{2,1,0:T(8,128)(2,1)S(1)} %convert_element_type.18), channel_id=1, replica_groups=mesh['depth'=16,'pair'=16,'core'=2] {'depth'}, dimensions={0} | all-to-all | bytes 131072 | tf_op jit(solution)/shard_map/all_to_all | solution.py:280
  53.5 0.0 copy-done.1
  53.5 0.8 %final.1 = f32[8,8,256]{2,1,0:T(8,128)} custom-call(f32[16,8,256]{2,1,0:T(8,128)S(1)} %convert_element_type.19.parts_ref, f32[8,8,256]{2,1,0:T(8,128)S(1)} %copy-done.1), custom_call_target="tpu_custom_call" | custom-call | tf_op jit(solution)/shard_map/final/pallas_call | solution.py:281
  (6 shorter events, 0.1 us)
Async XLA Ops:
  2.1 0.8 %copy-start.2 = (f32[8,8,256]{2,1,0:T(8,128)S(1)}, f32[8,8,256]{2,1,0:T(8,128)}, u32[]{:S(2)}) copy-start(f32[8,8,256]{2,1,0:T(8,128)} %meas_ref.1) | copy-start | bytes 196612
  2.9 29.9 %copy-start = (bf16[11,11,128,128]{3,2,1,0:T(8,128)(2,1)S(1)}, bf16[11,11,128,128]{3,2,1,0:T(8,128)(2,1)}, u32[]{:S(2)}) copy-start(bf16[11,11,128,128]{3,2,1,0:T(8,128)(2,1)} %psf_ref.5) | copy-start | bytes 11894788
  23.1 12.0 %collective-permute-start = (f16[16,8,384]{2,1,0:T(8,128)(2,1)S(1)}, f16[16,8,384]{2,1,0:T(8,128)(2,1)S(1)}, u32[]{:S(2)}, u32[]{:S(2)}) collective-permute-start(f16[16,8,384]{2,1,0:T(8,128)(2,1)S(1)} %slice.4), channel_id=1, source_target_pairs={{1,2},{3,4},{5,6},{7,8},{9,10},{11,12},{13,14},{15,16},{17,18},{19... | collective-permute-start | bytes 294920 | tf_op jit(solution)/shard_map/ppermute | solution.py:245
  35.1 18.4 %copy-start.1 = (f32[8,8,256]{2,1,0:T(8,128)S(1)}, f32[8,8,256]{2,1,0:T(8,128)}, u32[]{:S(2)}) copy-start(f32[8,8,256]{2,1,0:T(8,128)} %vol_ref.1) | copy-start | bytes 196612

commit v11 on v10

--- a/solution.py
+++ b/solution.py
@@ -31,7 +31,8 @@
 MEASURED_AT = [(2, W * i) for i in range(4)] + [(0, 4 * C)] + [(3, W * i) for i in range(3)]
 
 
-def pack_kernel(vol_ref, meas_ref, out_ref):
+def pack_kernel(both_ref, mate_ref, out_ref):
+    vol_ref, meas_ref = both_ref.at[0], both_ref.at[1]
     even = lax.axis_index("core") == 0
     lane = lanes()
     rows = {}
@@ -39,8 +40,11 @@
 
     def volume_row(j, half):
         here = slice(half * 128, half * 128 + 128)
-        odd = j + 6 if j < 2 * R else j - 7
-        a, b = [vol_ref[r // H, :, r % H, here] for r in (j, odd)]
+        a = vol_ref[:, j, here] if j < H else mate_ref[:, j - H, here]
+        if j < 2 * R:
+            b = mate_ref[:, j + 6, here] if j < 2 else vol_ref[:, j - 2, here]
+        else:
+            b = mate_ref[:, j - 7, here]
         return jnp.where(even, a, b).astype(BF16).astype(F32)
 
     def measured_row(j, half):
@@ -237,7 +241,7 @@
         compiler_params=PARAMS,
         cost_estimate=pl.CostEstimate(flops=20_000_000_000, bytes_accessed=2**20, transcendentals=0),
         name="pack",
-    )(lax.all_gather(volume, "core"), measured)
+    )(jnp.stack([volume, measured]), lax.ppermute(volume, "core", [(0, 1), (1, 0)]))
     own = lax.all_to_all(packed.astype(F16), "depth", 0, 0, tiled=True)
     tile = ("pair", "core")
     count = lax.axis_size(tile)

time: 54.5 us -> 54.8 us (level)
  blocking collectives: 37.7 us -> 35.5 us
  starting transfers between devices: 9.7 us -> 11.6 us
  other arithmetic: 0.08 us -> 0.96 us
  local copies, waits for them, and re-layouts: 0.87 us -> 0.03 us
    all_gather x1 -> x0, blocking collectives: 2.1 us -> none  [body(): lax.all_gather(volume, 'core')]
    ppermute x0 -> x1, starting transfers between devices: none -> 1.91 us  [body(): lax.ppermute(volume, 'core', [(0, 1), (1, 0)])]
    another operation x0 -> x1, other arithmetic: none -> 0.88 us  [body(): jnp.stack([volume, measured])]
    unnamed x6 -> x4, local copies, waits for them, and re-layouts: 0.85 us -> 0.01 us
  transfers between devices with their start and end apart: 1 -> 2, of which waited for: 1 -> 2; matrix products, arithmetic and copies ran while one was open for 0% -> 2% of each run, Pallas kernels for 2% -> 2%
where the time goes in v11:
time: 54.8 us; the launch traced here: 54.6 us
  blocking collectives  35.5 us (65%)
  starting transfers between devices  11.6 us (21%)
  Pallas kernels  4.84 us (9%)
  waiting for transfers between devices  1.59 us (3%)
  other arithmetic  0.96 us (2%)
    all_to_all x1, blocking collectives, body(): own = lax.all_to_all(packed.astype(F16), 'depth', 0, 0, tiled=True)  19.6 us
    all_to_all x1, blocking collectives, body(): lax.all_to_all(shares.astype(F16), 'depth', 0, 0, tiled=True).astype(F32)  14 us
    ppermute x1, starting transfers between devices, body(): beyond = lax.ppermute(own[:, :, :384], tile, pairs)  9.7 us
    ppermute x1, starting transfers between devices, body(): lax.ppermute(volume, 'core', [(0, 1), (1, 0)])  1.91 us
    all_gather x1, blocking collectives, body(): chip_ratio = lax.all_gather(ratio, 'core', tiled=True)  1.88 us
    pallas_call x1, Pallas kernels, body(): pl.pallas_call(back_kernel, out_shape=jax.ShapeDtypeStruct((TILES, 8, H *...  1.53 us
    pallas_call x1, Pallas kernels, body(): pl.pallas_call(inner_kernel, out_shape=[jax.ShapeDtypeStruct((rows * W, Z...  1.19 us
  transfers between devices with their start and end apart: 2, of which 2 were waited for; matrix products, arithmetic and copies ran while one was open for 2% of the time, Pallas kernels for 2%

profile of v11, /device:TPU:8, one launch (start us, length us, event | category | flops | bytes accessed | tf_op | source)
XLA Modules:
  0.0 54.6 jit_solution(438629909939399330)
XLA Ops:
  0.0 1.9 %collective-permute-start = (f32[8,8,256]{2,1,0:T(8,128)}, f32[8,8,256]{2,1,0:T(8,128)S(1)}, u32[]{:S(2)}, u32[]{:S(2)}) collective-permute-start(f32[8,8,256]{2,1,0:T(8,128)} %vol_ref.1), channel_id=1, source_target_pairs={{0,1},{1,0},{2,3},{3,2},{4,5},{5,4},{6,7},{7,6},{8,9},{9,8},{10,11... | collective-permute-start | bytes 196616 | tf_op jit(solution)/shard_map/ppermute | solution.py:244
  1.9 0.9 %pad_maximum_fusion.both_ref = f32[2,8,8,256]{3,2,1,0:T(8,128)S(1)} fusion(f32[1,8,8,256]{3,2,1,0:T(8,128)} %bitcast.3, f32[1,8,8,256]{3,2,1,0:T(8,128)} %bitcast.2), kind=kLoop, calls=%fused_computation | loop fusion | flops 32768 | bytes 262144 | tf_op jit(solution)/shard_map/stack | solution.py:244
  2.8 0.0 copy-start
  2.8 0.5 collective-permute-done.mate_ref
  3.4 0.4 pack.1
  3.8 19.6 %all_to_all.10 = f16[16,8,512]{2,1,0:T(8,128)(2,1)S(1)} all-to-all(f16[16,8,512]{2,1,0:T(8,128)(2,1)S(1)} %convert_element_type.15), channel_id=1, replica_groups=mesh['depth'=16,'pair'=16,'core'=2] {'depth'}, dimensions={0} | all-to-all | bytes 262144 | tf_op jit(solution)/shard_map/all_to_all | solution.py:245
  23.3 9.7 %collective-permute-start.1 = (f16[16,8,384]{2,1,0:T(8,128)(2,1)S(1)}, f16[16,8,384]{2,1,0:T(8,128)(2,1)S(1)}, u32[]{:S(2)}, u32[]{:S(2)}) collective-permute-start(f16[16,8,384]{2,1,0:T(8,128)(2,1)S(1)} %slice.4), channel_id=1, source_target_pairs={{1,2},{3,4},{5,6},{7,8},{9,10},{11,12},{13,14},{15,16},{17,18},{19... | collective-permute-start | bytes 294920 | tf_op jit(solution)/shard_map/ppermute | solution.py:249
  33.1 0.0 copy-done
  33.1 1.2 %inner.1 = (f32[208,128]{1,0:T(8,128)S(1)}, f32[128,128]{1,0:T(8,128)S(1)}) custom-call(f32[16,8,512]{2,1,0:T(8,128)S(1)} %convert_element_type.16.own_ref, bf16[11,11,128,128]{3,2,1,0:T(8,128)(2,1)S(1)} %copy-done), custom_call_target="tpu_custom_call" | custom-call | flops 507510784 | bytes 4194304 | tf_op jit(solution)/shard_map/inner/pallas_call | solution.py:252
  34.3 1.1 %collective-permute-done.1 = f16[16,8,384]{2,1,0:T(8,128)(2,1)S(1)} collective-permute-done((f16[16,8,384]{2,1,0:T(8,128)(2,1)S(1)}, f16[16,8,384]{2,1,0:T(8,128)(2,1)S(1)}, u32[]{:S(2)}, u32[]{:S(2)}) %collective-permute-start.1) | collective-permute-done | bytes 98336 | tf_op jit(solution)/shard_map/ppermute | solution.py:249
  35.3 0.0 copy-start.1
  35.4 0.9 %ratio.1 = bf16[208,128]{1,0:T(8,128)(2,1)S(1)} custom-call(f32[208,128]{1,0:T(8,128)S(1)} %get-tuple-element.7.inner_ref, f32[128,128]{1,0:T(8,128)S(1)} %get-tuple-element.8.meas_ref, f32[16,8,384]{2,1,0:T(8,128)S(1)} %convert_element_type.17.next_ref, bf16[11,11,128,128]{3,2,1,0:T(8,128)(2,1)S(1)} %copy-done), custom_call_target="tpu_custom_call" | custom-call | tf_op jit(solution)/shard_map/ratio/pallas_call | solution.py:262
  36.3 1.9 %all_gather.3.chip_ref = bf16[416,128]{1,0:T(8,128)(2,1)S(1)} all-gather(bf16[208,128]{1,0:T(8,128)(2,1)S(1)} %ratio.1), channel_id=1, replica_groups=mesh['depth'=16,'pair'=16,'core'=2] {'core'}, dimensions={0}, use_global_device_ids=true | all-gather | bytes 159744 | tf_op jit(solution)/shard_map/all_gather | solution.py:271
  38.2 1.5 %back.1 = f32[16,8,256]{2,1,0:T(8,128)S(1)} custom-call(bf16[416,128]{1,0:T(8,128)(2,1)S(1)} %all_gather.3.chip_ref, bf16[11,11,128,128]{3,2,1,0:T(8,128)(2,1)S(1)} %copy-done), custom_call_target="tpu_custom_call" | custom-call | tf_op jit(solution)/shard_map/back/pallas_call | solution.py:272
  39.7 14.0 %all_to_all.11 = f16[16,8,256]{2,1,0:T(8,128)(2,1)S(1)} all-to-all(f16[16,8,256]{2,1,0:T(8,128)(2,1)S(1)} %convert_element_type.18), channel_id=1, replica_groups=mesh['depth'=16,'pair'=16,'core'=2] {'depth'}, dimensions={0} | all-to-all | bytes 131072 | tf_op jit(solution)/shard_map/all_to_all | solution.py:284
  53.8 0.0 copy-done.1
  53.8 0.8 %final.1 = f32[8,8,256]{2,1,0:T(8,128)} custom-call(f32[16,8,256]{2,1,0:T(8,128)S(1)} %convert_element_type.19.parts_ref, f32[8,8,256]{2,1,0:T(8,128)S(1)} %copy-done.1), custom_call_target="tpu_custom_call" | custom-call | tf_op jit(solution)/shard_map/final/pallas_call | solution.py:285
  (6 shorter events, 0.1 us)
Async XLA Ops:
  0.0 3.3 %collective-permute-start = (f32[8,8,256]{2,1,0:T(8,128)}, f32[8,8,256]{2,1,0:T(8,128)S(1)}, u32[]{:S(2)}, u32[]{:S(2)}) collective-permute-start(f32[8,8,256]{2,1,0:T(8,128)} %vol_ref.1), channel_id=1, source_target_pairs={{0,1},{1,0},{2,3},{3,2},{4,5},{5,4},{6,7},{7,6},{8,9},{9,8},{10,11... | collective-permute-start | bytes 196616 | tf_op jit(solution)/shard_map/ppermute | solution.py:244
  2.8 30.3 %copy-start = (bf16[11,11,128,128]{3,2,1,0:T(8,128)(2,1)S(1)}, bf16[11,11,128,128]{3,2,1,0:T(8,128)(2,1)}, u32[]{:S(2)}) copy-start(bf16[11,11,128,128]{3,2,1,0:T(8,128)(2,1)} %psf_ref.5) | copy-start | bytes 11894788
  23.3 12.0 %collective-permute-start.1 = (f16[16,8,384]{2,1,0:T(8,128)(2,1)S(1)}, f16[16,8,384]{2,1,0:T(8,128)(2,1)S(1)}, u32[]{:S(2)}, u32[]{:S(2)}) collective-permute-start(f16[16,8,384]{2,1,0:T(8,128)(2,1)S(1)} %slice.4), channel_id=1, source_target_pairs={{1,2},{3,4},{5,6},{7,8},{9,10},{11,12},{13,14},{15,16},{17,18},{19... | collective-permute-start | bytes 294920 | tf_op jit(solution)/shard_map/ppermute | solution.py:249
  35.3 18.4 %copy-start.1 = (f32[8,8,256]{2,1,0:T(8,128)S(1)}, f32[8,8,256]{2,1,0:T(8,128)}, u32[]{:S(2)}) copy-start(f32[8,8,256]{2,1,0:T(8,128)} %vol_ref.1) | copy-start | bytes 196612

commit v12 on v10

--- a/solution.py
+++ b/solution.py
@@ -29,6 +29,10 @@
 VOLUME_AT = [(0, C * i) for i in range(4)] + [(1, C * i) for i in range(4)]
 VOLUME_AT += [(2, 64 + C * i) for i in range(2)] + [(3, 48 + C * i) for i in range(3)]
 MEASURED_AT = [(2, W * i) for i in range(4)] + [(0, 4 * C)] + [(3, W * i) for i in range(3)]
+
+
+def mark_kernel(out_ref):
+    out_ref[...] = jnp.zeros(out_ref.shape, F32)
 
 
 def pack_kernel(vol_ref, meas_ref, out_ref):
@@ -204,7 +208,7 @@
         out_ref[:, :, g * 128 : g * 128 + 128] = share.reshape(TILES, 8, 128)
 
 
-def final_kernel(parts_ref, vol_ref, out_ref):
+def final_kernel(parts_ref, vol_ref, mark_ref, out_ref):
     lane = lanes()
     for y in range(H):
         g, s = y // 4, y % 4
@@ -229,6 +233,14 @@
 
 
 def body(volume, measured, point_spread):
+    mark = pl.pallas_call(
+        mark_kernel,
+        out_shape=jax.ShapeDtypeStruct((8, 128), F32),
+        out_specs=VM,
+        cost_estimate=pl.CostEstimate(flops=20_000_000_000, bytes_accessed=2**20, transcendentals=0),
+        name="mark",
+    )()
+    volume_first, mark = lax.optimization_barrier((volume, mark))
     packed = pl.pallas_call(
         pack_kernel,
         out_shape=jax.ShapeDtypeStruct((TILES, 8, 512), F32),
@@ -237,7 +249,7 @@
         compiler_params=PARAMS,
         cost_estimate=pl.CostEstimate(flops=20_000_000_000, bytes_accessed=2**20, transcendentals=0),
         name="pack",
-    )(lax.all_gather(volume, "core"), measured)
+    )(lax.all_gather(volume_first, "core"), measured)
     own = lax.all_to_all(packed.astype(F16), "depth", 0, 0, tiled=True)
     tile = ("pair", "core")
     count = lax.axis_size(tile)
@@ -281,11 +293,11 @@
     return pl.pallas_call(
         final_kernel,
         out_shape=jax.ShapeDtypeStruct(volume.shape, F32),
-        in_specs=[VM, VM],
+        in_specs=[VM, VM, pl.BlockSpec(memory_space=pl.ANY)],
         out_specs=VM,
         compiler_params=PARAMS,
         name="final",
-    )(parts, volume)
+    )(parts, volume, mark)
 
 
 def solution(mesh):

time: 54.5 us -> 54.3 us (level)
  Pallas kernels: 4.83 us -> 5.43 us
  local copies, waits for them, and re-layouts: 0.87 us -> 0.28 us
    pallas_call x0 -> x1, Pallas kernels: none -> 0.59 us  [body(): pl.pallas_call(mark_kernel, out_shape=jax.ShapeDtypeStruct((8, 128), F32)...]
    unnamed x6 -> x8, local copies, waits for them, and re-layouts: 0.85 us -> 0.26 us
where the time goes in v12:
time: 54.3 us; the launch traced here: 54.1 us
  blocking collectives  37.5 us (69%)
  starting transfers between devices  9.7 us (18%)
  Pallas kernels  5.43 us (10%)
  waiting for transfers between devices  1.06 us (2%)
    all_to_all x1, blocking collectives, body(): own = lax.all_to_all(packed.astype(F16), 'depth', 0, 0, tiled=True)  19.7 us
    all_to_all x1, blocking collectives, body(): lax.all_to_all(shares.astype(F16), 'depth', 0, 0, tiled=True).astype(F32)  14 us
    ppermute x1, starting transfers between devices, body(): beyond = lax.ppermute(own[:, :, :384], tile, pairs)  9.7 us
    all_gather x1, blocking collectives, body(): lax.all_gather(volume_first, 'core')  1.89 us
    all_gather x1, blocking collectives, body(): chip_ratio = lax.all_gather(ratio, 'core', tiled=True)  1.88 us
    pallas_call x1, Pallas kernels, body(): pl.pallas_call(back_kernel, out_shape=jax.ShapeDtypeStruct((TILES, 8, H *...  1.53 us
    pallas_call x1, Pallas kernels, body(): pl.pallas_call(inner_kernel, out_shape=[jax.ShapeDtypeStruct((rows * W, Z...  1.19 us
  transfers between devices with their start and end apart: 1, of which 1 were waited for; matrix products, arithmetic and copies ran while one was open for 0% of the time, Pallas kernels for 2%

profile of v12, /device:TPU:8, one launch (start us, length us, event | category | flops | bytes accessed | tf_op | source)
XLA Modules:
  0.0 54.1 jit_solution(9378000434272638223)
XLA Ops:
  0.0 0.0 copy-start.1
  0.0 0.0 copy-start.3
  0.0 0.6 %mark.1.mark_ref = f32[8,128]{1,0:T(8,128)} custom-call(), custom_call_target="tpu_custom_call" | custom-call | flops 20000000000 | bytes 1048576 | tf_op jit(solution)/shard_map/mark/pallas_call | solution.py:236
  0.6 0.2 copy-done.1
  0.8 1.9 %all-gather = f32[16,8,256]{2,1,0:T(8,128)S(1)} all-gather(f32[8,8,256]{2,1,0:T(8,128)S(1)} %copy-done.1), channel_id=2, replica_groups=mesh['depth'=16,'pair'=16,'core'=2] {'core'}, dimensions={0}, use_global_device_ids=true | all-gather | bytes 196608 | tf_op jit(solution)/shard_map/all_gather | solution.py:252
  2.7 0.0 copy-done.3
  2.7 0.0 copy-start
  2.7 0.4 pack.1
  3.1 19.7 %all_to_all.10 = f16[16,8,512]{2,1,0:T(8,128)(2,1)S(1)} all-to-all(f16[16,8,512]{2,1,0:T(8,128)(2,1)S(1)} %convert_element_type.15), channel_id=1, replica_groups=mesh['depth'=16,'pair'=16,'core'=2] {'depth'}, dimensions={0} | all-to-all | bytes 262144 | tf_op jit(solution)/shard_map/all_to_all | solution.py:253
  22.8 9.7 %collective-permute-start = (f16[16,8,384]{2,1,0:T(8,128)(2,1)S(1)}, f16[16,8,384]{2,1,0:T(8,128)(2,1)S(1)}, u32[]{:S(2)}, u32[]{:S(2)}) collective-permute-start(f16[16,8,384]{2,1,0:T(8,128)(2,1)S(1)} %slice.4), channel_id=1, source_target_pairs={{1,2},{3,4},{5,6},{7,8},{9,10},{11,12},{13,14},{15,16},{17,18},{19... | collective-permute-start | bytes 294920 | tf_op jit(solution)/shard_map/ppermute | solution.py:257
  32.6 0.0 copy-done
  32.6 1.2 %inner.1 = (f32[208,128]{1,0:T(8,128)S(1)}, f32[128,128]{1,0:T(8,128)S(1)}) custom-call(f32[16,8,512]{2,1,0:T(8,128)S(1)} %convert_element_type.16.own_ref, bf16[11,11,128,128]{3,2,1,0:T(8,128)(2,1)S(1)} %copy-done), custom_call_target="tpu_custom_call" | custom-call | flops 507510784 | bytes 4194304 | tf_op jit(solution)/shard_map/inner/pallas_call | solution.py:260
  33.8 1.1 %collective-permute-done = f16[16,8,384]{2,1,0:T(8,128)(2,1)S(1)} collective-permute-done((f16[16,8,384]{2,1,0:T(8,128)(2,1)S(1)}, f16[16,8,384]{2,1,0:T(8,128)(2,1)S(1)}, u32[]{:S(2)}, u32[]{:S(2)}) %collective-permute-start) | collective-permute-done | bytes 98336 | tf_op jit(solution)/shard_map/ppermute | solution.py:257
  34.9 0.0 copy-start.2
  34.9 0.9 %ratio.1 = bf16[208,128]{1,0:T(8,128)(2,1)S(1)} custom-call(f32[208,128]{1,0:T(8,128)S(1)} %get-tuple-element.10.inner_ref, f32[128,128]{1,0:T(8,128)S(1)} %get-tuple-element.11.meas_ref, f32[16,8,384]{2,1,0:T(8,128)S(1)} %convert_element_type.17.next_ref, bf16[11,11,128,128]{3,2,1,0:T(8,128)(2,1)S(1)} %copy-done), custom_call_target="tpu_custom_call" | custom-call | tf_op jit(solution)/shard_map/ratio/pallas_call | solution.py:270
  35.8 1.9 %all_gather.11.chip_ref = bf16[416,128]{1,0:T(8,128)(2,1)S(1)} all-gather(bf16[208,128]{1,0:T(8,128)(2,1)S(1)} %ratio.1), channel_id=1, replica_groups=mesh['depth'=16,'pair'=16,'core'=2] {'core'}, dimensions={0}, use_global_device_ids=true | all-gather | bytes 159744 | tf_op jit(solution)/shard_map/all_gather | solution.py:279
  37.7 1.5 %back.1 = f32[16,8,256]{2,1,0:T(8,128)S(1)} custom-call(bf16[416,128]{1,0:T(8,128)(2,1)S(1)} %all_gather.11.chip_ref, bf16[11,11,128,128]{3,2,1,0:T(8,128)(2,1)S(1)} %copy-done), custom_call_target="tpu_custom_call" | custom-call | tf_op jit(solution)/shard_map/back/pallas_call | solution.py:280
  39.2 14.0 %all_to_all.11 = f16[16,8,256]{2,1,0:T(8,128)(2,1)S(1)} all-to-all(f16[16,8,256]{2,1,0:T(8,128)(2,1)S(1)} %convert_element_type.18), channel_id=1, replica_groups=mesh['depth'=16,'pair'=16,'core'=2] {'depth'}, dimensions={0} | all-to-all | bytes 131072 | tf_op jit(solution)/shard_map/all_to_all | solution.py:292
  53.3 0.0 copy-done.2
  53.3 0.8 %final.1 = f32[8,8,256]{2,1,0:T(8,128)} custom-call(f32[16,8,256]{2,1,0:T(8,128)S(1)} %convert_element_type.19.parts_ref, f32[8,8,256]{2,1,0:T(8,128)S(1)} %copy-done.1, f32[8,128]{1,0:T(8,128)S(1)} %copy-done.2), custom_call_target="tpu_custom_call" | custom-call | tf_op jit(solution)/shard_map/final/pallas_call | solution.py:293
  (6 shorter events, 0.1 us)
Async XLA Ops:
  0.0 0.8 %copy-start.1 = (f32[8,8,256]{2,1,0:T(8,128)S(1)}, f32[8,8,256]{2,1,0:T(8,128)}, u32[]{:S(2)}) copy-start(f32[8,8,256]{2,1,0:T(8,128)} %vol_ref.1) | copy-start | bytes 196612
  0.0 2.7 %copy-start.3 = (f32[8,8,256]{2,1,0:T(8,128)S(1)}, f32[8,8,256]{2,1,0:T(8,128)}, u32[]{:S(2)}) copy-start(f32[8,8,256]{2,1,0:T(8,128)} %meas_ref.1) | copy-start | bytes 196612
  2.7 29.9 %copy-start = (bf16[11,11,128,128]{3,2,1,0:T(8,128)(2,1)S(1)}, bf16[11,11,128,128]{3,2,1,0:T(8,128)(2,1)}, u32[]{:S(2)}) copy-start(bf16[11,11,128,128]{3,2,1,0:T(8,128)(2,1)} %psf_ref.5) | copy-start | bytes 11894788
  22.8 12.0 %collective-permute-start = (f16[16,8,384]{2,1,0:T(8,128)(2,1)S(1)}, f16[16,8,384]{2,1,0:T(8,128)(2,1)S(1)}, u32[]{:S(2)}, u32[]{:S(2)}) collective-permute-start(f16[16,8,384]{2,1,0:T(8,128)(2,1)S(1)} %slice.4), channel_id=1, source_target_pairs={{1,2},{3,4},{5,6},{7,8},{9,10},{11,12},{13,14},{15,16},{17,18},{19... | collective-permute-start | bytes 294920 | tf_op jit(solution)/shard_map/ppermute | solution.py:257
  34.9 18.4 %copy-start.2 = (f32[8,128]{1,0:T(8,128)S(1)}, f32[8,128]{1,0:T(8,128)}, u32[]{:S(2)}) copy-start(f32[8,128]{1,0:T(8,128)} %mark.1.mark_ref) | copy-start | bytes 12292

commit v13 on v10

--- a/solution.py
+++ b/solution.py
@@ -26,45 +26,35 @@
     return lax.broadcasted_iota(jnp.int32, shape, 1)
 
 
-VOLUME_AT = [(0, C * i) for i in range(4)] + [(1, C * i) for i in range(4)]
-VOLUME_AT += [(2, 64 + C * i) for i in range(2)] + [(3, 48 + C * i) for i in range(3)]
-MEASURED_AT = [(2, W * i) for i in range(4)] + [(0, 4 * C)] + [(3, W * i) for i in range(3)]
-
-
-def pack_kernel(vol_ref, meas_ref, out_ref):
-    even = lax.axis_index("core") == 0
+def pack_kernel(both_ref, out_ref):
+    vol_ref, meas_ref = both_ref.at[0], both_ref.at[1]
     lane = lanes()
     rows = {}
     rolled = {}
 
-    def volume_row(j, half):
-        here = slice(half * 128, half * 128 + 128)
-        odd = j + 6 if j < 2 * R else j - 7
-        a, b = [vol_ref[r // H, :, r % H, here] for r in (j, odd)]
-        return jnp.where(even, a, b).astype(BF16).astype(F32)
-
-    def measured_row(j, half):
-        here = slice(half * 128, half * 128 + 128)
-        odd = j + 3 if j < R else j - R
-        part = jnp.where(even, meas_ref[:, j, here], meas_ref[:, odd, here])
+    def volume_row(y, half):
+        return vol_ref[:, y, half * 128 : half * 128 + 128].astype(BF16).astype(F32)
+
+    def measured_row(y, half):
+        part = meas_ref[:, y, half * 128 : half * 128 + 128]
         part = part * part
         return part * part
 
-    def turned(make, j, half, shift):
-        name = (make, j, half)
+    def turned(make, y, half, shift):
+        name = (make, y, half)
         if name not in rows:
-            rows[name] = make(j, half)
+            rows[name] = make(y, half)
         shift = shift % 128
         if (name, shift) not in rolled:
             rolled[name, shift] = pltpu.roll(rows[name], shift, 1) if shift else rows[name]
         return rolled[name, shift]
 
-    def window(t, j, at):
+    def window(t, y, at):
         start = W * t - R
         low, high = max(start, 0) // 128, min(start + C - 1, 255) // 128
-        value = turned(volume_row, j, low, at - start)
+        value = turned(volume_row, y, low, at - start)
         if high != low:
-            value = jnp.where(lane - at < 128 - start, value, turned(volume_row, j, high, at - start))
+            value = jnp.where(lane - at < 128 - start, value, turned(volume_row, y, high, at - start))
         if start < 0:
             value = jnp.where(lane - at < -start, 0.0, value)
         if start + C > 256:
@@ -72,30 +62,46 @@
         return value
 
     for t in range(TILES):
-        for g in range(4):
-            parts = [(at, window(t, j, at)) for j, (where, at) in enumerate(VOLUME_AT) if where == g]
-            parts += [
-                (at, turned(measured_row, j, t // 8, at - W * t)) for j, (where, at) in enumerate(MEASURED_AT) if where == g
-            ]
-            parts.sort(key=lambda part: part[0])
-            value = parts[0][1]
-            for at, part in parts[1:]:
-                value = jnp.where(lane < at, value, part)
+        for g in range(2):
+            value = window(t, 4 * g, 0)
+            for i in range(1, 4):
+                value = jnp.where(lane < C * i, value, window(t, 4 * g + i, C * i))
             out_ref[t, :, g * 128 : g * 128 + 128] = value
-
-
-def turned_groups(packed_ref, count):
-    return [packed_ref[:, :, g * 128 : g * 128 + 128].reshape(Z, 128).T for g in range(count)]
+        value = turned(measured_row, 0, t // 8, -W * t)
+        for y in range(1, H):
+            value = jnp.where(lane < W * y, value, turned(measured_row, y, t // 8, W * y - W * t))
+        out_ref[t, :, 256:] = value
+
+
+def join_kernel(chip_ref, out_ref):
+    core = lax.axis_index("core")
+    even = core == 0
+    lane = lanes((Z, 128))
+
+    def group(i, g):
+        return chip_ref[i, :, :, g * 128 : g * 128 + 128].reshape(Z, 128)
+
+    def place(when_even, when_odd):
+        return jnp.where(even, pltpu.roll(mate, when_even, 1), pltpu.roll(mate, when_odd, 1))
+
+    own = [jnp.where(even, group(0, g), group(1, g)) for g in range(3)]
+    mate = jnp.where(even, group(1, 0), group(0, 1))
+    keep = (lane >= 48 * core) & (lane < 80 + 48 * core)
+    parts = [
+        jnp.where(lane < 4 * C, own[0], place(78, 26)),
+        jnp.where(lane < 4 * C, own[1], place(54, 2)),
+        jnp.where(keep, own[2], place(80, 76)),
+    ]
+    for g, part in enumerate(parts):
+        out_ref[:, :, g * 128 : g * 128 + 128] = part.reshape(TILES, 8, 128)
+
+
+def turned_groups(packed, count):
+    return [packed[:, :, g * 128 : g * 128 + 128].reshape(Z, 128).T for g in range(count)]
 
 
 def decoded(value):
     return jnp.where(value > 0.0, jnp.sqrt(jnp.sqrt(value)), 0.0)
-
-
-def fill_first_rows(blocks, rows_ref):
-    rows_ref[: 4 * C, :] = blocks[0][: 4 * C]
-    rows_ref[4 * C : 8 * C, :] = blocks[1][: 4 * C]
-    rows_ref[8 * C : 8 * C + 56, :] = blocks[2][64:120]
 
 
 def spread_row(rows_ref, taps_ref, start, row):
@@ -119,19 +125,16 @@
         sum_ref[here, :] = sum_ref[here, :] + part
 
 
-def inner_kernel(own_ref, psf_ref, sum_ref, meas_ref, rows_ref, taps_ref):
+def inner_kernel(chip_ref, psf_ref, sum_ref, meas_ref, rows_ref, taps_ref):
     core = lax.axis_index("core")
-    blocks = turned_groups(own_ref, 4)
-    fill_first_rows(blocks, rows_ref)
-    rows_ref[264:344, :] = blocks[3][48:]
-    for j in range(H + R):
-        if j < 2 * R:
-            spread_row(rows_ref, taps_ref, j * C, j + 3 * core)
-        else:
-            spread_row(rows_ref, taps_ref, 264 + (j - 2 * R) * C, j - 2 * R * core)
-    for part, even_row, odd_row in ((blocks[2][:64], 0, 3), (blocks[0][4 * C : 4 * C + W], 4, 7), (blocks[3][:48], 5, 0)):
-        row = even_row + (odd_row - even_row) * core
-        meas_ref[pl.ds(pl.multiple_of(row * W, W), part.shape[0]), :] = decoded(part)
+    for i in range(2):
+        for g, block in enumerate(turned_groups(chip_ref.at[i], 2)):
+            start = (2 * i + g) * 4 * C
+            rows_ref[start : start + 4 * C, :] = block[: 4 * C]
+    for y in range(2 * H):
+        spread_row(rows_ref, taps_ref, y * C, y)
+    coded = jnp.where(core == 0, chip_ref[0, :, :, 256:], chip_ref[1, :, :, 256:])
+    meas_ref[...] = decoded(coded.reshape(Z, 128)).T
     sum_ref[...] = jnp.zeros(sum_ref.shape, F32)
     for k in range(R, -R - 1, -2):
         steps = range(k, max(k - 2, -R - 1), -1)
@@ -141,7 +144,7 @@
             sum_ref,
             [R + i * (1 - 2 * core) for i in steps],
             H + k,
-            (R - k) * core,
+            (H - k) * core,
             [(R - i) * (1 - core) for i in steps],
             core == 1,
         )
@@ -151,9 +154,15 @@
     core = lax.axis_index("core")
     even = core == 0
     blocks = turned_groups(next_ref, 3)
-    fill_first_rows(blocks, rows_ref)
-    for j in range(2 * R):
-        spread_row(rows_ref, taps_ref, j * C, j)
+    rows_ref[: 4 * C, :] = blocks[0][: 4 * C]
+    rows_ref[4 * C : 8 * C, :] = blocks[1][: 4 * C]
+    rows_ref[208:240, :] = jnp.where(even, blocks[2][:32], blocks[2][80:112])
+    rows_ref[240:264, :] = blocks[0][4 * C :]
+    rows_ref[264:272, :] = blocks[1][4 * C : 4 * C + 8]
+    for y in range(H):
+        spread_row(rows_ref, taps_ref, y * C, y + 2 - 2 * core)
+    spread_row(rows_ref, taps_ref, 208, H * core)
+    spread_row(rows_ref, taps_ref, 240, H * core + 1)
     sum_ref[...] = inner_ref[...]
     for k in range(-R, R, 2):
         steps = (k, k + 1)
@@ -169,10 +178,9 @@
         )
     here = pl.ds(pl.multiple_of(R * W * (1 - core), W), H * W)
     out_ref[here, :] = (meas_ref[...] / sum_ref[here, :]).astype(BF16)
-    there = H * W * core
-    for part, row in ((blocks[2][:64], 0), (blocks[0][4 * C : 4 * C + W], 4)):
-        here = pl.ds(pl.multiple_of(there + row * W, W), part.shape[0])
-        out_ref[here, :] = (decoded(part) / sum_ref[here, :]).astype(BF16)
+    there = pl.ds(pl.multiple_of(H * W * core, W), R * W)
+    beyond = decoded(jnp.where(even, blocks[2][(H - R) * W :], blocks[2][: R * W]))
+    out_ref[there, :] = (beyond / sum_ref[there, :]).astype(BF16)
 
 
 def back_kernel(chip_ref, psf_ref, out_ref, rows_ref, sum_ref):
@@ -231,20 +239,29 @@
 def body(volume, measured, point_spread):
     packed = pl.pallas_call(
         pack_kernel,
-        out_shape=jax.ShapeDtypeStruct((TILES, 8, 512), F32),
-        in_specs=[VM] * 2,
+        out_shape=jax.ShapeDtypeStruct((TILES, 8, 384), F32),
+        in_specs=[VM],
         out_specs=VM,
         compiler_params=PARAMS,
         cost_estimate=pl.CostEstimate(flops=20_000_000_000, bytes_accessed=2**20, transcendentals=0),
         name="pack",
-    )(lax.all_gather(volume, "core"), measured)
+    )(jnp.stack([volume, measured]))
     own = lax.all_to_all(packed.astype(F16), "depth", 0, 0, tiled=True)
+    chip = lax.all_gather(own, "core").astype(F32)
+    joined = pl.pallas_call(
+        join_kernel,
+        out_shape=jax.ShapeDtypeStruct((TILES, 8, 384), F32),
+        in_specs=[VM],
+        out_specs=VM,
+        compiler_params=PARAMS,
+        name="join",
+    )(chip)
     tile = ("pair", "core")
     count = lax.axis_size(tile)
     pairs = [(i, i + 1) for i in range(1, count - 1, 2)] + [(i, i - 1) for i in range(2, count, 2)]
-    beyond = lax.ppermute(own[:, :, :384], tile, pairs)
+    beyond = lax.ppermute(joined.astype(F16), tile, pairs)
     rows = H + R
-    scratch = [pltpu.VMEM((rows * C + 14, Z), F32), pltpu.VMEM((rows * W, E * Z), BF16)]
+    scratch = [pltpu.VMEM((2 * H * C, Z), F32), pltpu.VMEM((2 * H * W, E * Z), BF16)]
     inner, near = pl.pallas_call(
         inner_kernel,
         out_shape=[jax.ShapeDtypeStruct((rows * W, Z), F32), jax.ShapeDtypeStruct((H * W, Z), F32)],
@@ -254,7 +271,7 @@
         compiler_params=PARAMS,
         cost_estimate=pl.CostEstimate(flops=2 * 88 * W * E * Z * Z, bytes_accessed=2**22, transcendentals=0),
         name="inner",
-    )(own.astype(F32), point_spread)
+    )(chip, point_spread)
     ratio = pl.pallas_call(
         ratio_kernel,
         out_shape=jax.ShapeDtypeStruct((rows * W, Z), BF16),

time: 54.5 us -> 54.9 us (level)
  starting transfers between devices: 9.7 us -> 11.4 us
  blocking collectives: 37.7 us -> 36.2 us
  other arithmetic: 0.08 us -> 0.98 us
  local copies, waits for them, and re-layouts: 0.87 us -> 0.01 us
    ppermute x1, starting transfers between devices: 9.7 us -> 11.4 us  [body(): beyond = lax.ppermute(joined.astype(F16), tile, pairs)]
    another operation x0 -> x1, other arithmetic: none -> 0.88 us  [body(): jnp.stack([volume, measured])]
    unnamed x6 -> x4, local copies, waits for them, and re-layouts: 0.85 us -> 0.01 us
    all_to_all x1, blocking collectives: 14 us -> 13.2 us  [body(): lax.all_to_all(shares.astype(F16), 'depth', 0, 0, tiled=True).astype(F32)]
    all_to_all x1, blocking collectives: 19.7 us -> 19.1 us  [body(): own = lax.all_to_all(packed.astype(F16), 'depth', 0, 0, tiled=True)]
where the time goes in v13:
time: 54.9 us; the launch traced here: 54.7 us
  blocking collectives  36.2 us (66%)
  starting transfers between devices  11.4 us (21%)
  Pallas kernels  4.92 us (9%)
  waiting for transfers between devices  1.12 us (2%)
  other arithmetic  0.98 us (2%)
    all_to_all x1, blocking collectives, body(): own = lax.all_to_all(packed.astype(F16), 'depth', 0, 0, tiled=True)  19.1 us
    all_to_all x1, blocking collectives, body(): lax.all_to_all(shares.astype(F16), 'depth', 0, 0, tiled=True).astype(F32)  13.2 us
    ppermute x1, starting transfers between devices, body(): beyond = lax.ppermute(joined.astype(F16), tile, pairs)  11.4 us
    all_gather x1, blocking collectives, body(): chip = lax.all_gather(own, 'core').astype(F32)  1.93 us
    all_gather x1, blocking collectives, body(): chip_ratio = lax.all_gather(ratio, 'core', tiled=True)  1.88 us
    pallas_call x1, Pallas kernels, body(): pl.pallas_call(back_kernel, out_shape=jax.ShapeDtypeStruct((TILES, 8, H *...  1.52 us
    pallas_call x1, Pallas kernels, body(): pl.pallas_call(inner_kernel, out_shape=[jax.ShapeDtypeStruct((rows * W, Z...  1.16 us
    ppermute x1, waiting for transfers between devices, body(): beyond = lax.ppermute(joined.astype(F16), tile, pairs)  1.12 us
  transfers between devices with their start and end apart: 1, of which 1 were waited for; matrix products, arithmetic and copies ran while one was open for 0% of the time, Pallas kernels for 2%

profile of v13, /device:TPU:8, one launch (start us, length us, event | category | flops | bytes accessed | tf_op | source)
XLA Modules:
  0.0 54.7 jit_solution(10453484540759144781)
XLA Ops:
  0.0 0.9 %pad_maximum_fusion.both_ref = f32[2,8,8,256]{3,2,1,0:T(8,128)S(1)} fusion(f32[1,8,8,256]{3,2,1,0:T(8,128)} %bitcast.6, f32[1,8,8,256]{3,2,1,0:T(8,128)} %bitcast.4), kind=kLoop, calls=%fused_computation | loop fusion | flops 32768 | bytes 262144 | tf_op jit(solution)/shard_map/stack | solution.py:248
  0.9 0.0 copy-start
  0.9 0.3 pack.1
  1.2 19.1 %all_to_all.10 = f16[16,8,384]{2,1,0:T(8,128)(2,1)S(1)} all-to-all(f16[16,8,384]{2,1,0:T(8,128)(2,1)S(1)} %convert_element_type.18), channel_id=1, replica_groups=mesh['depth'=16,'pair'=16,'core'=2] {'depth'}, dimensions={0} | all-to-all | bytes 196608 | tf_op jit(solution)/shard_map/all_to_all | solution.py:249
  20.3 1.9 %all-gather = f16[32,8,384]{2,1,0:T(8,128)(2,1)S(1)} all-gather(f16[16,8,384]{2,1,0:T(8,128)(2,1)S(1)} %all_to_all.10), channel_id=2, replica_groups=mesh['depth'=16,'pair'=16,'core'=2] {'core'}, dimensions={0}, use_global_device_ids=true | all-gather | bytes 294912 | tf_op jit(solution)/shard_map/all_gather | solution.py:250
  22.3 0.2 join.1
  22.5 11.4 %collective-permute-start = (f16[16,8,384]{2,1,0:T(8,128)(2,1)S(1)}, f16[16,8,384]{2,1,0:T(8,128)(2,1)S(1)}, u32[]{:S(2)}, u32[]{:S(2)}) collective-permute-start(f16[16,8,384]{2,1,0:T(8,128)(2,1)S(1)} %convert_element_type.20), channel_id=1, source_target_pairs={{1,2},{3,4},{5,6},{7,8},{9,10},{11,12},{13,14},{15,16},{17,18},{19... | collective-permute-start | bytes 294920 | tf_op jit(solution)/shard_map/ppermute | solution.py:262
  33.9 0.0 copy-done
  33.9 1.2 %inner.1 = (f32[208,128]{1,0:T(8,128)S(1)}, f32[128,128]{1,0:T(8,128)S(1)}) custom-call(f32[2,16,8,384]{3,2,1,0:T(8,128)S(1)} %convert.chip_ref, bf16[11,11,128,128]{3,2,1,0:T(8,128)(2,1)S(1)} %copy-done), custom_call_target="tpu_custom_call" | custom-call | flops 507510784 | bytes 4194304 | tf_op jit(solution)/shard_map/inner/pallas_call | solution.py:265
  35.1 1.1 %collective-permute-done = f16[16,8,384]{2,1,0:T(8,128)(2,1)S(1)} collective-permute-done((f16[16,8,384]{2,1,0:T(8,128)(2,1)S(1)}, f16[16,8,384]{2,1,0:T(8,128)(2,1)S(1)}, u32[]{:S(2)}, u32[]{:S(2)}) %collective-permute-start) | collective-permute-done | bytes 98336 | tf_op jit(solution)/shard_map/ppermute | solution.py:262
  36.2 0.0 copy-start.1
  36.2 0.9 %ratio.1 = bf16[208,128]{1,0:T(8,128)(2,1)S(1)} custom-call(f32[208,128]{1,0:T(8,128)S(1)} %get-tuple-element.7.inner_ref, f32[128,128]{1,0:T(8,128)S(1)} %get-tuple-element.8.meas_ref, f32[16,8,384]{2,1,0:T(8,128)S(1)} %convert_element_type.21.next_ref, bf16[11,11,128,128]{3,2,1,0:T(8,128)(2,1)S(1)} %copy-done), custom_call_target="tpu_custom_call" | custom-call | tf_op jit(solution)/shard_map/ratio/pallas_call | solution.py:275
  37.2 1.9 %all_gather.11.chip_ref = bf16[416,128]{1,0:T(8,128)(2,1)S(1)} all-gather(bf16[208,128]{1,0:T(8,128)(2,1)S(1)} %ratio.1), channel_id=1, replica_groups=mesh['depth'=16,'pair'=16,'core'=2] {'core'}, dimensions={0}, use_global_device_ids=true | all-gather | bytes 159744 | tf_op jit(solution)/shard_map/all_gather | solution.py:284
  39.1 1.5 %back.1 = f32[16,8,256]{2,1,0:T(8,128)S(1)} custom-call(bf16[416,128]{1,0:T(8,128)(2,1)S(1)} %all_gather.11.chip_ref, bf16[11,11,128,128]{3,2,1,0:T(8,128)(2,1)S(1)} %copy-done), custom_call_target="tpu_custom_call" | custom-call | tf_op jit(solution)/shard_map/back/pallas_call | solution.py:285
  40.6 13.2 %all_to_all.11 = f16[16,8,256]{2,1,0:T(8,128)(2,1)S(1)} all-to-all(f16[16,8,256]{2,1,0:T(8,128)(2,1)S(1)} %convert_element_type.22), channel_id=1, replica_groups=mesh['depth'=16,'pair'=16,'core'=2] {'depth'}, dimensions={0} | all-to-all | bytes 131072 | tf_op jit(solution)/shard_map/all_to_all | solution.py:297
  53.9 0.0 copy-done.1
  53.9 0.8 %final.1 = f32[8,8,256]{2,1,0:T(8,128)} custom-call(f32[16,8,256]{2,1,0:T(8,128)S(1)} %convert_element_type.23.parts_ref, f32[8,8,256]{2,1,0:T(8,128)S(1)} %copy-done.1), custom_call_target="tpu_custom_call" | custom-call | tf_op jit(solution)/shard_map/final/pallas_call | solution.py:298
  (6 shorter events, 0.1 us)
Async XLA Ops:
  0.9 33.0 %copy-start = (bf16[11,11,128,128]{3,2,1,0:T(8,128)(2,1)S(1)}, bf16[11,11,128,128]{3,2,1,0:T(8,128)(2,1)}, u32[]{:S(2)}) copy-start(bf16[11,11,128,128]{3,2,1,0:T(8,128)(2,1)} %psf_ref.5) | copy-start | bytes 11894788
  22.5 13.7 %collective-permute-start = (f16[16,8,384]{2,1,0:T(8,128)(2,1)S(1)}, f16[16,8,384]{2,1,0:T(8,128)(2,1)S(1)}, u32[]{:S(2)}, u32[]{:S(2)}) collective-permute-start(f16[16,8,384]{2,1,0:T(8,128)(2,1)S(1)} %convert_element_type.20), channel_id=1, source_target_pairs={{1,2},{3,4},{5,6},{7,8},{9,10},{11,12},{13,14},{15,16},{17,18},{19... | collective-permute-start | bytes 294920 | tf_op jit(solution)/shard_map/ppermute | solution.py:262
  36.2 17.6 %copy-start.1 = (f32[8,8,256]{2,1,0:T(8,128)S(1)}, f32[8,8,256]{2,1,0:T(8,128)}, u32[]{:S(2)}) copy-start(f32[8,8,256]{2,1,0:T(8,128)} %vol_ref.1) | copy-start | bytes 196612

commit v14 on v12

--- a/solution.py
+++ b/solution.py
@@ -208,28 +208,29 @@
         out_ref[:, :, g * 128 : g * 128 + 128] = share.reshape(TILES, 8, 128)
 
 
-def final_kernel(parts_ref, vol_ref, mark_ref, out_ref):
+def final_kernel(parts_ref, vol_ref, mark_ref, out_hbm, out_ref, sems):
     lane = lanes()
-    for y in range(H):
-        g, s = y // 4, y % 4
-        turned = []
-        for t in range(TILES):
-            part = parts_ref[t, :, g * 128 : g * 128 + 128]
-            shift = (W * t - R - S * s) % 128
-            turned.append(pltpu.roll(part, shift, 1) if shift else part)
-        for half in range(2):
+    copies = []
+    for half in range(2):
+        here = slice(half * 128, half * 128 + 128)
+        for y in range(H):
+            g, s = y // 4, y % 4
             sums = [None, None]
             for t in range(TILES):
                 start, stop = W * t - R - 128 * half, W * t + W + R - 128 * half
                 start, stop = max(start, 0), min(stop, 128)
                 if start >= stop:
                     continue
+                part = parts_ref[t, :, g * 128 : g * 128 + 128]
+                shift = (W * t - R - S * s) % 128
+                part = pltpu.roll(part, shift, 1) if shift else part
                 before = sums[t % 2]
-                sums[t % 2] = jnp.where(
-                    (lane >= start) & (lane < stop), turned[t], 0.0 if before is None else before
-                )
-            here = slice(half * 128, half * 128 + 128)
+                sums[t % 2] = jnp.where((lane >= start) & (lane < stop), part, 0.0 if before is None else before)
             out_ref[:, y, here] = vol_ref[:, y, here] * ((sums[0] + sums[1]) * (1 / SCALE))
+        copies.append(pltpu.make_async_copy(out_ref.at[:, :, here], out_hbm.at[:, :, here], sems.at[half]))
+        copies[-1].start()
+    for copy in copies:
+        copy.wait()
 
 
 def body(volume, measured, point_spread):
@@ -294,7 +295,8 @@
         final_kernel,
         out_shape=jax.ShapeDtypeStruct(volume.shape, F32),
         in_specs=[VM, VM, pl.BlockSpec(memory_space=pl.ANY)],
-        out_specs=VM,
+        out_specs=pl.BlockSpec(memory_space=pl.ANY),
+        scratch_shapes=[pltpu.VMEM(volume.shape, F32), pltpu.SemaphoreType.DMA((2,))],
         compiler_params=PARAMS,
         name="final",
     )(parts, volume, mark)

time: 54.3 us -> 54.4 us (level)
  no operation moved by 1% of the time
where the time goes in v14:
time: 54.4 us; the launch traced here: 54.1 us
  blocking collectives  37.5 us (69%)
  starting transfers between devices  9.7 us (18%)
  Pallas kernels  5.45 us (10%)
  waiting for transfers between devices  1.06 us (2%)
    all_to_all x1, blocking collectives, body(): own = lax.all_to_all(packed.astype(F16), 'depth', 0, 0, tiled=True)  19.7 us
    all_to_all x1, blocking collectives, body(): lax.all_to_all(shares.astype(F16), 'depth', 0, 0, tiled=True).astype(F32)  14 us
    ppermute x1, starting transfers between devices, body(): beyond = lax.ppermute(own[:, :, :384], tile, pairs)  9.7 us
    all_gather x1, blocking collectives, body(): lax.all_gather(volume_first, 'core')  1.89 us
    all_gather x1, blocking collectives, body(): chip_ratio = lax.all_gather(ratio, 'core', tiled=True)  1.88 us
    pallas_call x1, Pallas kernels, body(): pl.pallas_call(back_kernel, out_shape=jax.ShapeDtypeStruct((TILES, 8, H *...  1.53 us
    pallas_call x1, Pallas kernels, body(): pl.pallas_call(inner_kernel, out_shape=[jax.ShapeDtypeStruct((rows * W, Z...  1.19 us
  transfers between devices with their start and end apart: 1, of which 1 were waited for; matrix products, arithmetic and copies ran while one was open for 0% of the time, Pallas kernels for 2%

profile of v14, /device:TPU:8, one launch (start us, length us, event | category | flops | bytes accessed | tf_op | source)
XLA Modules:
  0.0 54.1 jit_solution(14688550502226432081)
XLA Ops:
  0.0 0.0 copy-start.1
  0.0 0.0 copy-start.3
  0.0 0.6 %mark.1.mark_ref = f32[8,128]{1,0:T(8,128)} custom-call(), custom_call_target="tpu_custom_call" | custom-call | flops 20000000000 | bytes 1048576 | tf_op jit(solution)/shard_map/mark/pallas_call | solution.py:237
  0.6 0.2 copy-done.1
  0.8 1.9 %all-gather = f32[16,8,256]{2,1,0:T(8,128)S(1)} all-gather(f32[8,8,256]{2,1,0:T(8,128)S(1)} %copy-done.1), channel_id=2, replica_groups=mesh['depth'=16,'pair'=16,'core'=2] {'core'}, dimensions={0}, use_global_device_ids=true | all-gather | bytes 196608 | tf_op jit(solution)/shard_map/all_gather | solution.py:253
  2.7 0.0 copy-done.3
  2.7 0.0 copy-start
  2.7 0.4 pack.1
  3.1 19.7 %all_to_all.10 = f16[16,8,512]{2,1,0:T(8,128)(2,1)S(1)} all-to-all(f16[16,8,512]{2,1,0:T(8,128)(2,1)S(1)} %convert_element_type.15), channel_id=1, replica_groups=mesh['depth'=16,'pair'=16,'core'=2] {'depth'}, dimensions={0} | all-to-all | bytes 262144 | tf_op jit(solution)/shard_map/all_to_all | solution.py:254
  22.8 9.7 %collective-permute-start = (f16[16,8,384]{2,1,0:T(8,128)(2,1)S(1)}, f16[16,8,384]{2,1,0:T(8,128)(2,1)S(1)}, u32[]{:S(2)}, u32[]{:S(2)}) collective-permute-start(f16[16,8,384]{2,1,0:T(8,128)(2,1)S(1)} %slice.4), channel_id=1, source_target_pairs={{1,2},{3,4},{5,6},{7,8},{9,10},{11,12},{13,14},{15,16},{17,18},{19... | collective-permute-start | bytes 294920 | tf_op jit(solution)/shard_map/ppermute | solution.py:258
  32.6 0.0 copy-done
  32.6 1.2 %inner.1 = (f32[208,128]{1,0:T(8,128)S(1)}, f32[128,128]{1,0:T(8,128)S(1)}) custom-call(f32[16,8,512]{2,1,0:T(8,128)S(1)} %convert_element_type.16.own_ref, bf16[11,11,128,128]{3,2,1,0:T(8,128)(2,1)S(1)} %copy-done), custom_call_target="tpu_custom_call" | custom-call | flops 507510784 | bytes 4194304 | tf_op jit(solution)/shard_map/inner/pallas_call | solution.py:261
  33.8 1.1 %collective-permute-done = f16[16,8,384]{2,1,0:T(8,128)(2,1)S(1)} collective-permute-done((f16[16,8,384]{2,1,0:T(8,128)(2,1)S(1)}, f16[16,8,384]{2,1,0:T(8,128)(2,1)S(1)}, u32[]{:S(2)}, u32[]{:S(2)}) %collective-permute-start) | collective-permute-done | bytes 98336 | tf_op jit(solution)/shard_map/ppermute | solution.py:258
  34.9 0.0 copy-start.2
  34.9 0.9 %ratio.1 = bf16[208,128]{1,0:T(8,128)(2,1)S(1)} custom-call(f32[208,128]{1,0:T(8,128)S(1)} %get-tuple-element.10.inner_ref, f32[128,128]{1,0:T(8,128)S(1)} %get-tuple-element.11.meas_ref, f32[16,8,384]{2,1,0:T(8,128)S(1)} %convert_element_type.17.next_ref, bf16[11,11,128,128]{3,2,1,0:T(8,128)(2,1)S(1)} %copy-done), custom_call_target="tpu_custom_call" | custom-call | tf_op jit(solution)/shard_map/ratio/pallas_call | solution.py:271
  35.8 1.9 %all_gather.11.chip_ref = bf16[416,128]{1,0:T(8,128)(2,1)S(1)} all-gather(bf16[208,128]{1,0:T(8,128)(2,1)S(1)} %ratio.1), channel_id=1, replica_groups=mesh['depth'=16,'pair'=16,'core'=2] {'core'}, dimensions={0}, use_global_device_ids=true | all-gather | bytes 159744 | tf_op jit(solution)/shard_map/all_gather | solution.py:280
  37.7 1.5 %back.1 = f32[16,8,256]{2,1,0:T(8,128)S(1)} custom-call(bf16[416,128]{1,0:T(8,128)(2,1)S(1)} %all_gather.11.chip_ref, bf16[11,11,128,128]{3,2,1,0:T(8,128)(2,1)S(1)} %copy-done), custom_call_target="tpu_custom_call" | custom-call | tf_op jit(solution)/shard_map/back/pallas_call | solution.py:281
  39.2 14.0 %all_to_all.11 = f16[16,8,256]{2,1,0:T(8,128)(2,1)S(1)} all-to-all(f16[16,8,256]{2,1,0:T(8,128)(2,1)S(1)} %convert_element_type.18), channel_id=1, replica_groups=mesh['depth'=16,'pair'=16,'core'=2] {'depth'}, dimensions={0} | all-to-all | bytes 131072 | tf_op jit(solution)/shard_map/all_to_all | solution.py:293
  53.3 0.0 copy-done.2
  53.3 0.9 %final.1 = f32[8,8,256]{2,1,0:T(8,128)} custom-call(f32[16,8,256]{2,1,0:T(8,128)S(1)} %convert_element_type.19.parts_ref, f32[8,8,256]{2,1,0:T(8,128)S(1)} %copy-done.1, f32[8,128]{1,0:T(8,128)S(1)} %copy-done.2), custom_call_target="tpu_custom_call" | custom-call | tf_op jit(solution)/shard_map/final/pallas_call | solution.py:294
  (6 shorter events, 0.1 us)
Async XLA Ops:
  0.0 0.8 %copy-start.1 = (f32[8,8,256]{2,1,0:T(8,128)S(1)}, f32[8,8,256]{2,1,0:T(8,128)}, u32[]{:S(2)}) copy-start(f32[8,8,256]{2,1,0:T(8,128)} %vol_ref.1) | copy-start | bytes 196612
  0.0 2.7 %copy-start.3 = (f32[8,8,256]{2,1,0:T(8,128)S(1)}, f32[8,8,256]{2,1,0:T(8,128)}, u32[]{:S(2)}) copy-start(f32[8,8,256]{2,1,0:T(8,128)} %meas_ref.1) | copy-start | bytes 196612
  2.7 29.9 %copy-start = (bf16[11,11,128,128]{3,2,1,0:T(8,128)(2,1)S(1)}, bf16[11,11,128,128]{3,2,1,0:T(8,128)(2,1)}, u32[]{:S(2)}) copy-start(bf16[11,11,128,128]{3,2,1,0:T(8,128)(2,1)} %psf_ref.5) | copy-start | bytes 11894788
  22.8 12.0 %collective-permute-start = (f16[16,8,384]{2,1,0:T(8,128)(2,1)S(1)}, f16[16,8,384]{2,1,0:T(8,128)(2,1)S(1)}, u32[]{:S(2)}, u32[]{:S(2)}) collective-permute-start(f16[16,8,384]{2,1,0:T(8,128)(2,1)S(1)} %slice.4), channel_id=1, source_target_pairs={{1,2},{3,4},{5,6},{7,8},{9,10},{11,12},{13,14},{15,16},{17,18},{19... | collective-permute-start | bytes 294920 | tf_op jit(solution)/shard_map/ppermute | solution.py:258
  34.9 18.4 %copy-start.2 = (f32[8,128]{1,0:T(8,128)S(1)}, f32[8,128]{1,0:T(8,128)}, u32[]{:S(2)}) copy-start(f32[8,128]{1,0:T(8,128)} %mark.1.mark_ref) | copy-start | bytes 12292

commit v15 on v12

--- a/solution.py
+++ b/solution.py
@@ -188,23 +188,28 @@
             if 0 <= row < H:
                 rows_ref[row * W : row * W + W, a * 128 : a * 128 + 128] = value
     rows_ref[H * W : H * W + W, :] = jnp.ones((W, E * Z), BF16)
-    sum_ref[...] = jnp.zeros((H * S, Z), F32)
     weight = jnp.zeros((1, Z), F32)
+    sums = [jnp.zeros((S, Z), F32) for _ in range(H)]
+    gap = jnp.zeros((16, 2 * Z), F32)
+    for y in range(H):
+        sum_ref[y * 48 : y * 48 + 16, :] = gap
+        sum_ref[y * 48 + 32 : y * 48 + 48, :] = gap
     for first in range(0, E, 2):
         pair = range(first, min(first + 2, E))
         kernel = jnp.concatenate(
             [psf_ref[a, first : first + len(pair)].reshape(len(pair) * Z, Z) for a in range(E)], axis=1
         )
         product = lax.dot_general(rows_ref[...], kernel, (((1,), (1,)), ((), ())), preferred_element_type=F32)
+        for y in range(H):
+            sum_ref[y * 48 + 16 : y * 48 + 32, : len(pair) * Z] = product[y * W : y * W + W]
         for i, b in enumerate(pair):
-            part = product[:, i * Z : i * Z + Z]
+            weight = weight + product[H * W : H * W + 1, i * Z : i * Z + Z]
             for y in range(H):
-                here = slice(y * S + b, y * S + b + W)
-                sum_ref[here, :] = sum_ref[here, :] + part[y * W : y * W + W]
-            weight = weight + part[H * W : H * W + 1]
+                start = y * 48 + 16 - b
+                sums[y] = sums[y] + sum_ref[start : start + S, i * Z : i * Z + Z]
     factor = SCALE / weight
     for g in range(2):
-        share = (sum_ref[g * 128 : g * 128 + 128, :] * factor).T
+        share = (jnp.concatenate(sums[4 * g : 4 * g + 4], axis=0) * factor).T
         out_ref[:, :, g * 128 : g * 128 + 128] = share.reshape(TILES, 8, 128)
 
 
@@ -284,7 +289,7 @@
         out_specs=VM,
         scratch_shapes=[
             pltpu.VMEM((H * W + W, E * Z), BF16),
-            pltpu.VMEM((H * S, Z), F32),
+            pltpu.VMEM((H * 48, 2 * Z), F32),
         ],
         compiler_params=PARAMS,
         name="back",

time: 54.3 us -> 54.3 us (level)
  no operation moved by 1% of the time
where the time goes in v15:
time: 54.3 us; the launch traced here: 54.1 us
  blocking collectives  37.5 us (69%)
  starting transfers between devices  9.7 us (18%)
  Pallas kernels  5.39 us (10%)
  waiting for transfers between devices  1.06 us (2%)
    all_to_all x1, blocking collectives, body(): own = lax.all_to_all(packed.astype(F16), 'depth', 0, 0, tiled=True)  19.7 us
    all_to_all x1, blocking collectives, body(): lax.all_to_all(shares.astype(F16), 'depth', 0, 0, tiled=True).astype(F32)  14 us
    ppermute x1, starting transfers between devices, body(): beyond = lax.ppermute(own[:, :, :384], tile, pairs)  9.7 us
    all_gather x1, blocking collectives, body(): lax.all_gather(volume_first, 'core')  1.89 us
    all_gather x1, blocking collectives, body(): chip_ratio = lax.all_gather(ratio, 'core', tiled=True)  1.88 us
    pallas_call x1, Pallas kernels, body(): pl.pallas_call(back_kernel, out_shape=jax.ShapeDtypeStruct((TILES, 8, H *...  1.48 us
    pallas_call x1, Pallas kernels, body(): pl.pallas_call(inner_kernel, out_shape=[jax.ShapeDtypeStruct((rows * W, Z...  1.19 us
  transfers between devices with their start and end apart: 1, of which 1 were waited for; matrix products, arithmetic and copies ran while one was open for 0% of the time, Pallas kernels for 2%

profile of v15, /device:TPU:8, one launch (start us, length us, event | category | flops | bytes accessed | tf_op | source)
XLA Modules:
  0.0 54.1 jit_solution(2591291551802009897)
XLA Ops:
  0.0 0.0 copy-start.1
  0.0 0.0 copy-start.3
  0.0 0.6 %mark.1.mark_ref = f32[8,128]{1,0:T(8,128)} custom-call(), custom_call_target="tpu_custom_call" | custom-call | flops 20000000000 | bytes 1048576 | tf_op jit(solution)/shard_map/mark/pallas_call | solution.py:241
  0.6 0.2 copy-done.1
  0.8 1.9 %all-gather = f32[16,8,256]{2,1,0:T(8,128)S(1)} all-gather(f32[8,8,256]{2,1,0:T(8,128)S(1)} %copy-done.1), channel_id=2, replica_groups=mesh['depth'=16,'pair'=16,'core'=2] {'core'}, dimensions={0}, use_global_device_ids=true | all-gather | bytes 196608 | tf_op jit(solution)/shard_map/all_gather | solution.py:257
  2.7 0.0 copy-done.3
  2.7 0.0 copy-start
  2.7 0.4 pack.1
  3.1 19.7 %all_to_all.10 = f16[16,8,512]{2,1,0:T(8,128)(2,1)S(1)} all-to-all(f16[16,8,512]{2,1,0:T(8,128)(2,1)S(1)} %convert_element_type.15), channel_id=1, replica_groups=mesh['depth'=16,'pair'=16,'core'=2] {'depth'}, dimensions={0} | all-to-all | bytes 262144 | tf_op jit(solution)/shard_map/all_to_all | solution.py:258
  22.8 9.7 %collective-permute-start = (f16[16,8,384]{2,1,0:T(8,128)(2,1)S(1)}, f16[16,8,384]{2,1,0:T(8,128)(2,1)S(1)}, u32[]{:S(2)}, u32[]{:S(2)}) collective-permute-start(f16[16,8,384]{2,1,0:T(8,128)(2,1)S(1)} %slice.4), channel_id=1, source_target_pairs={{1,2},{3,4},{5,6},{7,8},{9,10},{11,12},{13,14},{15,16},{17,18},{19... | collective-permute-start | bytes 294920 | tf_op jit(solution)/shard_map/ppermute | solution.py:262
  32.6 0.0 copy-done
  32.6 1.2 %inner.1 = (f32[208,128]{1,0:T(8,128)S(1)}, f32[128,128]{1,0:T(8,128)S(1)}) custom-call(f32[16,8,512]{2,1,0:T(8,128)S(1)} %convert_element_type.16.own_ref, bf16[11,11,128,128]{3,2,1,0:T(8,128)(2,1)S(1)} %copy-done), custom_call_target="tpu_custom_call" | custom-call | flops 507510784 | bytes 4194304 | tf_op jit(solution)/shard_map/inner/pallas_call | solution.py:265
  33.8 1.1 %collective-permute-done = f16[16,8,384]{2,1,0:T(8,128)(2,1)S(1)} collective-permute-done((f16[16,8,384]{2,1,0:T(8,128)(2,1)S(1)}, f16[16,8,384]{2,1,0:T(8,128)(2,1)S(1)}, u32[]{:S(2)}, u32[]{:S(2)}) %collective-permute-start) | collective-permute-done | bytes 98336 | tf_op jit(solution)/shard_map/ppermute | solution.py:262
  34.9 0.0 copy-start.2
  34.9 0.9 %ratio.1 = bf16[208,128]{1,0:T(8,128)(2,1)S(1)} custom-call(f32[208,128]{1,0:T(8,128)S(1)} %get-tuple-element.10.inner_ref, f32[128,128]{1,0:T(8,128)S(1)} %get-tuple-element.11.meas_ref, f32[16,8,384]{2,1,0:T(8,128)S(1)} %convert_element_type.17.next_ref, bf16[11,11,128,128]{3,2,1,0:T(8,128)(2,1)S(1)} %copy-done), custom_call_target="tpu_custom_call" | custom-call | tf_op jit(solution)/shard_map/ratio/pallas_call | solution.py:275
  35.8 1.9 %all_gather.11.chip_ref = bf16[416,128]{1,0:T(8,128)(2,1)S(1)} all-gather(bf16[208,128]{1,0:T(8,128)(2,1)S(1)} %ratio.1), channel_id=1, replica_groups=mesh['depth'=16,'pair'=16,'core'=2] {'core'}, dimensions={0}, use_global_device_ids=true | all-gather | bytes 159744 | tf_op jit(solution)/shard_map/all_gather | solution.py:284
  37.7 1.5 %back.1 = f32[16,8,256]{2,1,0:T(8,128)S(1)} custom-call(bf16[416,128]{1,0:T(8,128)(2,1)S(1)} %all_gather.11.chip_ref, bf16[11,11,128,128]{3,2,1,0:T(8,128)(2,1)S(1)} %copy-done), custom_call_target="tpu_custom_call" | custom-call | tf_op jit(solution)/shard_map/back/pallas_call | solution.py:285
  39.2 14.0 %all_to_all.11 = f16[16,8,256]{2,1,0:T(8,128)(2,1)S(1)} all-to-all(f16[16,8,256]{2,1,0:T(8,128)(2,1)S(1)} %convert_element_type.18), channel_id=1, replica_groups=mesh['depth'=16,'pair'=16,'core'=2] {'depth'}, dimensions={0} | all-to-all | bytes 131072 | tf_op jit(solution)/shard_map/all_to_all | solution.py:297
  53.2 0.0 copy-done.2
  53.2 0.8 %final.1 = f32[8,8,256]{2,1,0:T(8,128)} custom-call(f32[16,8,256]{2,1,0:T(8,128)S(1)} %convert_element_type.19.parts_ref, f32[8,8,256]{2,1,0:T(8,128)S(1)} %copy-done.1, f32[8,128]{1,0:T(8,128)S(1)} %copy-done.2), custom_call_target="tpu_custom_call" | custom-call | tf_op jit(solution)/shard_map/final/pallas_call | solution.py:298
  (6 shorter events, 0.1 us)
Async XLA Ops:
  0.0 0.8 %copy-start.1 = (f32[8,8,256]{2,1,0:T(8,128)S(1)}, f32[8,8,256]{2,1,0:T(8,128)}, u32[]{:S(2)}) copy-start(f32[8,8,256]{2,1,0:T(8,128)} %vol_ref.1) | copy-start | bytes 196612
  0.0 2.7 %copy-start.3 = (f32[8,8,256]{2,1,0:T(8,128)S(1)}, f32[8,8,256]{2,1,0:T(8,128)}, u32[]{:S(2)}) copy-start(f32[8,8,256]{2,1,0:T(8,128)} %meas_ref.1) | copy-start | bytes 196612
  2.7 29.9 %copy-start = (bf16[11,11,128,128]{3,2,1,0:T(8,128)(2,1)S(1)}, bf16[11,11,128,128]{3,2,1,0:T(8,128)(2,1)}, u32[]{:S(2)}) copy-start(bf16[11,11,128,128]{3,2,1,0:T(8,128)(2,1)} %psf_ref.5) | copy-start | bytes 11894788
  22.8 12.0 %collective-permute-start = (f16[16,8,384]{2,1,0:T(8,128)(2,1)S(1)}, f16[16,8,384]{2,1,0:T(8,128)(2,1)S(1)}, u32[]{:S(2)}, u32[]{:S(2)}) collective-permute-start(f16[16,8,384]{2,1,0:T(8,128)(2,1)S(1)} %slice.4), channel_id=1, source_target_pairs={{1,2},{3,4},{5,6},{7,8},{9,10},{11,12},{13,14},{15,16},{17,18},{19... | collective-permute-start | bytes 294920 | tf_op jit(solution)/shard_map/ppermute | solution.py:262
  34.9 18.4 %copy-start.2 = (f32[8,128]{1,0:T(8,128)S(1)}, f32[8,128]{1,0:T(8,128)}, u32[]{:S(2)}) copy-start(f32[8,128]{1,0:T(8,128)} %mark.1.mark_ref) | copy-start | bytes 12292

commit v16 on v12

--- a/solution.py
+++ b/solution.py
@@ -32,7 +32,7 @@
 
 
 def mark_kernel(out_ref):
-    out_ref[...] = jnp.zeros(out_ref.shape, F32)
+    out_ref[0] = 0
 
 
 def pack_kernel(vol_ref, meas_ref, out_ref):
@@ -235,8 +235,8 @@
 def body(volume, measured, point_spread):
     mark = pl.pallas_call(
         mark_kernel,
-        out_shape=jax.ShapeDtypeStruct((8, 128), F32),
-        out_specs=VM,
+        out_shape=jax.ShapeDtypeStruct((1,), jnp.int32),
+        out_specs=pl.BlockSpec(memory_space=pltpu.SMEM),
         cost_estimate=pl.CostEstimate(flops=20_000_000_000, bytes_accessed=2**20, transcendentals=0),
         name="mark",
     )()
@@ -293,7 +293,7 @@
     return pl.pallas_call(
         final_kernel,
         out_shape=jax.ShapeDtypeStruct(volume.shape, F32),
-        in_specs=[VM, VM, pl.BlockSpec(memory_space=pl.ANY)],
+        in_specs=[VM, VM, pl.BlockSpec(memory_space=pltpu.SMEM)],
         out_specs=VM,
         compiler_params=PARAMS,
         name="final",

time: 54.3 us -> 54.9 us (1.011)
    pallas_call x1, Pallas kernels: 0.84 us -> 1.46 us  [body(): pl.pallas_call(final_kernel, out_shape=jax.ShapeDtypeStruct(volume.shape,...]
where the time goes in v16:
time: 54.9 us; the launch traced here: 54.7 us
  blocking collectives  37.5 us (68%)
  starting transfers between devices  9.7 us (18%)
  Pallas kernels  5.97 us (11%)
  waiting for transfers between devices  1.06 us (2%)
    all_to_all x1, blocking collectives, body(): own = lax.all_to_all(packed.astype(F16), 'depth', 0, 0, tiled=True)  19.7 us
    all_to_all x1, blocking collectives, body(): lax.all_to_all(shares.astype(F16), 'depth', 0, 0, tiled=True).astype(F32)  14 us
    ppermute x1, starting transfers between devices, body(): beyond = lax.ppermute(own[:, :, :384], tile, pairs)  9.7 us
    all_gather x1, blocking collectives, body(): lax.all_gather(volume_first, 'core')  1.89 us
    all_gather x1, blocking collectives, body(): chip_ratio = lax.all_gather(ratio, 'core', tiled=True)  1.88 us
    pallas_call x1, Pallas kernels, body(): pl.pallas_call(back_kernel, out_shape=jax.ShapeDtypeStruct((TILES, 8, H *...  1.53 us
    pallas_call x1, Pallas kernels, body(): pl.pallas_call(final_kernel, out_shape=jax.ShapeDtypeStruct(volume.shape,...  1.46 us
    pallas_call x1, Pallas kernels, body(): pl.pallas_call(inner_kernel, out_shape=[jax.ShapeDtypeStruct((rows * W, Z...  1.18 us
  transfers between devices with their start and end apart: 1, of which 1 were waited for; matrix products, arithmetic and copies ran while one was open for 0% of the time, Pallas kernels for 2%

profile of v16, /device:TPU:8, one launch (start us, length us, event | category | flops | bytes accessed | tf_op | source)
XLA Modules:
  0.0 54.7 jit_solution(12693903704888037977)
XLA Ops:
  0.0 0.0 copy-start.1
  0.0 0.0 copy-start.2
  0.0 0.5 mark.1.mark_ref
  0.5 0.3 copy-done.1
  0.8 1.9 %all-gather = f32[16,8,256]{2,1,0:T(8,128)S(1)} all-gather(f32[8,8,256]{2,1,0:T(8,128)S(1)} %copy-done.1), channel_id=2, replica_groups=mesh['depth'=16,'pair'=16,'core'=2] {'core'}, dimensions={0}, use_global_device_ids=true | all-gather | bytes 196608 | tf_op jit(solution)/shard_map/all_gather | solution.py:252
  2.7 0.0 copy-done.2
  2.7 0.0 copy-start
  2.7 0.4 pack.1
  3.1 19.7 %all_to_all.10 = f16[16,8,512]{2,1,0:T(8,128)(2,1)S(1)} all-to-all(f16[16,8,512]{2,1,0:T(8,128)(2,1)S(1)} %convert_element_type.15), channel_id=1, replica_groups=mesh['depth'=16,'pair'=16,'core'=2] {'depth'}, dimensions={0} | all-to-all | bytes 262144 | tf_op jit(solution)/shard_map/all_to_all | solution.py:253
  22.8 9.7 %collective-permute-start = (f16[16,8,384]{2,1,0:T(8,128)(2,1)S(1)}, f16[16,8,384]{2,1,0:T(8,128)(2,1)S(1)}, u32[]{:S(2)}, u32[]{:S(2)}) collective-permute-start(f16[16,8,384]{2,1,0:T(8,128)(2,1)S(1)} %slice.4), channel_id=1, source_target_pairs={{1,2},{3,4},{5,6},{7,8},{9,10},{11,12},{13,14},{15,16},{17,18},{19... | collective-permute-start | bytes 294920 | tf_op jit(solution)/shard_map/ppermute | solution.py:257
  32.6 0.0 copy-done
  32.6 1.2 %inner.1 = (f32[208,128]{1,0:T(8,128)S(1)}, f32[128,128]{1,0:T(8,128)S(1)}) custom-call(f32[16,8,512]{2,1,0:T(8,128)S(1)} %convert_element_type.16.own_ref, bf16[11,11,128,128]{3,2,1,0:T(8,128)(2,1)S(1)} %copy-done), custom_call_target="tpu_custom_call" | custom-call | flops 507510784 | bytes 4194304 | tf_op jit(solution)/shard_map/inner/pallas_call | solution.py:260
  33.8 1.1 %collective-permute-done = f16[16,8,384]{2,1,0:T(8,128)(2,1)S(1)} collective-permute-done((f16[16,8,384]{2,1,0:T(8,128)(2,1)S(1)}, f16[16,8,384]{2,1,0:T(8,128)(2,1)S(1)}, u32[]{:S(2)}, u32[]{:S(2)}) %collective-permute-start) | collective-permute-done | bytes 98336 | tf_op jit(solution)/shard_map/ppermute | solution.py:257
  34.9 0.9 %ratio.1 = bf16[208,128]{1,0:T(8,128)(2,1)S(1)} custom-call(f32[208,128]{1,0:T(8,128)S(1)} %get-tuple-element.10.inner_ref, f32[128,128]{1,0:T(8,128)S(1)} %get-tuple-element.11.meas_ref, f32[16,8,384]{2,1,0:T(8,128)S(1)} %convert_element_type.17.next_ref, bf16[11,11,128,128]{3,2,1,0:T(8,128)(2,1)S(1)} %copy-done), custom_call_target="tpu_custom_call" | custom-call | tf_op jit(solution)/shard_map/ratio/pallas_call | solution.py:270
  35.8 1.9 %all_gather.11.chip_ref = bf16[416,128]{1,0:T(8,128)(2,1)S(1)} all-gather(bf16[208,128]{1,0:T(8,128)(2,1)S(1)} %ratio.1), channel_id=1, replica_groups=mesh['depth'=16,'pair'=16,'core'=2] {'core'}, dimensions={0}, use_global_device_ids=true | all-gather | bytes 159744 | tf_op jit(solution)/shard_map/all_gather | solution.py:279
  37.7 1.5 %back.1 = f32[16,8,256]{2,1,0:T(8,128)S(1)} custom-call(bf16[416,128]{1,0:T(8,128)(2,1)S(1)} %all_gather.11.chip_ref, bf16[11,11,128,128]{3,2,1,0:T(8,128)(2,1)S(1)} %copy-done), custom_call_target="tpu_custom_call" | custom-call | tf_op jit(solution)/shard_map/back/pallas_call | solution.py:280
  39.2 14.0 %all_to_all.11 = f16[16,8,256]{2,1,0:T(8,128)(2,1)S(1)} all-to-all(f16[16,8,256]{2,1,0:T(8,128)(2,1)S(1)} %convert_element_type.18), channel_id=1, replica_groups=mesh['depth'=16,'pair'=16,'core'=2] {'depth'}, dimensions={0} | all-to-all | bytes 131072 | tf_op jit(solution)/shard_map/all_to_all | solution.py:292
  53.3 1.5 %final.1 = f32[8,8,256]{2,1,0:T(8,128)} custom-call(f32[16,8,256]{2,1,0:T(8,128)S(1)} %convert_element_type.19.parts_ref, f32[8,8,256]{2,1,0:T(8,128)S(1)} %copy-done.1, s32[1]{0:T(128)} %mark.1.mark_ref), custom_call_target="tpu_custom_call" | custom-call | tf_op jit(solution)/shard_map/final/pallas_call | solution.py:293
  (6 shorter events, 0.1 us)
Async XLA Ops:
  0.0 0.8 %copy-start.1 = (f32[8,8,256]{2,1,0:T(8,128)S(1)}, f32[8,8,256]{2,1,0:T(8,128)}, u32[]{:S(2)}) copy-start(f32[8,8,256]{2,1,0:T(8,128)} %vol_ref.1) | copy-start | bytes 196612
  0.0 2.7 %copy-start.2 = (f32[8,8,256]{2,1,0:T(8,128)S(1)}, f32[8,8,256]{2,1,0:T(8,128)}, u32[]{:S(2)}) copy-start(f32[8,8,256]{2,1,0:T(8,128)} %meas_ref.1) | copy-start | bytes 196612
  2.7 29.9 %copy-start = (bf16[11,11,128,128]{3,2,1,0:T(8,128)(2,1)S(1)}, bf16[11,11,128,128]{3,2,1,0:T(8,128)(2,1)}, u32[]{:S(2)}) copy-start(bf16[11,11,128,128]{3,2,1,0:T(8,128)(2,1)} %psf_ref.5) | copy-start | bytes 11894788
  22.8 12.0 %collective-permute-start = (f16[16,8,384]{2,1,0:T(8,128)(2,1)S(1)}, f16[16,8,384]{2,1,0:T(8,128)(2,1)S(1)}, u32[]{:S(2)}, u32[]{:S(2)}) collective-permute-start(f16[16,8,384]{2,1,0:T(8,128)(2,1)S(1)} %slice.4), channel_id=1, source_target_pairs={{1,2},{3,4},{5,6},{7,8},{9,10},{11,12},{13,14},{15,16},{17,18},{19... | collective-permute-start | bytes 294920 | tf_op jit(solution)/shard_map/ppermute | solution.py:257
